TPU v7x, 32 devices: a whole 2x2x4 slice. The times are simulated.
32 devices in a mesh: ctx: 8 (over z, y), head: 4 (over x, core).
Axes of the slice: x: 2, y: 2, z: 4, core: 2. Of those that a mesh axis runs over, the one named last changes fastest.
Arguments:
- out_grad: bfloat16 [8192, 2048], P(('ctx', 'head')), may hold values from -6 to 6
- keep_mask: int32 [8192, 2048], P(('ctx', 'head')), may hold values 0 or 1
- out_weight: bfloat16 [2048, 2048], P('head'), may hold values from -0.125 to 0.125
- query_rows: bfloat16 [8192, 2048], P('ctx', 'head'), may hold values from -0.1875 to 0.1875
- key_rows: bfloat16 [8192, 2048], P('ctx', 'head'), may hold values from -0.1875 to 0.1875
- value_rows: bfloat16 [8192, 2048], P('ctx', 'head'), may hold values from -0.1875 to 0.1875
Outputs:
- query_grad: bfloat16 [8192, 2048], P('ctx', 'head')
- key_grad: bfloat16 [8192, 2048], P('ctx', 'head')
- value_grad: bfloat16 [8192, 2048], P('ctx', 'head')
All inputs are finite; a program needn't handle non-finite values. No bound on the sum of `keep_mask` on one device may be relied on, other than what follows from the above.
Results may differ from a plain program's by a relative error of at most 0.0065.
Values may be sent and summed in bfloat16 or wider, within the bound.
No kernel may reach another device: no remote copies, remote signals or barrier semaphores. Data moves between devices by JAX's collectives and lax.ppermute only.
A program may use at most 128 MiB of HBM per device.

v0:
```python
import jax
import jax.numpy as jnp
from jax import lax
from jax.sharding import PartitionSpec as P

HEAD_DIM = 128


KEEP_SCALE = 1.0 / 0.9


def prefix(array, axis, combine, identity, reverse):
    size, place = (lax.axis_size(axis), lax.axis_index(axis))
    everything = lax.all_gather(array, axis)
    start = jnp.broadcast_to(jnp.asarray(identity, array.dtype), array.shape)

    def step(k, before):
        at = size - 1 - k if reverse else k
        reached = at > place if reverse else at < place
        new = combine(before, everything[at])
        return jnp.where(reached, new, before)

    return lax.fori_loop(0, size, step, start)


def add_states(earlier, later):
    return jax.tree.map(jnp.add, earlier, later)


def per_device(out_grad, keep_mask, out_weight, query_rows, key_rows, value_rows):
    masked = (out_grad.astype(jnp.float32) * keep_mask.astype(jnp.float32) * KEEP_SCALE).astype(
        jnp.bfloat16
    )
    token_grad = lax.dot_general(
        masked,
        lax.all_gather(out_weight, "head", axis=0, tiled=True),
        (((1,), (1,)), ((), ())),
        preferred_element_type=jnp.float32,
    ).astype(jnp.bfloat16)
    head_grad = lax.all_to_all(token_grad, "head", split_axis=1, concat_axis=0, tiled=True)
    tokens = query_rows.shape[0]
    heads_here = query_rows.shape[1] // HEAD_DIM
    query_heads = query_rows.reshape(tokens, heads_here, HEAD_DIM)
    key_heads = key_rows.reshape(tokens, heads_here, HEAD_DIM)
    value_heads = value_rows.reshape(tokens, heads_here, HEAD_DIM)
    grad_heads = head_grad.reshape(tokens, heads_here, HEAD_DIM)
    key_value = jnp.einsum(
        "the,thf->hef", key_heads, value_heads, preferred_element_type=jnp.float32
    )
    query_state = jnp.einsum(
        "the,thf->hef", query_heads, grad_heads, preferred_element_type=jnp.float32
    )
    empty = jnp.zeros_like(key_value)
    state_prev = prefix(key_value, "ctx", add_states, empty, False)
    state_next = prefix(query_state, "ctx", add_states, empty, True)
    prev_round = state_prev.astype(jnp.bfloat16)
    next_round = state_next.astype(jnp.bfloat16)
    causal = lax.broadcasted_iota(jnp.int32, (tokens, tokens), 0) >= lax.broadcasted_iota(
        jnp.int32, (tokens, tokens), 1
    )
    grad_scores = jnp.einsum(
        "thf,shf->hts", grad_heads, value_heads, preferred_element_type=jnp.float32
    )
    grad_scores = jnp.where(causal, grad_scores, 0.0).astype(jnp.bfloat16)
    attn_scores = jnp.einsum(
        "the,she->hts", query_heads, key_heads, preferred_element_type=jnp.float32
    )
    attn_scores = jnp.where(causal, attn_scores, 0.0).astype(jnp.bfloat16)
    query_out = jnp.einsum(
        "hts,she->the", grad_scores, key_heads, preferred_element_type=jnp.float32
    )
    query_out = query_out + jnp.einsum(
        "thf,hef->the", grad_heads, prev_round, preferred_element_type=jnp.float32
    )
    key_out = jnp.einsum(
        "hts,the->she", grad_scores, query_heads, preferred_element_type=jnp.float32
    )
    key_out = key_out + jnp.einsum(
        "shf,hef->she", value_heads, next_round, preferred_element_type=jnp.float32
    )
    value_out = jnp.einsum(
        "hts,thf->shf", attn_scores, grad_heads, preferred_element_type=jnp.float32
    )
    value_out = value_out + jnp.einsum(
        "she,hef->shf", key_heads, next_round, preferred_element_type=jnp.float32
    )
    width = heads_here * HEAD_DIM
    return (
        query_out.astype(jnp.bfloat16).reshape(tokens, width),
        key_out.astype(jnp.bfloat16).reshape(tokens, width),
        value_out.astype(jnp.bfloat16).reshape(tokens, width),
    )


def solution(mesh):
    placed = (
        P(("ctx", "head"), None),
        P(("ctx", "head"), None),
        P("head", None),
        P("ctx", "head"),
        P("ctx", "head"),
        P("ctx", "head"),
    )
    return jax.shard_map(
        per_device,
        mesh=mesh,
        in_specs=placed,
        out_specs=(P("ctx", "head"), P("ctx", "head"), P("ctx", "head")),
        check_vma=False,
    )
```

profile of v0, /device:TPU:0, one launch (start us, length us, event | category | flops | bytes accessed | tf_op | source)
XLA Modules:
  0.0 201.8 jit_solution(16855095847920954929)
XLA Ops:
  8.7 1.2 fusion.7
  9.9 60.7 %all-gather.6.cloned.1.call-done = bf16[2048,2048]{1,0:T(8,128)(2,1)} async-done(((bf16[512,2048]{1,0:T(8,128)(2,1)}), bf16[2048,2048]{1,0:T(8,128)(2,1)}) %all-gather.6.cloned.1.call-update) | async-done | bytes 8388624 | tf_op jit(solution)/shard_map/all_gather | solution.py:36
  70.6 6.4 %convolution_convert_fusion = bf16[256,2048]{1,0:T(8,128)(2,1)S(1)} fusion(bf16[2048,2048]{1,0:T(8,128)(2,1)} %all-gather.6.cloned.1.call-done, s32[256,2048]{1,0:T(8,128)} %param.11, bf16[256,2048]{1,0:T(8,128)(2,1)S(1)} %copy-done.6), kind=kOutput, calls=%fused_computation.5 | convolution fusion | flops 2150629376 | bytes 12582912 | tf_op jit(solution)/shard_map/dot_general | solution.py:34
  77.0 1.1 copy.110
  78.1 3.5 %all-to-all-start = ((bf16[256,4,512]{2,0,1:T(8,128)(2,1)}), bf16[256,4,512]{2,0,1:T(8,128)(2,1)S(1)}, u32[]{:S(2)}, u32[]{:S(2)}) async-start(bf16[256,4,512]{2,0,1:T(8,128)(2,1)} %bitcast.105), calls=%async_computation | async-start | bytes 2097152 | tf_op jit(solution)/shard_map/all_to_all | solution.py:40
  81.9 1.3 iota_compare_fusion
  83.1 12.9 %all-to-all-done = bf16[256,4,512]{2,0,1:T(8,128)(2,1)S(1)} async-done(((bf16[256,4,512]{2,0,1:T(8,128)(2,1)}), bf16[256,4,512]{2,0,1:T(8,128)(2,1)S(1)}, u32[]{:S(2)}, u32[]{:S(2)}) %all-to-all-start) | async-done | bytes 1048608 | tf_op jit(solution)/shard_map/all_to_all | solution.py:40
  96.0 1.1 reshape.31
  97.1 1.6 copy.50
  98.7 1.7 convolution_bitcast_fusion
  101.3 21.4 %all-gather.8.cloned.1.call-done = f32[32,128,128]{2,1,0:T(8,128)} async-done(((f32[4,128,128]{2,1,0:T(8,128)}), f32[32,128,128]{2,1,0:T(8,128)}) %all-gather.8.cloned.1.call-update) | async-done | bytes 2097168 | tf_op jit(solution)/shard_map/all_gather | solution.py:14
  122.6 8.5 %while.30 = (s32[]{:T(128)}, f32[4,128,128]{2,1,0:T(8,128)S(1)}, s32[]{:T(128)}, f32[8,4,128,128]{3,2,1,0:T(8,128)}, s32[]{:T(128)}, /*index=5*/s32[]{:T(128)}) while((s32[]{:T(128)}, f32[4,128,128]{2,1,0:T(8,128)S(1)}, s32[]{:T(128)}, f32[8,4,128,128]{3,2,1,0:T(8,128)}, s32[]{:T(128)}, /*index=5*/s32[]{:T(128)}) %tuple.89), condition=%wide.region_1.2_spmd.clone, body=%wide.region_0.1_spmd.clone.sunk | while | flops 196612 | bytes 786533 | solution.py:23
  123.7 1.0 add_select_fusion.4
  124.8 1.0 add_select_fusion.4
  125.8 1.0 add_select_fusion.4
  126.9 1.0 add_select_fusion.4
  127.9 1.0 add_select_fusion.4
  129.0 1.0 add_select_fusion.4
  130.1 1.1 add_select_fusion.4
  131.1 4.1 %select_convert_fusion.1 = bf16[4,1024,1024]{2,1,0:T(8,128)(2,1)S(1)} fusion(bf16[1024,4,128]{0,2,1:T(8,128)(2,1)S(1)} %copy.50, pred[1024,1024]{1,0:T(8,128)(4,1)} %iota_compare_fusion, bf16[1024,512]{1,0:T(8,128)(2,1)S(1)} %copy-done), kind=kOutput, calls=%fused_computation.3 | convolution fusion | flops 1082130432 | bytes 11534336 | tf_op jit(solution)/shard_map/thf,shf->hts/dot_general | solution.py:61
  135.3 2.9 %fusion.9 = f32[4,1024,128]{1,2,0:T(8,128)S(1)} fusion(bf16[4,1024,1024]{2,1,0:T(8,128)(2,1)S(1)} %select_convert_fusion.1, bf16[1024,512]{1,0:T(8,128)(2,1)S(1)} %copy-done.3), kind=kOutput, calls=%fused_computation.19 | convolution fusion | flops 1073741824 | bytes 11534336 | tf_op jit(solution)/shard_map/hts,she->the/dot_general | solution.py:69
  138.5 1.4 fusion.2
  139.9 2.3 %copy.59 = bf16[1024,512]{1,0:T(8,128)(2,1)} copy(bf16[1024,512]{0,1:T(8,128)(2,1)} %bitcast.101) | data formatting | bytes 2097152
  142.2 7.2 %fusion = f32[4,128,1024]{2,1,0:T(8,128)} fusion(bf16[1024,4,128]{0,2,1:T(8,128)(2,1)S(1)} %copy.50, pred[1024,1024]{1,0:T(8,128)(4,1)} %iota_compare_fusion, bf16[1024,512]{1,0:T(8,128)(2,1)} %param.13, bf16[1024,512]{1,0:T(8,128)(2,1)} %param.14), kind=kOutput, calls=%fused_computation.6 | convolution fusion | flops 2155872256 | bytes 6291456 | tf_op jit(solution)/shard_map/hts,thf->shf/dot_general | solution.py:81
  149.4 23.3 %all-gather.10.cloned.1.call-done = f32[32,128,128]{2,1,0:T(8,128)} async-done(((f32[4,128,128]{2,1,0:T(8,128)}), f32[32,128,128]{2,1,0:T(8,128)}) %all-gather.10.cloned.1.call-update) | async-done | bytes 2097168 | tf_op jit(solution)/shard_map/all_gather | solution.py:14
  172.7 8.5 %while.31 = (s32[]{:T(128)}, f32[4,128,128]{2,1,0:T(8,128)S(1)}, s32[]{:T(128)}, f32[8,4,128,128]{3,2,1,0:T(8,128)}, s32[]{:T(128)}, /*index=5*/s32[]{:T(128)}, s32[]{:T(128)}, s32[]{:T(128)}) while((s32[]{:T(128)}, f32[4,128,128]{2,1,0:T(8,128)S(1)}, s32[]{:T(128)}, f32[8,4,128,128]{3,2,1,0:T(8,128)}, s32[]{:T(128)}, ...), condition=%wide.region_3.4_spmd.clone, body=%wide.region_2.3_spmd.clone.sunk | while | flops 196616 | bytes 786595 | solution.py:23
  174.8 1.0 add_select_fusion.5
  178.0 1.0 add_select_fusion.5
  183.2 1.5 add_convert_fusion
  184.6 2.3 %copy.61 = bf16[1024,512]{1,0:T(8,128)(2,1)} copy(bf16[1024,512]{0,1:T(8,128)(2,1)} %bitcast.102) | data formatting | bytes 2097152
  186.9 6.1 %fusion.1 = bf16[1024,4,128]{0,2,1:T(8,128)(2,1)} fusion(f32[4,128,1024]{2,1,0:T(8,128)S(1)} %fusion.14, bf16[4,1024,1024]{2,1,0:T(8,128)(2,1)} %copy-done.1, bf16[1024,512]{1,0:T(8,128)(2,1)} %param.13), kind=kOutput, calls=%fused_computation.8 | convolution fusion | flops 1074790400 | bytes 12582912 | tf_op jit(solution)/shard_map/hts,the->she/dot_general | solution.py:75
  193.0 2.3 %copy.60 = bf16[1024,512]{1,0:T(8,128)(2,1)} copy(bf16[1024,512]{0,1:T(8,128)(2,1)} %bitcast.103) | data formatting | bytes 2097152
  (31 shorter events, 12.1 us)
Async XLA Ops:
  7.2 1.2 copy-start
  7.2 1.5 copy-start.2
  7.2 63.4 %copy-start.6 = (bf16[256,2048]{1,0:T(8,128)(2,1)S(1)}, bf16[256,2048]{1,0:T(8,128)(2,1)}, u32[]{:S(2)}) copy-start(bf16[256,2048]{1,0:T(8,128)(2,1)} %param.10) | copy-start | bytes 3145732
  7.2 63.4 %all-gather.6.cloned.1.call-start = ((), (), s32[]{:S(2)}) async-start(), calls=%async_computation.1 | async-start | bytes 10485760 | tf_op jit(solution)/shard_map/all_gather | solution.py:36
  7.9 114.7 %all-gather.8.cloned.1.call-start = ((), (), s32[]{:S(2)}) async-start(), calls=%async_computation.2 | async-start | bytes 2359296 | tf_op jit(solution)/shard_map/all_gather | solution.py:14
  78.1 18.0 %all-to-all-start = ((bf16[256,4,512]{2,0,1:T(8,128)(2,1)}), bf16[256,4,512]{2,0,1:T(8,128)(2,1)S(1)}, u32[]{:S(2)}, u32[]{:S(2)}) async-start(bf16[256,4,512]{2,0,1:T(8,128)(2,1)} %bitcast.105), calls=%async_computation | async-start | bytes 2097152 | tf_op jit(solution)/shard_map/all_to_all | solution.py:40
  81.6 91.1 %all-gather.10.cloned.1.call-start = ((), (), s32[]{:S(2)}) async-start(), calls=%async_computation.3 | async-start | bytes 2359296 | tf_op jit(solution)/shard_map/all_gather | solution.py:14
  131.1 4.1 %copy-start.3 = (bf16[1024,512]{1,0:T(8,128)(2,1)S(1)}, bf16[1024,512]{1,0:T(8,128)(2,1)}, u32[]{:S(2)}) copy-start(bf16[1024,512]{1,0:T(8,128)(2,1)} %param.14) | copy-start | bytes 3145732
  135.2 3.2 %copy-start.1 = (bf16[4,1024,1024]{2,1,0:T(8,128)(2,1)}, bf16[4,1024,1024]{2,1,0:T(8,128)(2,1)S(1)}, u32[]{:S(2)}) copy-start(bf16[4,1024,1024]{2,1,0:T(8,128)(2,1)S(1)} %select_convert_fusion.1) | copy-start | bytes 25165828
  181.2 1.2 copy-start.4
  181.2 1.9 copy-start.5
Sparse Core Ops, SparseCore 0:
  9.6 60.9 all-gather.5
  73.3 49.2 all-gather.7
  124.8 47.8 all-gather.9
where the time goes:
time: 203 us; the launch traced here: 202 us
  waiting for transfers between devices  119 us (59%)
  matrix products  32.9 us (16%)
  other arithmetic  17.9 us (9%)
  local copies, waits for them, and re-layouts  14 us (7%)
  between operations  13.9 us (7%)
  starting transfers between devices  3.83 us (2%)
    all_gather x1, waiting for transfers between devices, per_device(): lax.all_gather(out_weight, 'head', axis=0, tiled=True)  60.7 us
    all_gather x2, waiting for transfers between devices, prefix(): everything = lax.all_gather(array, axis)  44.7 us
    select_n x16, other arithmetic, step(): return jnp.where(reached, new, before)  16.6 us
    all_to_all x1, waiting for transfers between devices, per_device(): lax.all_to_all(token_grad, 'head', split_axis=1, concat_axis=0, tiled=True)  12.9 us
    unnamed x17, local copies, waits for them, and re-layouts  9.37 us
    dot_general x1, matrix products, per_device(): jnp.einsum('hts,thf->shf', attn_scores, grad_heads, preferred_element_typ...  7.22 us
    dot_general x1, matrix products, per_device(): lax.dot_general(masked, lax.all_gather(out_weight, 'head', axis=0, tiled=...  6.39 us
    dot_general x1, matrix products, per_device(): jnp.einsum('hts,the->she', grad_scores, query_heads, preferred_element_ty...  6.14 us
  transfers between devices with their start and end apart: 4, of which 4 were waited for; matrix products, arithmetic and copies ran while one was open for 20% of the time, Pallas kernels for 0%

commit v1 on v0

v1 whole, which is shorter than its diff:
```python
import functools

import jax
import jax.numpy as jnp
from jax import lax
from jax.experimental import pallas as pl
from jax.experimental.pallas import tpu as pltpu
from jax.sharding import PartitionSpec as P

HEAD_DIM = 128
KEEP_SCALE = 1.0 / 0.9
CHUNKS = 4
SUB = 256
F32 = jnp.float32
BF16 = jnp.bfloat16
NT = (((1,), (1,)), ((), ()))
NN = (((1,), (0,)), ((), ()))
TN = (((0,), (0,)), ((), ()))
MIB = 1024 * 1024


def dot(left, right, dims):
    return lax.dot_general(left, right, dims, preferred_element_type=F32)


def vmem():
    return pl.BlockSpec(memory_space=pltpu.VMEM)


def smem():
    return pl.BlockSpec(memory_space=pltpu.SMEM)


def params(mib):
    return pltpu.CompilerParams(vmem_limit_bytes=mib * MIB)


def cost(flops, nbytes):
    return pl.CostEstimate(flops=flops, bytes_accessed=nbytes, transcendentals=0)


def kv_body(key_ref, value_ref, wide_ref, short_ref):
    for h in range(wide_ref.shape[0]):
        cols = slice(h * HEAD_DIM, (h + 1) * HEAD_DIM)
        state = dot(key_ref[:, cols], value_ref[:, cols], TN)
        wide_ref[h] = state
        short_ref[h] = state.astype(BF16)


def kv_state(key_rows, value_rows):
    tokens, width = key_rows.shape
    heads = width // HEAD_DIM
    shape = (heads, HEAD_DIM, HEAD_DIM)
    return pl.pallas_call(
        kv_body,
        out_shape=(jax.ShapeDtypeStruct(shape, F32), jax.ShapeDtypeStruct(shape, BF16)),
        in_specs=[vmem(), vmem()],
        out_specs=(vmem(), vmem()),
        compiler_params=params(12),
        cost_estimate=cost(2 * tokens * width * HEAD_DIM, 4 * tokens * width),
        name="kv_state",
    )(key_rows, value_rows)


def grad_body(pieces, first, last, own_rows, *refs):
    place_ref, query_ref, weight_ref = refs[:3]
    refs = refs[3:]
    before_ref = None
    if not first:
        before_ref, refs = refs[0], refs[1:]
    masked_refs, refs = refs[: len(pieces)], refs[len(pieces) :]
    grad_ref, state_ref = refs[:2]
    heads = state_ref.shape[0]
    place = place_ref[0]
    sums = [None if first else before_ref[h] for h in range(heads)]
    at = 0
    for ref, (flip, row) in zip(masked_refs, pieces):
        rows = ref.shape[0]
        grad = dot(ref[...], weight_ref[...], NT).astype(BF16)
        grad_ref[at : at + rows, :] = grad
        at += rows
        start = pl.multiple_of(jnp.bitwise_xor(place, flip) * own_rows + row, 16)
        query = query_ref[pl.ds(start, rows), :]
        for h in range(heads):
            cols = slice(h * HEAD_DIM, (h + 1) * HEAD_DIM)
            part = dot(query[:, cols], grad[:, cols], TN)
            sums[h] = part if sums[h] is None else sums[h] + part
    for h in range(heads):
        state_ref[h] = sums[h]
        if last:
            refs[2][h] = sums[h].astype(BF16)


def grad_part(place, query_rows, out_weight, before, pieces, arrays, own_rows, last, name):
    width, model = out_weight.shape
    heads = width // HEAD_DIM
    rows = sum(a.shape[0] for a in arrays)
    shape = (heads, HEAD_DIM, HEAD_DIM)
    out_shape = [jax.ShapeDtypeStruct((rows, width), BF16), jax.ShapeDtypeStruct(shape, F32)]
    if last:
        out_shape.append(jax.ShapeDtypeStruct(shape, BF16))
    first = before is None
    operands = [place, query_rows, out_weight] + ([] if first else [before]) + list(arrays)
    return pl.pallas_call(
        functools.partial(grad_body, pieces, first, last, own_rows),
        out_shape=tuple(out_shape),
        in_specs=[smem()] + [vmem()] * (len(operands) - 1),
        out_specs=tuple(vmem() for _ in out_shape),
        compiler_params=params(20),
        cost_estimate=cost(2 * rows * width * model, 2 * (rows + width) * model),
        name=name,
    )(*operands)


def block_body(places, own_rows, *refs):
    place_ref, query_ref, key_ref, value_ref, prev_ref = refs[:5]
    grad_refs = refs[5 : 5 + len(places)]
    query_out, key_part, value_part, grad = refs[5 + len(places) :]
    place = place_ref[0]
    for ref, pieces in zip(grad_refs, places):
        for at, rows, flip, row in pieces:
            start = pl.multiple_of(jnp.bitwise_xor(place, flip) * own_rows + row, 16)
            grad[pl.ds(start, rows), :] = ref[at : at + rows, :]
    tokens = query_ref.shape[0]
    count = tokens // SUB
    row_id = lax.broadcasted_iota(jnp.int32, (SUB, SUB), 0)
    col_id = lax.broadcasted_iota(jnp.int32, (SUB, SUB), 1)
    prev = prev_ref[0].astype(BF16)
    rows = [slice(i * SUB, (i + 1) * SUB) for i in range(count)]
    for i in range(count):
        g_i, q_i = grad[rows[i], :], query_ref[rows[i], :]
        total = dot(g_i, prev, NT)
        for j in range(i + 1):
            k_j, v_j = key_ref[rows[j], :], value_ref[rows[j], :]
            scores = dot(g_i, v_j, NT)
            scores_t = dot(v_j, g_i, NT)
            attn_t = dot(k_j, q_i, NT)
            if i == j:
                scores = jnp.where(row_id >= col_id, scores, 0.0)
                scores_t = jnp.where(col_id >= row_id, scores_t, 0.0)
                attn_t = jnp.where(col_id >= row_id, attn_t, 0.0)
            total = total + dot(scores.astype(BF16), k_j, NN)
            key_add = dot(scores_t.astype(BF16), q_i, NN)
            value_add = dot(attn_t.astype(BF16), g_i, NN)
            if i == j:
                key_part[rows[j], :] = key_add
                value_part[rows[j], :] = value_add
            else:
                key_part[rows[j], :] += key_add
                value_part[rows[j], :] += value_add
        query_out[rows[i], :] = total.astype(BF16)


def block_products(place, query_rows, key_rows, value_rows, prev, grads, places, own_rows):
    tokens, width = query_rows.shape
    heads = width // HEAD_DIM
    column = lambda rows: pl.BlockSpec((rows, HEAD_DIM), lambda h: (0, h))
    return pl.pallas_call(
        functools.partial(block_body, places, own_rows),
        out_shape=(
            jax.ShapeDtypeStruct((tokens, width), BF16),
            jax.ShapeDtypeStruct((tokens, width), F32),
            jax.ShapeDtypeStruct((tokens, width), F32),
        ),
        grid=(heads,),
        in_specs=[smem()]
        + [column(tokens)] * 3
        + [pl.BlockSpec((1, HEAD_DIM, HEAD_DIM), lambda h: (h, 0, 0))]
        + [column(g.shape[0]) for g in grads],
        out_specs=(column(tokens), column(tokens), column(tokens)),
        scratch_shapes=[pltpu.VMEM((tokens, HEAD_DIM), BF16)],
        compiler_params=params(20),
        cost_estimate=cost(10 * tokens * tokens * width, 20 * tokens * width),
        name="block_products",
    )(place, query_rows, key_rows, value_rows, prev, *grads)


def end_body(key_ref, value_ref, key_part, value_part, next_ref, key_out, value_out):
    state = next_ref[0].astype(BF16)
    key_out[...] = (key_part[...] + dot(value_ref[...], state, NT)).astype(BF16)
    value_out[...] = (value_part[...] + dot(key_ref[...], state, NN)).astype(BF16)


def end_products(key_rows, value_rows, key_part, value_part, state_next):
    tokens, width = key_rows.shape
    heads = width // HEAD_DIM
    column = pl.BlockSpec((tokens, HEAD_DIM), lambda h: (0, h))
    return pl.pallas_call(
        end_body,
        out_shape=(jax.ShapeDtypeStruct((tokens, width), BF16),) * 2,
        grid=(heads,),
        in_specs=[column] * 4 + [pl.BlockSpec((1, HEAD_DIM, HEAD_DIM), lambda h: (h, 0, 0))],
        out_specs=(column, column),
        compiler_params=params(12),
        cost_estimate=cost(4 * tokens * width * HEAD_DIM, 16 * tokens * width),
        name="end_products",
    )(key_rows, value_rows, key_part, value_part, state_next)


def radices(size):
    steps = []
    while size > 1:
        steps.append(2)
        size //= 2
    return steps


def scan_states(own, axis, reverse):
    size, place = lax.axis_size(axis), lax.axis_index(axis)
    total = own
    result = jnp.zeros(own.shape, F32)
    reach = 1
    group = own.astype(F32)
    if size > 1:
        other = lax.ppermute(own, axis, [(i, i ^ 1) for i in range(size)]).astype(F32)
        odd = (place % 2) == 1
        result = jnp.where(odd if not reverse else jnp.logical_not(odd), other, 0.0)
        group = group + other
        reach = 2
    first = True
    carried = group
    while reach < size:
        if reverse:
            pairs = [(i + reach, i) for i in range(size - reach)]
        else:
            pairs = [(i, i + reach) for i in range(size - reach)]
        got = lax.ppermute(carried.astype(BF16), axis, pairs).astype(F32)
        result = result + got
        carried = carried + got
        reach *= 2
    return result


def per_device(out_grad, keep_mask, out_weight, query_rows, key_rows, value_rows):
    size = lax.axis_size("head")
    place = lax.axis_index("head").astype(jnp.int32).reshape(1)
    own_rows = out_grad.shape[0]
    step = own_rows // CHUNKS

    def swap(array, distance):
        return lax.ppermute(array, "head", [(i, i ^ distance) for i in range(size)])

    masked = [
        (
            out_grad[c * step : (c + 1) * step].astype(F32)
            * keep_mask[c * step : (c + 1) * step].astype(F32)
            * KEEP_SCALE
        ).astype(BF16)
        for c in range(CHUNKS)
    ]
    far = [swap(m, 2) for m in masked]
    near = [swap(m, 1) for m in masked]
    both = [swap(m, 1) for m in far]

    kv_wide, kv_short = kv_state(key_rows, value_rows)
    state_prev = scan_states(kv_short, "ctx", False)

    parts = [
        [(0, c, masked[c]) for c in range(CHUNKS)] + [(1, c, near[c]) for c in range(CHUNKS)],
        [(2, c, far[c]) for c in range(CHUNKS - 1)] + [(3, c, both[c]) for c in range(CHUNKS - 1)],
        [(2, CHUNKS - 1, far[-1]), (3, CHUNKS - 1, both[-1])],
    ]
    before, grads, places = None, [], []
    for n, part in enumerate(parts):
        last = n == len(parts) - 1
        got = grad_part(
            place,
            query_rows,
            out_weight,
            before,
            tuple((flip, c * step) for flip, c, _ in part),
            [a for _, _, a in part],
            own_rows,
            last,
            "grad_part_%d" % n,
        )
        grads.append(got[0])
        places.append(tuple((i * step, step, flip, c * step) for i, (flip, c, _) in enumerate(part)))
        before = got[1]
    state_next = scan_states(got[2], "ctx", True)

    query_out, key_part, value_part = block_products(
        place, query_rows, key_rows, value_rows, state_prev, grads, tuple(places), own_rows
    )
    key_out, value_out = end_products(key_rows, value_rows, key_part, value_part, state_next)
    return query_out, key_out, value_out


def solution(mesh):
    placed = (
        P(("ctx", "head"), None),
        P(("ctx", "head"), None),
        P("head", None),
        P("ctx", "head"),
        P("ctx", "head"),
        P("ctx", "head"),
    )
    return jax.shard_map(
        per_device,
        mesh=mesh,
        in_specs=placed,
        out_specs=(P("ctx", "head"), P("ctx", "head"), P("ctx", "head")),
        check_vma=False,
    )
```

time: 203 us -> 82 us (0.40)
  waiting for transfers between devices: 119 us -> 21.1 us
  matrix products: 32.9 us -> 0 us
  Pallas kernels: 0 us -> 32.4 us
  starting transfers between devices: 3.83 us -> 20.6 us
  other arithmetic: 17.9 us -> 4.3 us
  between operations: 13.9 us -> 0.89 us
  local copies, waits for them, and re-layouts: 14 us -> 2.38 us
    all_gather x3 -> x0, waiting for transfers between devices: 105 us -> none  [the longest x1 60.7 us: per_device(): lax.all_gather(out_weight, 'head', axis=0, tiled=True)]
    dot_general x10 -> x0, matrix products: 32.9 us -> none  [the longest x1 7.22 us: per_device(): jnp.einsum('hts,thf->shf', attn_scores, grad_heads, preferred_element_typ...]
    pallas_call x0 -> x6, Pallas kernels: none -> 32.4 us  [the longest x3 16.1 us: grad_part(): pl.pallas_call(functools.partial(grad_body, pieces, first, last, own_rows...]
    ppermute x0 -> x18, waiting for transfers between devices: none -> 21.1 us  [the longest x12 11.7 us: swap(): return lax.ppermute(array, 'head', [(i, i ^ distance) for i in range(size)])]
    ppermute x0 -> x18, starting transfers between devices: none -> 20.6 us  [the longest x4 11 us: scan_states(): got = lax.ppermute(carried.astype(BF16), axis, pairs).astype(F32)]
    select_n x16 -> x0, other arithmetic: 16.6 us -> none  [step(): return jnp.where(reached, new, before)]
    all_to_all x1 -> x0, waiting for transfers between devices: 12.9 us -> none  [per_device(): lax.all_to_all(token_grad, 'head', split_axis=1, concat_axis=0, tiled=True)]
    unnamed x17 -> x24, local copies, waits for them, and re-layouts: 9.37 us -> 2.38 us
  transfers between devices with their start and end apart: 4 -> 18, of which waited for: 4 -> 6; matrix products, arithmetic and copies ran while one was open for 20% -> 1% of each run, Pallas kernels for 0% -> 36%
where the time goes in v1:
time: 82 us; the launch traced here: 81.8 us
  Pallas kernels  32.4 us (40%)
  waiting for transfers between devices  21.1 us (26%)
  starting transfers between devices  20.6 us (25%)
  other arithmetic  4.3 us (5%)
  local copies, waits for them, and re-layouts  2.38 us (3%)
  between operations  0.89 us (1%)
    pallas_call x3, Pallas kernels, grad_part(): pl.pallas_call(functools.partial(grad_body, pieces, first, last, own_rows...  16.1 us
    pallas_call x1, Pallas kernels, block_products(): pl.pallas_call(functools.partial(block_body, places, own_rows), out_shape...  11.9 us
    ppermute x12, waiting for transfers between devices, swap(): return lax.ppermute(array, 'head', [(i, i ^ distance) for i in range(size)])  11.7 us
    ppermute x4, starting transfers between devices, scan_states(): got = lax.ppermute(carried.astype(BF16), axis, pairs).astype(F32)  11 us
    ppermute x12, starting transfers between devices, swap(): return lax.ppermute(array, 'head', [(i, i ^ distance) for i in range(size)])  6.6 us
    ppermute x4, waiting for transfers between devices, scan_states(): got = lax.ppermute(carried.astype(BF16), axis, pairs).astype(F32)  5.61 us
    ppermute x2, waiting for transfers between devices, scan_states(): lax.ppermute(own, axis, [(i, i ^ 1) for i in range(size)]).astype(F32)  3.84 us
    pallas_call x1, Pallas kernels, end_products(): pl.pallas_call(end_body, out_shape=(jax.ShapeDtypeStruct((tokens, width),...  3.17 us
  transfers between devices with their start and end apart: 18, of which 6 were waited for; matrix products, arithmetic and copies ran while one was open for 1% of the time, Pallas kernels for 36%

profile of v1, /device:TPU:0, one launch (start us, length us, event | category | flops | bytes accessed | tf_op | source)
XLA Modules:
  0.0 81.8 jit_solution(14924970254983439273)
XLA Ops:
  0.7 3.1 %multiply_convert_fusion = (bf16[64,2048]{1,0:T(8,128)(2,1)S(1)}, bf16[64,2048]{1,0:T(8,128)(2,1)}, bf16[64,2048]{1,0:T(8,128)(2,1)}, bf16[64,2048]{1,0:T(8,128)(2,1)}) fusion(s32[256,2048]{1,0:T(8,128)} %param.7, bf16[256,2048]{1,0:T(8,128)(2,1)} %param.6), kind=kLoop, calls=%fused_computation | loop fusion | flops 2621440 | bytes 4194304 | tf_op jit(solution)/shard_map/convert_element_type | solution.py:248
  3.8 2.9 %collective-permute-start.13 = (bf16[64,2048]{1,0:T(8,128)(2,1)S(1)}, bf16[64,2048]{1,0:T(8,128)(2,1)S(1)}, u32[]{:S(2)}, u32[]{:S(2)}) collective-permute-start(bf16[64,2048]{1,0:T(8,128)(2,1)S(1)} %get-tuple-element.27.refs_6_), channel_id=1, source_target_pairs={{0,2},{1,3},{2,0},{3,1},{4,6},{5,7},{6,4},{7,5},{8,10},{9,11},{10,... | collective-permute-start | bytes 786440 | tf_op jit(solution)/shard_map/ppermute | solution.py:241
  6.7 1.2 %kv_state.1 = (f32[4,128,128]{2,1,0:T(8,128)}, bf16[4,128,128]{2,1,0:T(8,128)(2,1)S(1)}) custom-call(bf16[1024,512]{1,0:T(8,128)(2,1)S(1)} %copy-done.2, bf16[1024,512]{1,0:T(8,128)(2,1)S(1)} %copy-done.4), custom_call_target="tpu_custom_call" | custom-call | flops 134217728 | bytes 2097152 | tf_op jit(solution)/shard_map/kv_state/pallas_call | solution.py:54
  7.9 1.5 %collective-permute-start = (bf16[4,128,128]{2,1,0:T(8,128)(2,1)S(1)}, bf16[4,128,128]{2,1,0:T(8,128)(2,1)S(1)}, u32[]{:S(2)}, u32[]{:S(2)}) collective-permute-start(bf16[4,128,128]{2,1,0:T(8,128)(2,1)S(1)} %get-tuple-element.15), channel_id=1, source_target_pairs={{0,4},{4,0},{8,12},{12,8},{16,20},{20,16},{24,28},{28,24},{1,5},{5... | collective-permute-start | bytes 393224 | tf_op jit(solution)/shard_map/ppermute | solution.py:215
  9.4 0.5 collective-permute-start.8
  10.0 3.8 %collective-permute-done = bf16[4,128,128]{2,1,0:T(8,128)(2,1)S(1)} collective-permute-done((bf16[4,128,128]{2,1,0:T(8,128)(2,1)S(1)}, bf16[4,128,128]{2,1,0:T(8,128)(2,1)S(1)}, u32[]{:S(2)}, u32[]{:S(2)}) %collective-permute-start) | collective-permute-done | bytes 131104 | tf_op jit(solution)/shard_map/ppermute | solution.py:215
  13.8 0.3 collective-permute-start.7
  14.1 0.7 copy-done.6
  14.8 0.7 copy-done.8
  15.5 1.8 %collective-permute-start.9 = (bf16[64,2048]{1,0:T(8,128)(2,1)}, bf16[64,2048]{1,0:T(8,128)(2,1)}, u32[]{:S(2)}, u32[]{:S(2)}) collective-permute-start(bf16[64,2048]{1,0:T(8,128)(2,1)} %get-tuple-element.30.refs_5_), channel_id=1, source_target_pairs={{0,2},{1,3},{2,0},{3,1},{4,6},{5,7},{6,4},{7,5},{8,10},{9,11},{10,... | collective-permute-start | bytes 786440 | tf_op jit(solution)/shard_map/ppermute | solution.py:241
  17.3 1.9 %collective-permute-done.8.refs_5_ = bf16[64,2048]{1,0:T(8,128)(2,1)} collective-permute-done((bf16[64,2048]{1,0:T(8,128)(2,1)}, bf16[64,2048]{1,0:T(8,128)(2,1)}, u32[]{:S(2)}, u32[]{:S(2)}) %collective-permute-start.8) | collective-permute-done | bytes 262176 | tf_op jit(solution)/shard_map/ppermute | solution.py:241
  19.2 0.5 collective-permute-start.14
  19.7 5.1 %collective-permute-done.7.refs_4_ = bf16[64,2048]{1,0:T(8,128)(2,1)} collective-permute-done((bf16[64,2048]{1,0:T(8,128)(2,1)}, bf16[64,2048]{1,0:T(8,128)(2,1)}, u32[]{:S(2)}, u32[]{:S(2)}) %collective-permute-start.7) | collective-permute-done | bytes 262176 | tf_op jit(solution)/shard_map/ppermute | solution.py:241
  24.8 0.5 collective-permute-start.10
  25.4 4.6 %collective-permute-done.9.refs_6_ = bf16[64,2048]{1,0:T(8,128)(2,1)} collective-permute-done((bf16[64,2048]{1,0:T(8,128)(2,1)}, bf16[64,2048]{1,0:T(8,128)(2,1)}, u32[]{:S(2)}, u32[]{:S(2)}) %collective-permute-start.9) | collective-permute-done | bytes 262176 | tf_op jit(solution)/shard_map/ppermute | solution.py:241
  30.0 0.9 %fusion.4 = bf16[4,128,128]{2,1,0:T(8,128)(2,1)S(1)} fusion(bf16[4,128,128]{2,1,0:T(8,128)(2,1)} %copy-done.10, bf16[4,128,128]{2,1,0:T(8,128)(2,1)S(1)} %get-tuple-element.15), kind=kLoop, calls=%fused_computation.16 | loop fusion | flops 262144 | bytes 393216 | tf_op jit(solution)/shard_map/convert_element_type | solution.py:227
  30.9 3.7 %collective-permute-start.1 = (bf16[4,128,128]{2,1,0:T(8,128)(2,1)S(1)}, bf16[4,128,128]{2,1,0:T(8,128)(2,1)S(1)}, u32[]{:S(2)}, u32[]{:S(2)}) collective-permute-start(bf16[4,128,128]{2,1,0:T(8,128)(2,1)S(1)} %fusion.4), channel_id=1, source_target_pairs={{0,8},{4,12},{8,16},{12,20},{16,24},{20,28},{1,9},{5,13},{9,17},{1... | collective-permute-start | bytes 393224 | tf_op jit(solution)/shard_map/ppermute | solution.py:227
  34.7 0.9 %copy-done.9 = bf16[64,2048]{1,0:T(8,128)(2,1)S(1)} copy-done((bf16[64,2048]{1,0:T(8,128)(2,1)S(1)}, bf16[64,2048]{1,0:T(8,128)(2,1)}, u32[]{:S(2)}) %copy-start.9) | copy-done | bytes 262168
  35.6 7.7 %grad_part_0.1 = (bf16[512,512]{1,0:T(8,128)(2,1)S(1)}, f32[4,128,128]{2,1,0:T(8,128)S(1)}) custom-call(s32[1]{0:T(128)} %bitcast.refs_0_, bf16[1024,512]{1,0:T(8,128)(2,1)S(1)} %copy-done.1, bf16[512,2048]{1,0:T(8,128)(2,1)S(1)} %copy-done, bf16[64,2048]{1,0:T(8,128)(2,1)} %get-tuple-element.29.refs_3_, bf16[64,2048]{1,0:T(8,128)(2,1)} %get-tuple-element.28.refs_4_, ...), custom_call_target="tpu_custom_call" | custom-call | flops 1073741824 | bytes 4194304 | tf_op jit(solution)/shard_map/grad_part_0/pallas_call | solution.py:104
  43.4 6.0 %grad_part_1.1 = (bf16[384,512]{1,0:T(8,128)(2,1)S(1)}, f32[4,128,128]{2,1,0:T(8,128)S(1)}) custom-call(s32[1]{0:T(128)} %bitcast.refs_0_, bf16[1024,512]{1,0:T(8,128)(2,1)S(1)} %copy-done.1, bf16[512,2048]{1,0:T(8,128)(2,1)S(1)} %copy-done, f32[4,128,128]{2,1,0:T(8,128)S(1)} %get-tuple-element.17.refs_3_, bf16[64,2048]{1,0:T(8,128)(2,1)} %collective-permute-done.7.refs_4_, ...), custom_call_target="tpu_custom_call" | custom-call | flops 805306368 | bytes 3670016 | tf_op jit(solution)/shard_map/grad_part_1/pallas_call | solution.py:104
  49.5 2.4 %grad_part_2.1 = (bf16[128,512]{1,0:T(8,128)(2,1)S(1)}, f32[4,128,128]{2,1,0:T(8,128)}, bf16[4,128,128]{2,1,0:T(8,128)(2,1)S(1)}) custom-call(s32[1]{0:T(128)} %bitcast.refs_0_, bf16[1024,512]{1,0:T(8,128)(2,1)S(1)} %copy-done.1, bf16[512,2048]{1,0:T(8,128)(2,1)S(1)} %copy-done, f32[4,128,128]{2,1,0:T(8,128)S(1)} %get-tuple-element.19.refs_3_, ...), custom_call_target="tpu_custom_call" | custom-call | flops 268435456 | bytes 2621440 | tf_op jit(solution)/shard_map/grad_part_2/pallas_call | solution.py:104
  51.9 1.5 %collective-permute-start.15 = (bf16[4,128,128]{2,1,0:T(8,128)(2,1)S(1)}, bf16[4,128,128]{2,1,0:T(8,128)(2,1)S(1)}, u32[]{:S(2)}, u32[]{:S(2)}) collective-permute-start(bf16[4,128,128]{2,1,0:T(8,128)(2,1)S(1)} %get-tuple-element.24), channel_id=1, source_target_pairs={{0,4},{4,0},{8,12},{12,8},{16,20},{20,16},{24,28},{28,24},{1,5},{5... | collective-permute-start | bytes 393224 | tf_op jit(solution)/shard_map/ppermute | solution.py:215
  53.4 0.1 fusion.1
  53.5 4.5 %collective-permute-start.2 = (bf16[4,128,128]{2,1,0:T(8,128)(2,1)S(1)}, bf16[4,128,128]{2,1,0:T(8,128)(2,1)S(1)}, u32[]{:S(2)}, u32[]{:S(2)}) collective-permute-start(bf16[4,128,128]{2,1,0:T(8,128)(2,1)S(1)} %fusion.1), channel_id=1, source_target_pairs={{0,16},{4,20},{8,24},{12,28},{1,17},{5,21},{9,25},{13,29},{2,18},{... | collective-permute-start | bytes 393224 | tf_op jit(solution)/shard_map/ppermute | solution.py:227
  58.1 1.3 %collective-permute-start.16 = (bf16[4,128,128]{2,1,0:T(8,128)(2,1)S(1)}, bf16[4,128,128]{2,1,0:T(8,128)(2,1)S(1)}, u32[]{:S(2)}, u32[]{:S(2)}) collective-permute-start(bf16[4,128,128]{2,1,0:T(8,128)(2,1)S(1)} %fusion.5), channel_id=1, source_target_pairs={{8,0},{12,4},{16,8},{20,12},{24,16},{28,20},{9,1},{13,5},{17,9},{2... | collective-permute-start | bytes 393224 | tf_op jit(solution)/shard_map/ppermute | solution.py:227
  59.4 1.5 %collective-permute-done.2 = bf16[4,128,128]{2,1,0:T(8,128)(2,1)S(1)} collective-permute-done((bf16[4,128,128]{2,1,0:T(8,128)(2,1)S(1)}, bf16[4,128,128]{2,1,0:T(8,128)(2,1)S(1)}, u32[]{:S(2)}, u32[]{:S(2)}) %collective-permute-start.2) | collective-permute-done | bytes 131104 | tf_op jit(solution)/shard_map/ppermute | solution.py:227
  60.9 0.1 fusion.refs_4_
  60.9 4.1 %collective-permute-done.16 = bf16[4,128,128]{2,1,0:T(8,128)(2,1)S(1)} collective-permute-done((bf16[4,128,128]{2,1,0:T(8,128)(2,1)S(1)}, bf16[4,128,128]{2,1,0:T(8,128)(2,1)S(1)}, u32[]{:S(2)}, u32[]{:S(2)}) %collective-permute-start.16) | collective-permute-done | bytes 131104 | tf_op jit(solution)/shard_map/ppermute | solution.py:227
  65.0 0.1 fusion.3
  65.1 1.5 %collective-permute-start.17 = (bf16[4,128,128]{2,1,0:T(8,128)(2,1)S(1)}, bf16[4,128,128]{2,1,0:T(8,128)(2,1)S(1)}, u32[]{:S(2)}, u32[]{:S(2)}) collective-permute-start(bf16[4,128,128]{2,1,0:T(8,128)(2,1)S(1)} %fusion.3), channel_id=1, source_target_pairs={{16,0},{20,4},{24,8},{28,12},{17,1},{21,5},{25,9},{29,13},{18,2},{... | collective-permute-start | bytes 393224 | tf_op jit(solution)/shard_map/ppermute | solution.py:227
  66.6 11.9 %block_products.1 = (bf16[1024,512]{1,0:T(8,128)(2,1)}, f32[1024,512]{1,0:T(8,128)S(1)}, f32[1024,512]{1,0:T(8,128)S(1)}) custom-call(s32[1]{0:T(128)} %bitcast.refs_0_, bf16[1024,512]{1,0:T(8,128)(2,1)S(1)} %copy-done.1, bf16[1024,512]{1,0:T(8,128)(2,1)S(1)} %copy-done.3, bf16[1024,512]{1,0:T(8,128)(2,1)S(1)} %copy-done.5, f32[4,128,128]{2,1,0:T(8,128)S(1)} %fusion.refs_4_, ...), custom_call_target="tpu_custom_call" | custom-call | flops 5368709120 | bytes 10485760 | tf_op jit(solution)/shard_map/block_products/pallas_call | solution.py:158
  78.6 3.2 %end_products.1 = (bf16[1024,512]{1,0:T(8,128)(2,1)}, bf16[1024,512]{1,0:T(8,128)(2,1)}) custom-call(bf16[1024,512]{1,0:T(8,128)(2,1)S(1)} %copy-done.3, bf16[1024,512]{1,0:T(8,128)(2,1)S(1)} %copy-done.5, f32[1024,512]{1,0:T(8,128)S(1)} %get-tuple-element.22.key_part, f32[1024,512]{1,0:T(8,128)S(1)} %get-tuple-element.23.value_part, ...), custom_call_target="tpu_custom_call" | custom-call | flops 268435456 | bytes 8388608 | tf_op jit(solution)/shard_map/end_products/pallas_call | solution.py:188
  (41 shorter events, 0.2 us)
Async XLA Ops:
  0.6 6.1 %copy-start.4 = (bf16[1024,512]{1,0:T(8,128)(2,1)S(1)}, bf16[1024,512]{1,0:T(8,128)(2,1)}, u32[]{:S(2)}) copy-start(bf16[1024,512]{1,0:T(8,128)(2,1)} %value_ref.3) | copy-start | bytes 3145732
  0.6 6.1 %copy-start.2 = (bf16[1024,512]{1,0:T(8,128)(2,1)S(1)}, bf16[1024,512]{1,0:T(8,128)(2,1)}, u32[]{:S(2)}) copy-start(bf16[1024,512]{1,0:T(8,128)(2,1)} %key_ref.3) | copy-start | bytes 3145732
  0.7 34.0 %copy-start.1 = (bf16[1024,512]{1,0:T(8,128)(2,1)S(1)}, bf16[1024,512]{1,0:T(8,128)(2,1)}, u32[]{:S(2)}) copy-start(bf16[1024,512]{1,0:T(8,128)(2,1)} %refs_1_.7) | copy-start | bytes 3145732
  3.8 30.9 %copy-start = (bf16[512,2048]{1,0:T(8,128)(2,1)S(1)}, bf16[512,2048]{1,0:T(8,128)(2,1)}, u32[]{:S(2)}) copy-start(bf16[512,2048]{1,0:T(8,128)(2,1)} %refs_2_.6) | copy-start | bytes 6291460
  3.8 10.4 %collective-permute-start.13 = (bf16[64,2048]{1,0:T(8,128)(2,1)S(1)}, bf16[64,2048]{1,0:T(8,128)(2,1)S(1)}, u32[]{:S(2)}, u32[]{:S(2)}) collective-permute-start(bf16[64,2048]{1,0:T(8,128)(2,1)S(1)} %get-tuple-element.27.refs_6_), channel_id=1, source_target_pairs={{0,2},{1,3},{2,0},{3,1},{4,6},{5,7},{6,4},{7,5},{8,10},{9,11},{10,... | collective-permute-start | bytes 786440 | tf_op jit(solution)/shard_map/ppermute | solution.py:241
  6.7 7.4 %collective-permute-start.6 = (bf16[64,2048]{1,0:T(8,128)(2,1)S(1)}, bf16[64,2048]{1,0:T(8,128)(2,1)S(1)}, u32[]{:S(2)}, u32[]{:S(2)}) collective-permute-start(bf16[64,2048]{1,0:T(8,128)(2,1)S(1)} %get-tuple-element.27.refs_6_), channel_id=1, source_target_pairs={{0,1},{1,0},{2,3},{3,2},{4,5},{5,4},{6,7},{7,6},{8,9},{9,8},{10,11... | collective-permute-start | bytes 786440 | tf_op jit(solution)/shard_map/ppermute | solution.py:241
  7.9 5.9 %collective-permute-start = (bf16[4,128,128]{2,1,0:T(8,128)(2,1)S(1)}, bf16[4,128,128]{2,1,0:T(8,128)(2,1)S(1)}, u32[]{:S(2)}, u32[]{:S(2)}) collective-permute-start(bf16[4,128,128]{2,1,0:T(8,128)(2,1)S(1)} %get-tuple-element.15), channel_id=1, source_target_pairs={{0,4},{4,0},{8,12},{12,8},{16,20},{20,16},{24,28},{28,24},{1,5},{5... | collective-permute-start | bytes 393224 | tf_op jit(solution)/shard_map/ppermute | solution.py:215
  9.4 9.8 %collective-permute-start.8 = (bf16[64,2048]{1,0:T(8,128)(2,1)}, bf16[64,2048]{1,0:T(8,128)(2,1)}, u32[]{:S(2)}, u32[]{:S(2)}) collective-permute-start(bf16[64,2048]{1,0:T(8,128)(2,1)} %get-tuple-element.28.refs_4_), channel_id=1, source_target_pairs={{0,2},{1,3},{2,0},{3,1},{4,6},{5,7},{6,4},{7,5},{8,10},{9,11},{10,... | collective-permute-start | bytes 786440 | tf_op jit(solution)/shard_map/ppermute | solution.py:241
  10.0 9.3 %collective-permute-start.4 = (bf16[64,2048]{1,0:T(8,128)(2,1)}, bf16[64,2048]{1,0:T(8,128)(2,1)}, u32[]{:S(2)}, u32[]{:S(2)}) collective-permute-start(bf16[64,2048]{1,0:T(8,128)(2,1)} %get-tuple-element.28.refs_4_), channel_id=1, source_target_pairs={{0,1},{1,0},{2,3},{3,2},{4,5},{5,4},{6,7},{7,6},{8,9},{9,8},{10,11... | collective-permute-start | bytes 786440 | tf_op jit(solution)/shard_map/ppermute | solution.py:241
  13.8 1.7 %copy-start.10 = (bf16[4,128,128]{2,1,0:T(8,128)(2,1)}, bf16[4,128,128]{2,1,0:T(8,128)(2,1)S(1)}, u32[]{:S(2)}) copy-start(bf16[4,128,128]{2,1,0:T(8,128)(2,1)S(1)} %collective-permute-done) | copy-start | bytes 393220
  13.8 11.0 %collective-permute-start.7 = (bf16[64,2048]{1,0:T(8,128)(2,1)}, bf16[64,2048]{1,0:T(8,128)(2,1)}, u32[]{:S(2)}, u32[]{:S(2)}) collective-permute-start(bf16[64,2048]{1,0:T(8,128)(2,1)} %get-tuple-element.29.refs_3_), channel_id=1, source_target_pairs={{0,2},{1,3},{2,0},{3,1},{4,6},{5,7},{6,4},{7,5},{8,10},{9,11},{10,... | collective-permute-start | bytes 786440 | tf_op jit(solution)/shard_map/ppermute | solution.py:241
  14.1 0.7 copy-start.6
  14.1 10.7 %collective-permute-start.3 = (bf16[64,2048]{1,0:T(8,128)(2,1)}, bf16[64,2048]{1,0:T(8,128)(2,1)}, u32[]{:S(2)}, u32[]{:S(2)}) collective-permute-start(bf16[64,2048]{1,0:T(8,128)(2,1)} %get-tuple-element.29.refs_3_), channel_id=1, source_target_pairs={{0,1},{1,0},{2,3},{3,2},{4,5},{5,4},{6,7},{7,6},{8,9},{9,8},{10,11... | collective-permute-start | bytes 786440 | tf_op jit(solution)/shard_map/ppermute | solution.py:241
  14.8 0.7 copy-start.8
  15.5 14.4 %collective-permute-start.9 = (bf16[64,2048]{1,0:T(8,128)(2,1)}, bf16[64,2048]{1,0:T(8,128)(2,1)}, u32[]{:S(2)}, u32[]{:S(2)}) collective-permute-start(bf16[64,2048]{1,0:T(8,128)(2,1)} %get-tuple-element.30.refs_5_), channel_id=1, source_target_pairs={{0,2},{1,3},{2,0},{3,1},{4,6},{5,7},{6,4},{7,5},{8,10},{9,11},{10,... | collective-permute-start | bytes 786440 | tf_op jit(solution)/shard_map/ppermute | solution.py:241
  19.2 11.7 %collective-permute-start.5 = (bf16[64,2048]{1,0:T(8,128)(2,1)}, bf16[64,2048]{1,0:T(8,128)(2,1)}, u32[]{:S(2)}, u32[]{:S(2)}) collective-permute-start(bf16[64,2048]{1,0:T(8,128)(2,1)} %get-tuple-element.30.refs_5_), channel_id=1, source_target_pairs={{0,1},{1,0},{2,3},{3,2},{4,5},{5,4},{6,7},{7,6},{8,9},{9,8},{10,11... | collective-permute-start | bytes 786440 | tf_op jit(solution)/shard_map/ppermute | solution.py:241
  19.2 30.2 %collective-permute-start.14 = (bf16[64,2048]{1,0:T(8,128)(2,1)}, bf16[64,2048]{1,0:T(8,128)(2,1)S(1)}, u32[]{:S(2)}, u32[]{:S(2)}) collective-permute-start(bf16[64,2048]{1,0:T(8,128)(2,1)} %copy-done.6), channel_id=1, source_target_pairs={{0,1},{1,0},{2,3},{3,2},{4,5},{5,4},{6,7},{7,6},{8,9},{9,8},{10,11... | collective-permute-start | bytes 786440 | tf_op jit(solution)/shard_map/ppermute | solution.py:241
  24.8 18.5 %collective-permute-start.11 = (bf16[64,2048]{1,0:T(8,128)(2,1)}, bf16[64,2048]{1,0:T(8,128)(2,1)S(1)}, u32[]{:S(2)}, u32[]{:S(2)}) collective-permute-start(bf16[64,2048]{1,0:T(8,128)(2,1)} %collective-permute-done.8.refs_5_), channel_id=1, source_target_pairs={{0,1},{1,0},{2,3},{3,2},{4,5},{5,4},{6,7},{7,6},{8,9},{9,8},{10,11... | collective-permute-start | bytes 786440 | tf_op jit(solution)/shard_map/ppermute | solution.py:241
  24.8 18.5 %collective-permute-start.10 = (bf16[64,2048]{1,0:T(8,128)(2,1)}, bf16[64,2048]{1,0:T(8,128)(2,1)S(1)}, u32[]{:S(2)}, u32[]{:S(2)}) collective-permute-start(bf16[64,2048]{1,0:T(8,128)(2,1)} %collective-permute-done.7.refs_4_), channel_id=1, source_target_pairs={{0,1},{1,0},{2,3},{3,2},{4,5},{5,4},{6,7},{7,6},{8,9},{9,8},{10,11... | collective-permute-start | bytes 786440 | tf_op jit(solution)/shard_map/ppermute | solution.py:241
  30.0 13.4 %collective-permute-start.12 = (bf16[64,2048]{1,0:T(8,128)(2,1)}, bf16[64,2048]{1,0:T(8,128)(2,1)S(1)}, u32[]{:S(2)}, u32[]{:S(2)}) collective-permute-start(bf16[64,2048]{1,0:T(8,128)(2,1)} %collective-permute-done.9.refs_6_), channel_id=1, source_target_pairs={{0,1},{1,0},{2,3},{3,2},{4,5},{5,4},{6,7},{7,6},{8,9},{9,8},{10,11... | collective-permute-start | bytes 786440 | tf_op jit(solution)/shard_map/ppermute | solution.py:241
  30.9 22.5 %collective-permute-start.1 = (bf16[4,128,128]{2,1,0:T(8,128)(2,1)S(1)}, bf16[4,128,128]{2,1,0:T(8,128)(2,1)S(1)}, u32[]{:S(2)}, u32[]{:S(2)}) collective-permute-start(bf16[4,128,128]{2,1,0:T(8,128)(2,1)S(1)} %fusion.4), channel_id=1, source_target_pairs={{0,8},{4,12},{8,16},{12,20},{16,24},{20,28},{1,9},{5,13},{9,17},{1... | collective-permute-start | bytes 393224 | tf_op jit(solution)/shard_map/ppermute | solution.py:227
  34.7 1.0 %copy-start.9 = (bf16[64,2048]{1,0:T(8,128)(2,1)S(1)}, bf16[64,2048]{1,0:T(8,128)(2,1)}, u32[]{:S(2)}) copy-start(bf16[64,2048]{1,0:T(8,128)(2,1)} %copy-done.8) | copy-start | bytes 786436
  43.4 6.1 %copy-start.7 = (bf16[64,2048]{1,0:T(8,128)(2,1)S(1)}, bf16[64,2048]{1,0:T(8,128)(2,1)}, u32[]{:S(2)}) copy-start(bf16[64,2048]{1,0:T(8,128)(2,1)} %copy-done.6) | copy-start | bytes 786436
  49.4 4.0 %copy-start.11 = (bf16[4,128,128]{2,1,0:T(8,128)(2,1)S(1)}, bf16[4,128,128]{2,1,0:T(8,128)(2,1)}, u32[]{:S(2)}) copy-start(bf16[4,128,128]{2,1,0:T(8,128)(2,1)} %copy-done.10) | copy-start | bytes 393220
  49.5 17.1 %copy-start.3 = (bf16[1024,512]{1,0:T(8,128)(2,1)S(1)}, bf16[1024,512]{1,0:T(8,128)(2,1)}, u32[]{:S(2)}) copy-start(bf16[1024,512]{1,0:T(8,128)(2,1)} %key_ref.3) | copy-start | bytes 3145732
  49.5 17.1 %copy-start.5 = (bf16[1024,512]{1,0:T(8,128)(2,1)S(1)}, bf16[1024,512]{1,0:T(8,128)(2,1)}, u32[]{:S(2)}) copy-start(bf16[1024,512]{1,0:T(8,128)(2,1)} %value_ref.3) | copy-start | bytes 3145732
  51.9 6.1 %collective-permute-start.15 = (bf16[4,128,128]{2,1,0:T(8,128)(2,1)S(1)}, bf16[4,128,128]{2,1,0:T(8,128)(2,1)S(1)}, u32[]{:S(2)}, u32[]{:S(2)}) collective-permute-start(bf16[4,128,128]{2,1,0:T(8,128)(2,1)S(1)} %get-tuple-element.24), channel_id=1, source_target_pairs={{0,4},{4,0},{8,12},{12,8},{16,20},{20,16},{24,28},{28,24},{1,5},{5... | collective-permute-start | bytes 393224 | tf_op jit(solution)/shard_map/ppermute | solution.py:215
  53.5 7.4 %collective-permute-start.2 = (bf16[4,128,128]{2,1,0:T(8,128)(2,1)S(1)}, bf16[4,128,128]{2,1,0:T(8,128)(2,1)S(1)}, u32[]{:S(2)}, u32[]{:S(2)}) collective-permute-start(bf16[4,128,128]{2,1,0:T(8,128)(2,1)S(1)} %fusion.1), channel_id=1, source_target_pairs={{0,16},{4,20},{8,24},{12,28},{1,17},{5,21},{9,25},{13,29},{2,18},{... | collective-permute-start | bytes 393224 | tf_op jit(solution)/shard_map/ppermute | solution.py:227
  58.1 7.0 %collective-permute-start.16 = (bf16[4,128,128]{2,1,0:T(8,128)(2,1)S(1)}, bf16[4,128,128]{2,1,0:T(8,128)(2,1)S(1)}, u32[]{:S(2)}, u32[]{:S(2)}) collective-permute-start(bf16[4,128,128]{2,1,0:T(8,128)(2,1)S(1)} %fusion.5), channel_id=1, source_target_pairs={{8,0},{12,4},{16,8},{20,12},{24,16},{28,20},{9,1},{13,5},{17,9},{2... | collective-permute-start | bytes 393224 | tf_op jit(solution)/shard_map/ppermute | solution.py:227
  65.1 13.4 %collective-permute-start.17 = (bf16[4,128,128]{2,1,0:T(8,128)(2,1)S(1)}, bf16[4,128,128]{2,1,0:T(8,128)(2,1)S(1)}, u32[]{:S(2)}, u32[]{:S(2)}) collective-permute-start(bf16[4,128,128]{2,1,0:T(8,128)(2,1)S(1)} %fusion.3), channel_id=1, source_target_pairs={{16,0},{20,4},{24,8},{28,12},{17,1},{21,5},{25,9},{29,13},{18,2},{... | collective-permute-start | bytes 393224 | tf_op jit(solution)/shard_map/ppermute | solution.py:227

commit v2 on v0

v2 whole, which is shorter than its diff:
```python
import functools

import jax
import jax.numpy as jnp
from jax import lax
from jax.experimental import pallas as pl
from jax.experimental.pallas import tpu as pltpu
from jax.sharding import PartitionSpec as P

HEAD_DIM = 128
KEEP_SCALE = 1.0 / 0.9
F32 = jnp.float32
BF16 = jnp.bfloat16
NT = (((1,), (1,)), ((), ()))
NN = (((1,), (0,)), ((), ()))
TN = (((0,), (0,)), ((), ()))
MIB = 1024 * 1024


def dot(left, right, dims):
    return lax.dot_general(left, right, dims, preferred_element_type=F32)


def vmem():
    return pl.BlockSpec(memory_space=pltpu.VMEM)


def smem():
    return pl.BlockSpec(memory_space=pltpu.SMEM)


def hbm():
    return pl.BlockSpec(memory_space=pltpu.HBM)


def params(mib):
    return pltpu.CompilerParams(vmem_limit_bytes=mib * MIB)


def cost(flops, nbytes):
    return pl.CostEstimate(flops=flops, bytes_accessed=nbytes, transcendentals=0)


def head_cols(h):
    return slice(h * HEAD_DIM, (h + 1) * HEAD_DIM)


def masked_rows(grad, keep):
    return (grad.astype(F32) * keep.astype(F32) * KEEP_SCALE).astype(BF16)


def fetch(source, target, sems, row, rows, pieces):
    size = rows // pieces
    copies = []
    for n in range(pieces):
        copy = pltpu.make_async_copy(
            source.at[pl.ds(row + n * size, size), :],
            target.at[pl.ds(n * size, size), :],
            sems.at[n],
        )
        copy.start()
        copies.append(copy)
    return copies


def mask_body(grad_ref, keep_ref, *refs):
    out_refs, (grad, keep, grad_sems, keep_sems) = refs[:-4], refs[-4:]
    rows = grad.shape[0]
    pieces = keep_sems.shape[0]
    size = rows // pieces
    keep_copies = fetch(keep_ref, keep, keep_sems, 0, rows, pieces)
    grad_copies = fetch(grad_ref, grad, grad_sems, 0, rows, pieces)
    for n in range(pieces):
        keep_copies[n].wait()
        grad_copies[n].wait()
        low, high = n * size, (n + 1) * size
        value = masked_rows(grad[low:high, :], keep[low:high, :])
        out_refs[0][low:high, :] = value
        at = 0
        for ref in out_refs[1:]:
            end = at + ref.shape[0]
            top, bottom = max(low, at), min(high, end)
            if top < bottom:
                ref[top - at : bottom - at, :] = value[top - low : bottom - low, :]
            at = end


def mask_all(out_grad, keep_mask, split):
    rows, model = out_grad.shape
    pieces = 8
    shapes = [rows] + list(split)
    return pl.pallas_call(
        mask_body,
        out_shape=tuple(jax.ShapeDtypeStruct((n, model), BF16) for n in shapes),
        in_specs=[hbm(), hbm()],
        out_specs=(vmem(),) * len(shapes),
        scratch_shapes=[
            pltpu.VMEM((rows, model), BF16),
            pltpu.VMEM((rows, model), jnp.int32),
            pltpu.SemaphoreType.DMA((pieces,)),
            pltpu.SemaphoreType.DMA((pieces,)),
        ],
        compiler_params=params(56),
        cost_estimate=cost(1, 1),
        name="mask_all",
    )(out_grad, keep_mask)


def kv_body(sub, key_ref, value_ref, wide_ref, short_ref, local_ref):
    for h in range(wide_ref.shape[0]):
        total = jnp.zeros(wide_ref.shape[1:], F32)
        for n in range(local_ref.shape[0]):
            local_ref[n, h] = total
            rows = slice(n * sub, (n + 1) * sub)
            total = total + dot(key_ref[rows, head_cols(h)], value_ref[rows, head_cols(h)], TN)
        wide_ref[h] = total
        short_ref[h] = total.astype(BF16)


def kv_state(key_rows, value_rows, sub):
    tokens, width = key_rows.shape
    heads = width // HEAD_DIM
    shape = (heads, HEAD_DIM, HEAD_DIM)
    return pl.pallas_call(
        functools.partial(kv_body, sub),
        out_shape=(
            jax.ShapeDtypeStruct(shape, F32),
            jax.ShapeDtypeStruct(shape, BF16),
            jax.ShapeDtypeStruct((tokens // sub,) + shape, F32),
        ),
        in_specs=[vmem(), vmem()],
        out_specs=(vmem(), vmem(), vmem()),
        compiler_params=params(12),
        cost_estimate=cost(1, 1),
        name="kv_state",
    )(key_rows, value_rows)


def group_body(count, wide_ref, *refs):
    total = wide_ref[...]
    for ref in refs[:count]:
        total = total + ref[...].astype(F32)
    refs[-1][...] = total.astype(BF16)


def after(array, *others):
    return lax.optimization_barrier((array,) + others)[0]


def group_state(wide, received, ties, name):
    received = received[:-1] + [after(received[-1], *ties)]
    return pl.pallas_call(
        functools.partial(group_body, len(received)),
        out_shape=jax.ShapeDtypeStruct(wide.shape, BF16),
        in_specs=[vmem()] * (1 + len(received)),
        out_specs=vmem(),
        compiler_params=params(4),
        cost_estimate=cost(1, 1),
        name=name,
    )(wide, *received)


def grad_body(pieces, sub, befores, last, *refs):
    place_ref, query_ref, weight_ref = refs[:3]
    refs = refs[3:]
    before_refs, refs = refs[:befores], refs[befores:]
    masked_refs, refs = refs[: len(pieces)], refs[len(pieces) :]
    grad_ref, state_ref = refs[:2]
    masked, query = refs[-2:]
    place = place_ref[0]
    spots, at = [], 0
    for ref, (flip, row) in zip(masked_refs, pieces):
        rows = ref.shape[0]
        masked[at : at + rows, :] = ref[...]
        start = pl.multiple_of(jnp.bitwise_xor(place, flip) * sub + row, 16)
        query[at : at + rows, :] = query_ref[pl.ds(start, rows), :]
        spots.append(slice(at, at + rows))
        at += rows
    grad = dot(masked[...], weight_ref[...], NT).astype(BF16)
    grad_ref[...] = grad
    for h in range(state_ref.shape[1]):
        total = None
        for n, rows in enumerate(spots):
            state = dot(query[rows, head_cols(h)], grad[rows, head_cols(h)], TN)
            if last:
                state = state + before_refs[0][n, h]
                other = before_refs[1][n, h]
                total = state + other if total is None else total + (state + other)
            state_ref[n, h] = state
        if last:
            wide_ref, short_ref = refs[2:4]
            wide_ref[h] = total
            short_ref[h] = total.astype(BF16)


def grad_part(place, query_rows, out_weight, sub, befores, pieces, arrays, name):
    width, model = out_weight.shape
    heads = width // HEAD_DIM
    rows = sum(a.shape[0] for a in arrays)
    shape = (heads, HEAD_DIM, HEAD_DIM)
    last = len(befores) > 0
    out_shape = [
        jax.ShapeDtypeStruct((rows, width), BF16),
        jax.ShapeDtypeStruct((len(pieces),) + shape, F32),
    ]
    if last:
        out_shape += [jax.ShapeDtypeStruct(shape, F32), jax.ShapeDtypeStruct(shape, BF16)]
    operands = [place, query_rows, out_weight] + list(befores) + list(arrays)
    return pl.pallas_call(
        functools.partial(grad_body, pieces, sub, len(befores), last),
        out_shape=tuple(out_shape),
        in_specs=[smem()] + [vmem()] * (len(operands) - 1),
        out_specs=tuple(vmem() for _ in out_shape),
        scratch_shapes=[pltpu.VMEM((rows, model), BF16), pltpu.VMEM((rows, width), BF16)],
        compiler_params=params(20),
        cost_estimate=cost(1, 1),
        name=name,
    )(*operands)


def gather_grad(place_ref, grad_refs, places, own_rows, grad):
    place = place_ref[0]
    for ref, pieces in zip(grad_refs, places):
        for at, rows, flip, row in pieces:
            start = pl.multiple_of(jnp.bitwise_xor(place, flip) * own_rows + row, 16)
            grad[pl.ds(start, rows), :] = ref[at : at + rows, :]


def causal(size, turned):
    row_id = lax.broadcasted_iota(jnp.int32, (size, size), 0)
    col_id = lax.broadcasted_iota(jnp.int32, (size, size), 1)
    return col_id >= row_id if turned else row_id >= col_id


def pair_state(ctx_ref, refs, reverse):
    odd = jnp.bitwise_and(ctx_ref[0], 1) == 1
    use = jnp.logical_not(odd) if reverse else odd
    total = None
    for n, ref in enumerate(refs):
        value = ref[0].astype(F32)
        if n == 0:
            value = value * use.astype(F32)
        total = value if total is None else total + value
    return total


def query_body(places, sub, parts, place_ref, ctx_ref, key_ref, value_ref, *refs):
    prev_refs, local_ref, refs = refs[:parts], refs[parts], refs[parts + 1 :]
    grad_refs, (out_ref, grad) = refs[: len(places)], refs[len(places) :]
    gather_grad(place_ref, grad_refs, places, sub, grad)
    prev = pair_state(ctx_ref, prev_refs, False)
    keep = causal(sub, False)
    parts = [slice(n * sub, (n + 1) * sub) for n in range(local_ref.shape[0])]
    scores = [dot(grad[rows, :], value_ref[rows, :], NT) for rows in parts]
    states = [(prev + local_ref[n, 0]).astype(BF16) for n in range(len(parts))]
    totals = [dot(grad[rows, :], state, NT) for rows, state in zip(parts, states)]
    scores = [jnp.where(keep, score, 0.0).astype(BF16) for score in scores]
    for rows, score, total in zip(parts, scores, totals):
        total = total + dot(score, key_ref[rows, :], NN)
        out_ref[rows, :] = total.astype(BF16)


def later_body(places, sub, place_ref, query_ref, key_ref, value_ref, near_ref, far_ref, *refs):
    grad_refs, (key_out, value_out, local_ref, grad) = refs[: len(places)], refs[len(places) :]
    gather_grad(place_ref, grad_refs, places, sub, grad)
    place = place_ref[0]
    states = [near_ref[0, 0], near_ref[1, 0], far_ref[0, 0], far_ref[1, 0]]
    keep = causal(sub, True)
    parts = [slice(n * sub, (n + 1) * sub) for n in range(local_ref.shape[0])]
    masked = lambda scores: [jnp.where(keep, score, 0.0).astype(BF16) for score in scores]
    scores = [dot(value_ref[rows, :], grad[rows, :], NT) for rows in parts]
    attn = [dot(key_ref[rows, :], query_ref[rows, :], NT) for rows in parts]
    scores = masked(scores)
    for rows, score in zip(parts, scores):
        key_out[rows, :] = dot(score, query_ref[rows, :], NN)
    attn = masked(attn)
    for rows, score in zip(parts, attn):
        value_out[rows, :] = dot(score, grad[rows, :], NN)
    for n in range(len(parts)):
        total = None
        for flip, state in enumerate(states):
            part = jnp.where(jnp.bitwise_xor(place, flip) > n, state, 0.0)
            total = part if total is None else total + part
        local_ref[n, 0] = total


def column(rows):
    return pl.BlockSpec((rows, HEAD_DIM), lambda h: (0, h))


def head_state():
    return pl.BlockSpec((1, HEAD_DIM, HEAD_DIM), lambda h: (h, 0, 0))


def local_states(count):
    return pl.BlockSpec((count, 1, HEAD_DIM, HEAD_DIM), lambda h: (0, h, 0, 0))


def query_products(place, ctx, key_rows, value_rows, prevs, local_prev, grads, places, sub):
    tokens, width = key_rows.shape
    return pl.pallas_call(
        functools.partial(query_body, places, sub, len(prevs)),
        out_shape=jax.ShapeDtypeStruct((tokens, width), BF16),
        grid=(width // HEAD_DIM,),
        in_specs=[smem(), smem()]
        + [column(tokens)] * 2
        + [head_state()] * len(prevs)
        + [local_states(local_prev.shape[0])]
        + [column(g.shape[0]) for g in grads],
        out_specs=column(tokens),
        scratch_shapes=[pltpu.VMEM((tokens, HEAD_DIM), BF16)],
        compiler_params=params(16),
        cost_estimate=cost(4 * tokens * tokens * width, 8 * tokens * width),
        name="query_products",
    )(place, ctx, key_rows, value_rows, *prevs, local_prev, *grads)


def later_products(place, query_rows, key_rows, value_rows, near, far, grads, places, sub):
    tokens, width = key_rows.shape
    heads, count = width // HEAD_DIM, tokens // sub
    return pl.pallas_call(
        functools.partial(later_body, places, sub),
        out_shape=(
            jax.ShapeDtypeStruct((tokens, width), F32),
            jax.ShapeDtypeStruct((tokens, width), F32),
            jax.ShapeDtypeStruct((count, heads, HEAD_DIM, HEAD_DIM), F32),
        ),
        grid=(heads,),
        in_specs=[smem()]
        + [column(tokens)] * 3
        + [local_states(near.shape[0]), local_states(far.shape[0])]
        + [column(g.shape[0]) for g in grads],
        out_specs=(column(tokens), column(tokens), local_states(count)),
        scratch_shapes=[pltpu.VMEM((tokens, HEAD_DIM), BF16)],
        compiler_params=params(16),
        cost_estimate=cost(8 * tokens * tokens * width, 10 * tokens * width),
        name="later_products",
    )(place, query_rows, key_rows, value_rows, near, far, *grads)


def end_body(sub, ctx_ref, key_ref, value_ref, key_part, value_part, local_ref, *refs):
    later = pair_state(ctx_ref, refs[:-2], True)
    key_out, value_out = refs[-2:]
    for n in range(local_ref.shape[0]):
        rows = slice(n * sub, (n + 1) * sub)
        state = (later + local_ref[n, 0]).astype(BF16)
        key_out[rows, :] = (key_part[rows, :] + dot(value_ref[rows, :], state, NT)).astype(BF16)
        value_out[rows, :] = (value_part[rows, :] + dot(key_ref[rows, :], state, NN)).astype(BF16)


def end_products(ctx, key_rows, value_rows, key_part, value_part, local_next, nexts, sub):
    tokens, width = key_rows.shape
    return pl.pallas_call(
        functools.partial(end_body, sub),
        out_shape=(jax.ShapeDtypeStruct((tokens, width), BF16),) * 2,
        grid=(width // HEAD_DIM,),
        in_specs=[smem()]
        + [column(tokens)] * 4
        + [local_states(local_next.shape[0])]
        + [head_state()] * len(nexts),
        out_specs=(column(tokens), column(tokens)),
        compiler_params=params(16),
        cost_estimate=cost(4 * tokens * width * HEAD_DIM, 16 * tokens * width),
        name="end_products",
    )(ctx, key_rows, value_rows, key_part, value_part, local_next, *nexts)


def scan_step(payload, axis, reach, reverse):
    size = lax.axis_size(axis)
    if reach == 1:
        pairs = [(i, i ^ 1) for i in range(size)]
    elif reverse:
        pairs = [(i + reach, i) for i in range(size - reach)]
    else:
        pairs = [(i, i + reach) for i in range(size - reach)]
    return lax.ppermute(payload, axis, pairs)


def scan_states(wide, short, axis, reverse, ties, name, between=None):
    received, sents, reach, payload = [], [short], 1, short
    size = lax.axis_size(axis)
    while reach < size:
        if reach > 1:
            step_ties = ties[len(received) - 1 : len(received)]
            if between is not None and reach > 2:
                step_ties = [between(payload)]
                between = None
            payload = group_state(wide, received, step_ties, "%s_%d" % (name, reach))
            sents.append(payload)
        received.append(scan_step(payload, axis, reach, reverse))
        reach *= 2
    if between is not None:
        between(payload)
    return received, sents


def per_device(out_grad, keep_mask, out_weight, query_rows, key_rows, value_rows):
    size = lax.axis_size("head")
    place = lax.axis_index("head").astype(jnp.int32).reshape(1)
    ctx = lax.axis_index("ctx").astype(jnp.int32).reshape(1)
    own_rows = out_grad.shape[0]
    split = 9 * own_rows // 16

    def swap(array, distance):
        return lax.ppermute(array, "head", [(i, i ^ distance) for i in range(size)])

    own, first, last = mask_all(out_grad, keep_mask, (split, own_rows - split))
    near = swap(own, 1)
    far_first, far_last = swap(first, 2), swap(last, 2)
    kv_wide, kv_short, local_prev = kv_state(key_rows, value_rows, own_rows)

    part = functools.partial(grad_part, place, query_rows, out_weight, own_rows)
    grads, places, states = [], [], []

    def run(befores, pieces, arrays, name):
        got = part(befores, pieces, arrays, name)
        at, spots = 0, []
        for (flip, row), array in zip(pieces, arrays):
            spots.append((at, array.shape[0], flip, row))
            at += array.shape[0]
        grads.append(got[0])
        places.append(tuple(spots))
        states.append(got[1])
        return got

    def near_part(sent):
        return run([], ((0, 0), (1, 0)), [own, after(near, sent)], "grad_near")[1]

    prevs, _ = scan_states(kv_wide, kv_short, "ctx", False, [], "prev", near_part)

    far_first = after(far_first, prevs[-1], states[0])
    run([], ((2, 0), (3, 0)), [far_first, swap(far_first, 1)], "grad_far")
    _, far, wide, short = run(
        [states[1], states[0]],
        ((2, split), (3, split)),
        [far_last, swap(far_last, 1)],
        "grad_last",
    )

    query_out = query_products(
        place, ctx, key_rows, value_rows, prevs, local_prev, grads, tuple(places), own_rows
    )
    nexts, _ = scan_states(wide, short, "ctx", True, [query_out], "next")
    key_part, value_part, local_next = later_products(
        place, query_rows, key_rows, value_rows, states[0], far, grads, tuple(places), own_rows
    )
    key_out, value_out = end_products(
        ctx, key_rows, value_rows, key_part, value_part, local_next, nexts, own_rows
    )
    return query_out, key_out, value_out


def solution(mesh):
    placed = (
        P(("ctx", "head"), None),
        P(("ctx", "head"), None),
        P("head", None),
        P("ctx", "head"),
        P("ctx", "head"),
        P("ctx", "head"),
    )
    return jax.shard_map(
        per_device,
        mesh=mesh,
        in_specs=placed,
        out_specs=(P("ctx", "head"), P("ctx", "head"), P("ctx", "head")),
        check_vma=False,
    )
```

time: 203 us -> 66.2 us (0.33)
  waiting for transfers between devices: 119 us -> 18.8 us
  matrix products: 32.9 us -> 0 us
  Pallas kernels: 0 us -> 25.1 us
  other arithmetic: 17.9 us -> 0 us
  starting transfers between devices: 3.83 us -> 17.8 us
  between operations: 13.9 us -> 0.84 us
  local copies, waits for them, and re-layouts: 14 us -> 3.03 us
    all_gather x3 -> x0, waiting for transfers between devices: 105 us -> none  [the longest x1 60.7 us: per_device(): lax.all_gather(out_weight, 'head', axis=0, tiled=True)]
    dot_general x10 -> x0, matrix products: 32.9 us -> none  [the longest x1 7.22 us: per_device(): jnp.einsum('hts,thf->shf', attn_scores, grad_heads, preferred_element_typ...]
    pallas_call x0 -> x12, Pallas kernels: none -> 25.1 us  [the longest x3 7.39 us: grad_part(): pl.pallas_call(functools.partial(grad_body, pieces, sub, len(befores), la...]
    ppermute x0 -> x11, waiting for transfers between devices: none -> 18.8 us  [the longest x6 17 us: scan_step(): return lax.ppermute(payload, axis, pairs)]
    ppermute x0 -> x11, starting transfers between devices: none -> 17.8 us  [the longest x6 13.7 us: scan_step(): return lax.ppermute(payload, axis, pairs)]
    select_n x16 -> x0, other arithmetic: 16.6 us -> none  [step(): return jnp.where(reached, new, before)]
    all_to_all x1 -> x0, waiting for transfers between devices: 12.9 us -> none  [per_device(): lax.all_to_all(token_grad, 'head', split_axis=1, concat_axis=0, tiled=True)]
    unnamed x17 -> x26, local copies, waits for them, and re-layouts: 9.37 us -> 3.03 us
  transfers between devices with their start and end apart: 4 -> 11, of which waited for: 4 -> 5; matrix products, arithmetic and copies ran while one was open for 20% -> 0% of each run, Pallas kernels for 0% -> 24%
where the time goes in v2:
time: 66.2 us; the launch traced here: 65.6 us
  Pallas kernels  25.1 us (38%)
  waiting for transfers between devices  18.8 us (28%)
  starting transfers between devices  17.8 us (27%)
  local copies, waits for them, and re-layouts  3.03 us (5%)
  between operations  0.84 us (1%)
    ppermute x6, waiting for transfers between devices, scan_step(): return lax.ppermute(payload, axis, pairs)  17 us
    ppermute x6, starting transfers between devices, scan_step(): return lax.ppermute(payload, axis, pairs)  13.7 us
    pallas_call x3, Pallas kernels, grad_part(): pl.pallas_call(functools.partial(grad_body, pieces, sub, len(befores), la...  7.39 us
    pallas_call x1, Pallas kernels, later_products(): pl.pallas_call(functools.partial(later_body, places, sub), out_shape=(jax...  4.58 us
    pallas_call x1, Pallas kernels, query_products(): pl.pallas_call(functools.partial(query_body, places, sub, len(prevs)), ou...  4.17 us
    ppermute x5, starting transfers between devices, swap(): return lax.ppermute(array, 'head', [(i, i ^ distance) for i in range(size)])  4.13 us
    pallas_call x1, Pallas kernels, mask_all(): pl.pallas_call(mask_body, out_shape=tuple((jax.ShapeDtypeStruct((n, model...  3.42 us
    pallas_call x1, Pallas kernels, end_products(): pl.pallas_call(functools.partial(end_body, sub), out_shape=(jax.ShapeDtyp...  3.27 us
  transfers between devices with their start and end apart: 11, of which 5 were waited for; matrix products, arithmetic and copies ran while one was open for 0% of the time, Pallas kernels for 24%

profile of v2, /device:TPU:0, one launch (start us, length us, event | category | flops | bytes accessed | tf_op | source)
XLA Modules:
  0.0 65.6 jit_solution(10050316693226873784)
XLA Ops:
  0.6 0.0 copy-start.4
  0.6 0.0 copy-start.2
  0.7 3.4 %mask_all.1 = (bf16[256,2048]{1,0:T(8,128)(2,1)}, bf16[144,2048]{1,0:T(8,128)(2,1)}, bf16[112,2048]{1,0:T(8,128)(2,1)}) custom-call(bf16[256,2048]{1,0:T(8,128)(2,1)} %grad_ref.1, s32[256,2048]{1,0:T(8,128)} %keep_ref.1), custom_call_target="tpu_custom_call" | custom-call | flops 1 | bytes 1 | tf_op jit(solution)/shard_map/mask_all/pallas_call | solution.py:92
  4.1 0.0 copy-start
  4.1 0.5 collective-permute-start.2
  4.6 2.6 %collective-permute-start.4 = (bf16[144,2048]{1,0:T(8,128)(2,1)}, bf16[144,2048]{1,0:T(8,128)(2,1)}, u32[]{:S(2)}, u32[]{:S(2)}) collective-permute-start(bf16[144,2048]{1,0:T(8,128)(2,1)} %get-tuple-element.34), channel_id=1, source_target_pairs={{0,2},{1,3},{2,0},{3,1},{4,6},{5,7},{6,4},{7,5},{8,10},{9,11},{10,... | collective-permute-start | bytes 1769480 | tf_op jit(solution)/shard_map/ppermute | solution.py:405
  7.2 0.5 kv_state.1
  7.7 0.0 copy-start.9
  7.7 1.0 %copy-done.9 = f32[4,4,128,128]{3,2,1,0:T(8,128)} copy-done((f32[4,4,128,128]{3,2,1,0:T(8,128)}, f32[4,4,128,128]{3,2,1,0:T(8,128)S(1)}, u32[]{:S(2)}) %copy-start.9) | copy-done | bytes 1048600
  8.7 1.5 %collective-permute-start = (bf16[4,128,128]{2,1,0:T(8,128)(2,1)S(1)}, bf16[4,128,128]{2,1,0:T(8,128)(2,1)S(1)}, u32[]{:S(2)}, u32[]{:S(2)}) collective-permute-start(bf16[4,128,128]{2,1,0:T(8,128)(2,1)S(1)} %get-tuple-element.26), channel_id=1, source_target_pairs={{0,4},{4,0},{8,12},{12,8},{16,20},{20,16},{24,28},{28,24},{1,5},{5... | collective-permute-start | bytes 393224 | tf_op jit(solution)/shard_map/ppermute | solution.py:376
  10.2 0.5 collective-permute-start.6
  10.7 3.5 %collective-permute-done.refs_0_ = bf16[4,128,128]{2,1,0:T(8,128)(2,1)S(1)} collective-permute-done((bf16[4,128,128]{2,1,0:T(8,128)(2,1)S(1)}, bf16[4,128,128]{2,1,0:T(8,128)(2,1)S(1)}, u32[]{:S(2)}, u32[]{:S(2)}) %collective-permute-start) | collective-permute-done | bytes 131104 | tf_op jit(solution)/shard_map/ppermute | solution.py:376
  14.2 0.7 %prev_2.1 = bf16[4,128,128]{2,1,0:T(8,128)(2,1)} custom-call(f32[4,128,128]{2,1,0:T(8,128)S(1)} %get-tuple-element.27.wide_ref, bf16[4,128,128]{2,1,0:T(8,128)(2,1)S(1)} %collective-permute-done.refs_0_), custom_call_target="tpu_custom_call" | custom-call | flops 1 | bytes 1 | tf_op jit(solution)/shard_map/prev_2/pallas_call | solution.py:152
  14.9 4.1 %collective-permute-start.1 = (bf16[4,128,128]{2,1,0:T(8,128)(2,1)}, bf16[4,128,128]{2,1,0:T(8,128)(2,1)}, u32[]{:S(2)}, u32[]{:S(2)}) collective-permute-start(bf16[4,128,128]{2,1,0:T(8,128)(2,1)} %prev_2.1), channel_id=1, source_target_pairs={{0,8},{4,12},{8,16},{12,20},{16,24},{20,28},{1,9},{5,13},{9,17},{1... | collective-permute-start | bytes 393224 | tf_op jit(solution)/shard_map/ppermute | solution.py:376
  19.0 1.2 %copy-done.6 = bf16[256,2048]{1,0:T(8,128)(2,1)S(1)} copy-done((bf16[256,2048]{1,0:T(8,128)(2,1)S(1)}, bf16[256,2048]{1,0:T(8,128)(2,1)}, u32[]{:S(2)}) %copy-start.6) | copy-done | bytes 1048600
  20.3 2.8 %grad_near.1 = (bf16[512,512]{1,0:T(8,128)(2,1)S(1)}, f32[2,4,128,128]{3,2,1,0:T(8,128)S(1)}) custom-call(s32[1]{0:T(128)} %bitcast.refs_0_.place_ref, bf16[1024,512]{1,0:T(8,128)(2,1)S(1)} %copy-done.1, bf16[512,2048]{1,0:T(8,128)(2,1)S(1)} %copy-done, bf16[256,2048]{1,0:T(8,128)(2,1)S(1)} %copy-done.6, bf16[256,2048]{1,0:T(8,128)(2,1)} %collective-permute-done.2.refs_4_), custom_call_target="tpu_custom_call" | custom-call | flops 1 | bytes 1 | tf_op jit(solution)/shard_map/grad_near/pallas_call | solution.py:209
  23.1 0.8 %copy-done.11 = bf16[512,512]{1,0:T(8,128)(2,1)} copy-done((bf16[512,512]{1,0:T(8,128)(2,1)}, bf16[512,512]{1,0:T(8,128)(2,1)S(1)}, u32[]{:S(2)}) %copy-start.11) | copy-done | bytes 524312
  23.9 1.1 %prev_4.1 = bf16[4,128,128]{2,1,0:T(8,128)(2,1)S(1)} custom-call(f32[4,128,128]{2,1,0:T(8,128)S(1)} %get-tuple-element.27.wide_ref, bf16[4,128,128]{2,1,0:T(8,128)(2,1)S(1)} %collective-permute-done.refs_0_, bf16[4,128,128]{2,1,0:T(8,128)(2,1)} %collective-permute-done.1.refs_1_), custom_call_target="tpu_custom_call" | custom-call | flops 1 | bytes 1 | tf_op jit(solution)/shard_map/prev_4/pallas_call | solution.py:152
  24.9 3.9 %collective-permute-start.3 = (bf16[4,128,128]{2,1,0:T(8,128)(2,1)S(1)}, bf16[4,128,128]{2,1,0:T(8,128)(2,1)S(1)}, u32[]{:S(2)}, u32[]{:S(2)}) collective-permute-start(bf16[4,128,128]{2,1,0:T(8,128)(2,1)S(1)} %prev_4.1), channel_id=1, source_target_pairs={{0,16},{4,20},{8,24},{12,28},{1,17},{5,21},{9,25},{13,29},{2,18},{... | collective-permute-start | bytes 393224 | tf_op jit(solution)/shard_map/ppermute | solution.py:376
  28.8 2.5 %collective-permute-done.3.refs_2_ = bf16[4,128,128]{2,1,0:T(8,128)(2,1)S(1)} collective-permute-done((bf16[4,128,128]{2,1,0:T(8,128)(2,1)S(1)}, bf16[4,128,128]{2,1,0:T(8,128)(2,1)S(1)}, u32[]{:S(2)}, u32[]{:S(2)}) %collective-permute-start.3) | collective-permute-done | bytes 131104 | tf_op jit(solution)/shard_map/ppermute | solution.py:376
  31.3 0.5 collective-permute-start.7
  31.8 1.8 %collective-permute-done.5.refs_4_ = bf16[144,2048]{1,0:T(8,128)(2,1)} collective-permute-done((bf16[144,2048]{1,0:T(8,128)(2,1)}, bf16[144,2048]{1,0:T(8,128)(2,1)}, u32[]{:S(2)}, u32[]{:S(2)}) %collective-permute-start.5) | collective-permute-done | bytes 589856 | tf_op jit(solution)/shard_map/ppermute | solution.py:405
  33.7 2.3 %grad_far.1 = (bf16[288,512]{1,0:T(8,128)(2,1)S(1)}, f32[2,4,128,128]{3,2,1,0:T(8,128)S(1)}) custom-call(s32[1]{0:T(128)} %bitcast.refs_0_.place_ref, bf16[1024,512]{1,0:T(8,128)(2,1)S(1)} %copy-done.1, bf16[512,2048]{1,0:T(8,128)(2,1)S(1)} %copy-done, bf16[144,2048]{1,0:T(8,128)(2,1)} %collective-permute-done.4.refs_3_, ...), custom_call_target="tpu_custom_call" | custom-call | flops 1 | bytes 1 | tf_op jit(solution)/shard_map/grad_far/pallas_call | solution.py:209
  36.0 2.3 %grad_last.1 = (bf16[224,512]{1,0:T(8,128)(2,1)S(1)}, f32[2,4,128,128]{3,2,1,0:T(8,128)S(1)}, f32[4,128,128]{2,1,0:T(8,128)S(1)}, bf16[4,128,128]{2,1,0:T(8,128)(2,1)S(1)}) custom-call(s32[1]{0:T(128)} %bitcast.refs_0_.place_ref, bf16[1024,512]{1,0:T(8,128)(2,1)S(1)} %copy-done.1, bf16[512,2048]{1,0:T(8,128)(2,1)S(1)} %copy-done, ...), custom_call_target="tpu_custom_call" | custom-call | flops 1 | bytes 1 | tf_op jit(solution)/shard_map/grad_last/pallas_call | solution.py:209
  38.3 1.6 %collective-permute-start.8 = (bf16[4,128,128]{2,1,0:T(8,128)(2,1)S(1)}, bf16[4,128,128]{2,1,0:T(8,128)(2,1)S(1)}, u32[]{:S(2)}, u32[]{:S(2)}) collective-permute-start(bf16[4,128,128]{2,1,0:T(8,128)(2,1)S(1)} %get-tuple-element.44), channel_id=1, source_target_pairs={{0,4},{4,0},{8,12},{12,8},{16,20},{20,16},{24,28},{28,24},{1,5},{5... | collective-permute-start | bytes 393224 | tf_op jit(solution)/shard_map/ppermute | solution.py:376
  39.9 4.2 %query_products.1 = bf16[1024,512]{1,0:T(8,128)(2,1)} custom-call(s32[1]{0:T(128)} %bitcast.refs_0_.place_ref, s32[1]{0:T(128)} %bitcast.1.ctx_ref, bf16[1024,512]{1,0:T(8,128)(2,1)S(1)} %copy-done.3, bf16[1024,512]{1,0:T(8,128)(2,1)S(1)} %copy-done.5, bf16[4,128,128]{2,1,0:T(8,128)(2,1)S(1)} %collective-permute-done.refs_0_, ...), custom_call_target="tpu_custom_call" | custom-call | flops 2147483648 | bytes 4194304 | tf_op jit(solution)/shard_map/query_products/pallas_call | solution.py:301
  44.1 1.3 %collective-permute-start.9 = (bf16[4,128,128]{2,1,0:T(8,128)(2,1)S(1)}, bf16[4,128,128]{2,1,0:T(8,128)(2,1)S(1)}, u32[]{:S(2)}, u32[]{:S(2)}) collective-permute-start(bf16[4,128,128]{2,1,0:T(8,128)(2,1)S(1)} %next_2.1), channel_id=1, source_target_pairs={{8,0},{12,4},{16,8},{20,12},{24,16},{28,20},{9,1},{13,5},{17,9},{2... | collective-permute-start | bytes 393224 | tf_op jit(solution)/shard_map/ppermute | solution.py:376
  45.4 6.6 %collective-permute-done.9.refs_1_ = bf16[4,128,128]{2,1,0:T(8,128)(2,1)S(1)} collective-permute-done((bf16[4,128,128]{2,1,0:T(8,128)(2,1)S(1)}, bf16[4,128,128]{2,1,0:T(8,128)(2,1)S(1)}, u32[]{:S(2)}, u32[]{:S(2)}) %collective-permute-start.9) | collective-permute-done | bytes 131104 | tf_op jit(solution)/shard_map/ppermute | solution.py:376
  52.0 1.3 %collective-permute-start.10 = (bf16[4,128,128]{2,1,0:T(8,128)(2,1)S(1)}, bf16[4,128,128]{2,1,0:T(8,128)(2,1)S(1)}, u32[]{:S(2)}, u32[]{:S(2)}) collective-permute-start(bf16[4,128,128]{2,1,0:T(8,128)(2,1)S(1)} %next_4.1), channel_id=1, source_target_pairs={{16,0},{20,4},{24,8},{28,12},{17,1},{21,5},{25,9},{29,13},{18,2},{... | collective-permute-start | bytes 393224 | tf_op jit(solution)/shard_map/ppermute | solution.py:376
  53.3 4.6 %later_products.1 = (f32[1024,512]{1,0:T(8,128)S(1)}, f32[1024,512]{1,0:T(8,128)S(1)}, f32[4,4,128,128]{3,2,1,0:T(8,128)S(1)}) custom-call(s32[1]{0:T(128)} %bitcast.refs_0_.place_ref, bf16[1024,512]{1,0:T(8,128)(2,1)S(1)} %copy-done.1, bf16[1024,512]{1,0:T(8,128)(2,1)S(1)} %copy-done.3, bf16[1024,512]{1,0:T(8,128)(2,1)S(1)} %copy-done.5, ...), custom_call_target="tpu_custom_call" | custom-call | flops 4294967296 | bytes 5242880 | tf_op jit(solution)/shard_map/later_products/pallas_call | solution.py:321
  57.9 4.4 %collective-permute-done.10.refs_2_ = bf16[4,128,128]{2,1,0:T(8,128)(2,1)S(1)} collective-permute-done((bf16[4,128,128]{2,1,0:T(8,128)(2,1)S(1)}, bf16[4,128,128]{2,1,0:T(8,128)(2,1)S(1)}, u32[]{:S(2)}, u32[]{:S(2)}) %collective-permute-start.10) | collective-permute-done | bytes 131104 | tf_op jit(solution)/shard_map/ppermute | solution.py:376
  62.4 3.3 %end_products.1 = (bf16[1024,512]{1,0:T(8,128)(2,1)}, bf16[1024,512]{1,0:T(8,128)(2,1)}) custom-call(s32[1]{0:T(128)} %bitcast.1.ctx_ref, bf16[1024,512]{1,0:T(8,128)(2,1)S(1)} %copy-done.3, bf16[1024,512]{1,0:T(8,128)(2,1)S(1)} %copy-done.5, f32[1024,512]{1,0:T(8,128)S(1)} %get-tuple-element.41.key_part, f32[1024,512]{1,0:T(8,128)S(1)} %get-tuple-element.42.value_part, ...), custom_call_target="tpu_custom_call" | custom-call | flops 268435456 | bytes 8388608 | tf_op jit(solution)/shard_map/end_products/pallas_call | solution.py:353
  (28 shorter events, 0.1 us)
Async XLA Ops:
  0.6 6.6 %copy-start.4 = (bf16[1024,512]{1,0:T(8,128)(2,1)S(1)}, bf16[1024,512]{1,0:T(8,128)(2,1)}, u32[]{:S(2)}) copy-start(bf16[1024,512]{1,0:T(8,128)(2,1)} %value_ref.7) | copy-start | bytes 3145732
  0.6 6.6 %copy-start.2 = (bf16[1024,512]{1,0:T(8,128)(2,1)S(1)}, bf16[1024,512]{1,0:T(8,128)(2,1)}, u32[]{:S(2)}) copy-start(bf16[1024,512]{1,0:T(8,128)(2,1)} %key_ref.7) | copy-start | bytes 3145732
  0.7 18.4 %copy-start.1 = (bf16[1024,512]{1,0:T(8,128)(2,1)S(1)}, bf16[1024,512]{1,0:T(8,128)(2,1)}, u32[]{:S(2)}) copy-start(bf16[1024,512]{1,0:T(8,128)(2,1)} %query_ref.1) | copy-start | bytes 3145732
  4.1 14.9 %copy-start = (bf16[512,2048]{1,0:T(8,128)(2,1)S(1)}, bf16[512,2048]{1,0:T(8,128)(2,1)}, u32[]{:S(2)}) copy-start(bf16[512,2048]{1,0:T(8,128)(2,1)} %refs_2_.5) | copy-start | bytes 6291460
  4.1 14.9 %collective-permute-start.2 = (bf16[256,2048]{1,0:T(8,128)(2,1)}, bf16[256,2048]{1,0:T(8,128)(2,1)}, u32[]{:S(2)}, u32[]{:S(2)}) collective-permute-start(bf16[256,2048]{1,0:T(8,128)(2,1)} %get-tuple-element.28.refs_3_), channel_id=1, source_target_pairs={{0,1},{1,0},{2,3},{3,2},{4,5},{5,4},{6,7},{7,6},{8,9},{9,8},{10,11... | collective-permute-start | bytes 3145736 | tf_op jit(solution)/shard_map/ppermute | solution.py:405
  4.6 24.2 %collective-permute-start.4 = (bf16[144,2048]{1,0:T(8,128)(2,1)}, bf16[144,2048]{1,0:T(8,128)(2,1)}, u32[]{:S(2)}, u32[]{:S(2)}) collective-permute-start(bf16[144,2048]{1,0:T(8,128)(2,1)} %get-tuple-element.34), channel_id=1, source_target_pairs={{0,2},{1,3},{2,0},{3,1},{4,6},{5,7},{6,4},{7,5},{8,10},{9,11},{10,... | collective-permute-start | bytes 1769480 | tf_op jit(solution)/shard_map/ppermute | solution.py:405
  7.7 1.0 %copy-start.9 = (f32[4,4,128,128]{3,2,1,0:T(8,128)}, f32[4,4,128,128]{3,2,1,0:T(8,128)S(1)}, u32[]{:S(2)}) copy-start(f32[4,4,128,128]{3,2,1,0:T(8,128)S(1)} %get-tuple-element.32.refs_3_) | copy-start | bytes 3145732
  8.7 5.6 %collective-permute-start = (bf16[4,128,128]{2,1,0:T(8,128)(2,1)S(1)}, bf16[4,128,128]{2,1,0:T(8,128)(2,1)S(1)}, u32[]{:S(2)}, u32[]{:S(2)}) collective-permute-start(bf16[4,128,128]{2,1,0:T(8,128)(2,1)S(1)} %get-tuple-element.26), channel_id=1, source_target_pairs={{0,4},{4,0},{8,12},{12,8},{16,20},{20,16},{24,28},{28,24},{1,5},{5... | collective-permute-start | bytes 393224 | tf_op jit(solution)/shard_map/ppermute | solution.py:376
  10.2 21.1 %collective-permute-start.6 = (bf16[112,2048]{1,0:T(8,128)(2,1)}, bf16[112,2048]{1,0:T(8,128)(2,1)}, u32[]{:S(2)}, u32[]{:S(2)}) collective-permute-start(bf16[112,2048]{1,0:T(8,128)(2,1)} %get-tuple-element.38), channel_id=1, source_target_pairs={{0,2},{1,3},{2,0},{3,1},{4,6},{5,7},{6,4},{7,5},{8,10},{9,11},{10,... | collective-permute-start | bytes 1376264 | tf_op jit(solution)/shard_map/ppermute | solution.py:405
  14.9 9.0 %collective-permute-start.1 = (bf16[4,128,128]{2,1,0:T(8,128)(2,1)}, bf16[4,128,128]{2,1,0:T(8,128)(2,1)}, u32[]{:S(2)}, u32[]{:S(2)}) collective-permute-start(bf16[4,128,128]{2,1,0:T(8,128)(2,1)} %prev_2.1), channel_id=1, source_target_pairs={{0,8},{4,12},{8,16},{12,20},{16,24},{20,28},{1,9},{5,13},{9,17},{1... | collective-permute-start | bytes 393224 | tf_op jit(solution)/shard_map/ppermute | solution.py:376
  19.0 1.2 %copy-start.6 = (bf16[256,2048]{1,0:T(8,128)(2,1)S(1)}, bf16[256,2048]{1,0:T(8,128)(2,1)}, u32[]{:S(2)}) copy-start(bf16[256,2048]{1,0:T(8,128)(2,1)} %get-tuple-element.28.refs_3_) | copy-start | bytes 3145732
  23.1 0.8 %copy-start.11 = (bf16[512,512]{1,0:T(8,128)(2,1)}, bf16[512,512]{1,0:T(8,128)(2,1)S(1)}, u32[]{:S(2)}) copy-start(bf16[512,512]{1,0:T(8,128)(2,1)S(1)} %get-tuple-element.33.refs_4_.refs_0_) | copy-start | bytes 1572868
  23.8 1.1 %copy-start.7 = (f32[2,4,128,128]{3,2,1,0:T(8,128)}, f32[2,4,128,128]{3,2,1,0:T(8,128)S(1)}, u32[]{:S(2)}) copy-start(f32[2,4,128,128]{3,2,1,0:T(8,128)S(1)} %get-tuple-element.30.refs_4_.near_ref) | copy-start | bytes 1572868
  24.9 6.4 %collective-permute-start.3 = (bf16[4,128,128]{2,1,0:T(8,128)(2,1)S(1)}, bf16[4,128,128]{2,1,0:T(8,128)(2,1)S(1)}, u32[]{:S(2)}, u32[]{:S(2)}) collective-permute-start(bf16[4,128,128]{2,1,0:T(8,128)(2,1)S(1)} %prev_4.1), channel_id=1, source_target_pairs={{0,16},{4,20},{8,24},{12,28},{1,17},{5,21},{9,25},{13,29},{2,18},{... | collective-permute-start | bytes 393224 | tf_op jit(solution)/shard_map/ppermute | solution.py:376
  31.3 2.3 %collective-permute-start.5 = (bf16[144,2048]{1,0:T(8,128)(2,1)}, bf16[144,2048]{1,0:T(8,128)(2,1)}, u32[]{:S(2)}, u32[]{:S(2)}) collective-permute-start(bf16[144,2048]{1,0:T(8,128)(2,1)} %collective-permute-done.4.refs_3_), channel_id=1, source_target_pairs={{0,1},{1,0},{2,3},{3,2},{4,5},{5,4},{6,7},{7,6},{8,9},{9,8},{10,11... | collective-permute-start | bytes 1769480 | tf_op jit(solution)/shard_map/ppermute | solution.py:405
  31.3 4.7 %collective-permute-start.7 = (bf16[112,2048]{1,0:T(8,128)(2,1)}, bf16[112,2048]{1,0:T(8,128)(2,1)}, u32[]{:S(2)}, u32[]{:S(2)}) collective-permute-start(bf16[112,2048]{1,0:T(8,128)(2,1)} %collective-permute-done.6.refs_5_), channel_id=1, source_target_pairs={{0,1},{1,0},{2,3},{3,2},{4,5},{5,4},{6,7},{7,6},{8,9},{9,8},{10,11... | collective-permute-start | bytes 1376264 | tf_op jit(solution)/shard_map/ppermute | solution.py:405
  31.8 4.2 %copy-start.8 = (f32[2,4,128,128]{3,2,1,0:T(8,128)S(1)}, f32[2,4,128,128]{3,2,1,0:T(8,128)}, u32[]{:S(2)}) copy-start(f32[2,4,128,128]{3,2,1,0:T(8,128)} %copy-done.7) | copy-start | bytes 1572868
  36.0 3.9 %copy-start.3 = (bf16[1024,512]{1,0:T(8,128)(2,1)S(1)}, bf16[1024,512]{1,0:T(8,128)(2,1)}, u32[]{:S(2)}) copy-start(bf16[1024,512]{1,0:T(8,128)(2,1)} %key_ref.7) | copy-start | bytes 3145732
  36.0 3.9 %copy-start.5 = (bf16[1024,512]{1,0:T(8,128)(2,1)S(1)}, bf16[1024,512]{1,0:T(8,128)(2,1)}, u32[]{:S(2)}) copy-start(bf16[1024,512]{1,0:T(8,128)(2,1)} %value_ref.7) | copy-start | bytes 3145732
  36.0 3.9 %copy-start.10 = (f32[4,4,128,128]{3,2,1,0:T(8,128)S(1)}, f32[4,4,128,128]{3,2,1,0:T(8,128)}, u32[]{:S(2)}) copy-start(f32[4,4,128,128]{3,2,1,0:T(8,128)} %copy-done.9) | copy-start | bytes 3145732
  36.0 3.9 %copy-start.12 = (bf16[512,512]{1,0:T(8,128)(2,1)S(1)}, bf16[512,512]{1,0:T(8,128)(2,1)}, u32[]{:S(2)}) copy-start(bf16[512,512]{1,0:T(8,128)(2,1)} %copy-done.11) | copy-start | bytes 1572868
  38.3 5.8 %collective-permute-start.8 = (bf16[4,128,128]{2,1,0:T(8,128)(2,1)S(1)}, bf16[4,128,128]{2,1,0:T(8,128)(2,1)S(1)}, u32[]{:S(2)}, u32[]{:S(2)}) collective-permute-start(bf16[4,128,128]{2,1,0:T(8,128)(2,1)S(1)} %get-tuple-element.44), channel_id=1, source_target_pairs={{0,4},{4,0},{8,12},{12,8},{16,20},{20,16},{24,28},{28,24},{1,5},{5... | collective-permute-start | bytes 393224 | tf_op jit(solution)/shard_map/ppermute | solution.py:376
  44.1 7.9 %collective-permute-start.9 = (bf16[4,128,128]{2,1,0:T(8,128)(2,1)S(1)}, bf16[4,128,128]{2,1,0:T(8,128)(2,1)S(1)}, u32[]{:S(2)}, u32[]{:S(2)}) collective-permute-start(bf16[4,128,128]{2,1,0:T(8,128)(2,1)S(1)} %next_2.1), channel_id=1, source_target_pairs={{8,0},{12,4},{16,8},{20,12},{24,16},{28,20},{9,1},{13,5},{17,9},{2... | collective-permute-start | bytes 393224 | tf_op jit(solution)/shard_map/ppermute | solution.py:376
  52.0 10.3 %collective-permute-start.10 = (bf16[4,128,128]{2,1,0:T(8,128)(2,1)S(1)}, bf16[4,128,128]{2,1,0:T(8,128)(2,1)S(1)}, u32[]{:S(2)}, u32[]{:S(2)}) collective-permute-start(bf16[4,128,128]{2,1,0:T(8,128)(2,1)S(1)} %next_4.1), channel_id=1, source_target_pairs={{16,0},{20,4},{24,8},{28,12},{17,1},{21,5},{25,9},{29,13},{18,2},{... | collective-permute-start | bytes 393224 | tf_op jit(solution)/shard_map/ppermute | solution.py:376

commit v3 on v2

v3 whole, which is shorter than its diff:
```python
import functools

import jax
import jax.numpy as jnp
from jax import lax
from jax.experimental import pallas as pl
from jax.experimental.pallas import tpu as pltpu
from jax.sharding import PartitionSpec as P

HEAD_DIM = 128
KEEP_SCALE = 1.0 / 0.9
F32 = jnp.float32
BF16 = jnp.bfloat16
NT = (((1,), (1,)), ((), ()))
NN = (((1,), (0,)), ((), ()))
TN = (((0,), (0,)), ((), ()))
MIB = 1024 * 1024


def dot(left, right, dims):
    return lax.dot_general(left, right, dims, preferred_element_type=F32)


def vmem():
    return pl.BlockSpec(memory_space=pltpu.VMEM)


def smem():
    return pl.BlockSpec(memory_space=pltpu.SMEM)


def hbm():
    return pl.BlockSpec(memory_space=pltpu.HBM)


def params(mib):
    return pltpu.CompilerParams(vmem_limit_bytes=mib * MIB)


def cost(flops, nbytes):
    return pl.CostEstimate(flops=flops, bytes_accessed=nbytes, transcendentals=0)


def head_cols(h):
    return slice(h * HEAD_DIM, (h + 1) * HEAD_DIM)


def masked_rows(grad, keep):
    return (grad.astype(F32) * keep.astype(F32) * KEEP_SCALE).astype(BF16)


def fetch(source, target, sems, row, rows, pieces):
    size = rows // pieces
    copies = []
    for n in range(pieces):
        copy = pltpu.make_async_copy(
            source.at[pl.ds(row + n * size, size), :],
            target.at[pl.ds(n * size, size), :],
            sems.at[n],
        )
        copy.start()
        copies.append(copy)
    return copies


def mask_body(row, grad_ref, keep_ref, *refs):
    out_refs, (grad, keep, grad_sems, keep_sems) = refs[:-4], refs[-4:]
    rows = grad.shape[0]
    pieces = keep_sems.shape[0]
    size = rows // pieces
    keep_copies = fetch(keep_ref, keep, keep_sems, row, rows, pieces)
    grad_copies = fetch(grad_ref, grad, grad_sems, row, rows, pieces)
    for n in range(pieces):
        keep_copies[n].wait()
        grad_copies[n].wait()
        low, high = n * size, (n + 1) * size
        value = masked_rows(grad[low:high, :], keep[low:high, :])
        out_refs[0][low:high, :] = value
        at = 0
        for ref in out_refs[1:]:
            end = at + ref.shape[0]
            top, bottom = max(low, at), min(high, end)
            if top < bottom:
                ref[top - at : bottom - at, :] = value[top - low : bottom - low, :]
            at = end


def mask_rows(out_grad, keep_mask, row, split, name):
    model = out_grad.shape[1]
    rows = sum(split)
    pieces = rows // 16
    return pl.pallas_call(
        functools.partial(mask_body, row),
        out_shape=tuple(jax.ShapeDtypeStruct((n, model), BF16) for n in [rows] + list(split)),
        in_specs=[hbm(), hbm()],
        out_specs=(vmem(),) * (1 + len(split)),
        scratch_shapes=[
            pltpu.VMEM((rows, model), BF16),
            pltpu.VMEM((rows, model), jnp.int32),
            pltpu.SemaphoreType.DMA((pieces,)),
            pltpu.SemaphoreType.DMA((pieces,)),
        ],
        compiler_params=params(56),
        cost_estimate=cost(1, 1),
        name=name,
    )(out_grad, keep_mask)


def kv_body(key_ref, value_ref, wide_ref, short_ref):
    for h in range(wide_ref.shape[0]):
        total = dot(key_ref[:, head_cols(h)], value_ref[:, head_cols(h)], TN)
        wide_ref[h] = total
        short_ref[h] = total.astype(BF16)


def kv_state(key_rows, value_rows):
    heads = key_rows.shape[1] // HEAD_DIM
    shape = (heads, HEAD_DIM, HEAD_DIM)
    return pl.pallas_call(
        kv_body,
        out_shape=(jax.ShapeDtypeStruct(shape, F32), jax.ShapeDtypeStruct(shape, BF16)),
        in_specs=[vmem(), vmem()],
        out_specs=(vmem(), vmem()),
        compiler_params=params(12),
        cost_estimate=cost(1, 1),
        name="kv_state",
    )(key_rows, value_rows)


def group_body(count, wide_ref, *refs):
    total = wide_ref[...]
    for ref in refs[:count]:
        total = total + ref[...].astype(F32)
    refs[-1][...] = total.astype(BF16)


def after(array, *others):
    return lax.optimization_barrier((array,) + others)[0]


def group_state(wide, received, ties, name):
    received = received[:-1] + [after(received[-1], *ties)]
    return pl.pallas_call(
        functools.partial(group_body, len(received)),
        out_shape=jax.ShapeDtypeStruct(wide.shape, BF16),
        in_specs=[vmem()] * (1 + len(received)),
        out_specs=vmem(),
        compiler_params=params(4),
        cost_estimate=cost(1, 1),
        name=name,
    )(wide, *received)


def swap_body(count, ctx_ref, half_ref, prev_ref, wide_ref, *refs):
    total = wide_ref[...]
    for ref in refs[:count]:
        total = total + ref[...].astype(F32)
    upper = ctx_ref[0] >= half_ref[0]
    refs[-1][...] = jnp.where(upper, total, prev_ref[...].astype(F32)).astype(BF16)


def swap_state(ctx, half, prev, wide, received):
    return pl.pallas_call(
        functools.partial(swap_body, len(received)),
        out_shape=jax.ShapeDtypeStruct(wide.shape, BF16),
        in_specs=[smem(), smem()] + [vmem()] * (2 + len(received)),
        out_specs=vmem(),
        compiler_params=params(4),
        cost_estimate=cost(1, 1),
        name="swap_state",
    )(ctx, half, prev, wide, *received)


def grad_body(pieces, sub, befores, last, *refs):
    place_ref, query_ref, weight_ref = refs[:3]
    refs = refs[3:]
    before_refs, refs = refs[:befores], refs[befores:]
    masked_refs, refs = refs[: len(pieces)], refs[len(pieces) :]
    grad_ref, state_ref = refs[:2]
    masked, query = refs[-2:]
    place = place_ref[0]
    spots, at = [], 0
    for ref, (flip, row) in zip(masked_refs, pieces):
        rows = ref.shape[0]
        masked[at : at + rows, :] = ref[...]
        start = pl.multiple_of(jnp.bitwise_xor(place, flip) * sub + row, 16)
        query[at : at + rows, :] = query_ref[pl.ds(start, rows), :]
        if spots and spots[-1][0] == flip:
            spots[-1][2] = at + rows
        else:
            spots.append([flip, at, at + rows])
        at += rows
    spots = [slice(low, high) for _, low, high in spots]
    grad = dot(masked[...], weight_ref[...], NT).astype(BF16)
    grad_ref[...] = grad
    for h in range(state_ref.shape[1]):
        total = None
        for n, rows in enumerate(spots):
            state = dot(query[rows, head_cols(h)], grad[rows, head_cols(h)], TN)
            if last:
                state = state + before_refs[0][n, h]
                other = before_refs[1][n, h]
                total = state + other if total is None else total + (state + other)
            state_ref[n, h] = state
        if last:
            wide_ref, short_ref = refs[2:4]
            wide_ref[h] = total
            short_ref[h] = total.astype(BF16)


def grad_part(place, query_rows, out_weight, sub, befores, pieces, arrays, name):
    width, model = out_weight.shape
    heads = width // HEAD_DIM
    rows = sum(a.shape[0] for a in arrays)
    shape = (heads, HEAD_DIM, HEAD_DIM)
    last = len(befores) > 0
    out_shape = [
        jax.ShapeDtypeStruct((rows, width), BF16),
        jax.ShapeDtypeStruct((2,) + shape, F32),
    ]
    if last:
        out_shape += [jax.ShapeDtypeStruct(shape, F32), jax.ShapeDtypeStruct(shape, BF16)]
    operands = [place, query_rows, out_weight] + list(befores) + list(arrays)
    return pl.pallas_call(
        functools.partial(grad_body, pieces, sub, len(befores), last),
        out_shape=tuple(out_shape),
        in_specs=[smem()] + [vmem()] * (len(operands) - 1),
        out_specs=tuple(vmem() for _ in out_shape),
        scratch_shapes=[pltpu.VMEM((rows, model), BF16), pltpu.VMEM((rows, width), BF16)],
        compiler_params=params(20),
        cost_estimate=cost(1, 1),
        name=name,
    )(*operands)


def gather_grad(place_ref, grad_refs, places, own_rows, grad):
    place = place_ref[0]
    for ref, pieces in zip(grad_refs, places):
        for at, rows, flip, row in pieces:
            start = pl.multiple_of(jnp.bitwise_xor(place, flip) * own_rows + row, 16)
            grad[pl.ds(start, rows), :] = ref[at : at + rows, :]


def causal(size, turned):
    row_id = lax.broadcasted_iota(jnp.int32, (size, size), 0)
    col_id = lax.broadcasted_iota(jnp.int32, (size, size), 1)
    return col_id >= row_id if turned else row_id >= col_id


def pair_state(ctx_ref, refs, reverse):
    odd = jnp.bitwise_and(ctx_ref[0], 1) == 1
    use = jnp.logical_not(odd) if reverse else odd
    total = None
    for n, ref in enumerate(refs):
        value = ref[0].astype(F32)
        if n == 0:
            value = value * use.astype(F32)
        total = value if total is None else total + value
    return total


def query_body(places, sub, parts, place_ref, ctx_ref, key_ref, value_ref, *refs):
    prev_refs, refs = refs[:parts], refs[parts:]
    grad_refs, (out_ref, grad) = refs[: len(places)], refs[len(places) :]
    gather_grad(place_ref, grad_refs, places, sub, grad)
    keep = causal(sub, False)
    rows = [slice(at, at + sub) for at in range(0, key_ref.shape[0], sub)]
    scores = [dot(grad[at, :], value_ref[at, :], NT) for at in rows]
    states = [pair_state(ctx_ref, prev_refs, False)]
    for at in rows[:-1]:
        states.append(states[-1] + dot(key_ref[at, :], value_ref[at, :], TN))
    totals = [dot(grad[at, :], state.astype(BF16), NT) for at, state in zip(rows, states)]
    scores = [jnp.where(keep, score, 0.0).astype(BF16) for score in scores]
    for at, score, total in zip(rows, scores, totals):
        out_ref[at, :] = total + dot(score, key_ref[at, :], NN)


def later_body(places, sub, parts, place_ref, ctx_ref, query_ref, key_ref, value_ref, *refs):
    near_ref, far_ref = refs[:2]
    next_refs, refs = refs[2 : 2 + parts], refs[2 + parts :]
    grad_refs, (key_out, value_out, grad_out, grad) = refs[: len(places)], refs[len(places) :]
    gather_grad(place_ref, grad_refs, places, sub, grad)
    grad_out[...] = grad[...]
    place = place_ref[0]
    keep = causal(sub, True)
    rows = [slice(at, at + sub) for at in range(0, key_ref.shape[0], sub)]
    masked = lambda scores: [jnp.where(keep, score, 0.0).astype(BF16) for score in scores]
    scores = [dot(value_ref[at, :], grad[at, :], NT) for at in rows]
    attn = [dot(key_ref[at, :], query_ref[at, :], NT) for at in rows]
    later = pair_state(ctx_ref, next_refs, True)
    own = [near_ref[0, 0], near_ref[1, 0], far_ref[0, 0], far_ref[1, 0]]
    states = []
    for n in range(len(rows)):
        total = later
        for flip, state in enumerate(own):
            total = total + jnp.where(jnp.bitwise_xor(place, flip) > n, state, 0.0)
        states.append(total.astype(BF16))
    scores = masked(scores)
    for at, score, state in zip(rows, scores, states):
        key_out[at, :] = dot(value_ref[at, :], state, NT) + dot(score, query_ref[at, :], NN)
    attn = masked(attn)
    for at, score, state in zip(rows, attn, states):
        value_out[at, :] = dot(key_ref[at, :], state, NN) + dot(score, grad[at, :], NN)


def column(rows):
    return pl.BlockSpec((rows, HEAD_DIM), lambda h: (0, h))


def head_state():
    return pl.BlockSpec((1, HEAD_DIM, HEAD_DIM), lambda h: (h, 0, 0))


def local_states(count):
    return pl.BlockSpec((count, 1, HEAD_DIM, HEAD_DIM), lambda h: (0, h, 0, 0))


def query_products(place, ctx, key_rows, value_rows, prevs, grads, places, sub):
    tokens, width = key_rows.shape
    return pl.pallas_call(
        functools.partial(query_body, places, sub, len(prevs)),
        out_shape=jax.ShapeDtypeStruct((tokens, width), F32),
        grid=(width // HEAD_DIM,),
        in_specs=[smem(), smem()]
        + [column(tokens)] * 2
        + [head_state()] * len(prevs)
        + [column(g.shape[0]) for g in grads],
        out_specs=column(tokens),
        scratch_shapes=[pltpu.VMEM((tokens, HEAD_DIM), BF16)],
        compiler_params=params(16),
        cost_estimate=cost(4 * tokens * tokens * width, 8 * tokens * width),
        name="query_products",
    )(place, ctx, key_rows, value_rows, *prevs, *grads)


def later_products(place, ctx, query_rows, key_rows, value_rows, near, far, nexts, grads, places, sub):
    tokens, width = key_rows.shape
    return pl.pallas_call(
        functools.partial(later_body, places, sub, len(nexts)),
        out_shape=(
            jax.ShapeDtypeStruct((tokens, width), F32),
            jax.ShapeDtypeStruct((tokens, width), F32),
            jax.ShapeDtypeStruct((tokens, width), BF16),
        ),
        grid=(width // HEAD_DIM,),
        in_specs=[smem(), smem()]
        + [column(tokens)] * 3
        + [local_states(2), local_states(2)]
        + [head_state()] * len(nexts)
        + [column(g.shape[0]) for g in grads],
        out_specs=(column(tokens),) * 3,
        scratch_shapes=[pltpu.VMEM((tokens, HEAD_DIM), BF16)],
        compiler_params=params(16),
        cost_estimate=cost(8 * tokens * tokens * width, 10 * tokens * width),
        name="later_products",
    )(place, ctx, query_rows, key_rows, value_rows, near, far, *nexts, *grads)


def end_body(sub, ctx_ref, half_ref, got_ref, key_ref, value_ref, grad_ref, *refs):
    part_refs, out_refs, (done, sems) = refs[:3], refs[3:6], refs[6:]
    upper = ctx_ref[0] >= half_ref[0]
    heads = got_ref.shape[0]
    copies = []
    for n in range(key_ref.shape[0] // sub):
        rows = slice(n * sub, (n + 1) * sub)
        for h in range(heads):
            cols = head_cols(h)
            got = got_ref[h].astype(F32)
            down = jnp.where(upper, 0.0, got).astype(BF16)
            up = jnp.where(upper, got, 0.0).astype(BF16)
            adds = (
                dot(grad_ref[rows, cols], up, NT),
                dot(value_ref[rows, cols], down, NT),
                dot(key_ref[rows, cols], down, NN),
            )
            for k in range(3):
                done[k, rows, cols] = (part_refs[k][rows, cols] + adds[k]).astype(BF16)
        for k in range(3):
            copy = pltpu.make_async_copy(
                done.at[k, pl.ds(n * sub, sub), :],
                out_refs[k].at[pl.ds(n * sub, sub), :],
                sems.at[k, n],
            )
            copy.start()
            copies.append(copy)
    for copy in copies:
        copy.wait()


def end_products(ctx, half, got, key_rows, value_rows, grad_rows, parts, sub):
    tokens, width = key_rows.shape
    return pl.pallas_call(
        functools.partial(end_body, sub),
        out_shape=(jax.ShapeDtypeStruct((tokens, width), BF16),) * 3,
        in_specs=[smem(), smem()] + [vmem()] * 7,
        out_specs=(hbm(),) * 3,
        scratch_shapes=[
            pltpu.VMEM((3, tokens, width), BF16),
            pltpu.SemaphoreType.DMA((3, tokens // sub)),
        ],
        compiler_params=params(16),
        cost_estimate=cost(6 * tokens * width * HEAD_DIM, 16 * tokens * width),
        name="end_products",
    )(ctx, half, got, key_rows, value_rows, grad_rows, *parts)


def exchange(payload, reach, reverse):
    size = lax.axis_size("ctx")
    if reach == 1:
        pairs = [(i, i ^ 1) for i in range(size)]
    elif reverse:
        pairs = [(i + reach, i) for i in range(size - reach)]
    else:
        pairs = [(i, i + reach) for i in range(size - reach)]
    return lax.ppermute(payload, "ctx", pairs)


def scan_states(wide, short, reverse, tie, name):
    received, reach, payload = [], 1, short
    while reach < lax.axis_size("ctx") // 2:
        if reach > 1:
            payload = group_state(wide, received, [tie] if reach == 2 else [], "%s_%d" % (name, reach))
        received.append(exchange(payload, reach, reverse))
        reach *= 2
    return received


def per_device(out_grad, keep_mask, out_weight, query_rows, key_rows, value_rows):
    size = lax.axis_size("head")
    place = lax.axis_index("head").astype(jnp.int32).reshape(1)
    ctx = lax.axis_index("ctx").astype(jnp.int32).reshape(1)
    own_rows = out_grad.shape[0]
    half = jnp.full((1,), lax.axis_size("ctx") // 2, jnp.int32)
    unit = own_rows // 16
    split = 9 * unit

    def swap(array, distance):
        return lax.ppermute(array, "head", [(i, i ^ distance) for i in range(size)])

    first, *near_first = mask_rows(out_grad, keep_mask, 0, (5 * unit, 4 * unit), "mask_first")
    last, *near_last = mask_rows(out_grad, keep_mask, split, (4 * unit, 3 * unit), "mask_last")
    far_first, far_last = swap(first, 2), swap(last, 2)
    near = [swap(piece, 1) for piece in near_first + near_last]
    kv_wide, kv_short = kv_state(key_rows, value_rows)

    part = functools.partial(grad_part, place, query_rows, out_weight, own_rows)
    grads, places, states = [], [], []

    def run(befores, pieces, arrays, name):
        got = part(befores, pieces, arrays, name)
        at, spots = 0, []
        for (flip, row), array in zip(pieces, arrays):
            spots.append((at, array.shape[0], flip, row))
            at += array.shape[0]
        grads.append(got[0])
        places.append(tuple(spots))
        states.append(got[1])
        return got

    pieces = ((0, 0), (0, split), (1, 0), (1, 5 * unit), (1, split), (1, split + 4 * unit))
    run([], pieces, [first, last] + near[:-1] + [after(near[-1], kv_short)], "grad_near")

    prevs = scan_states(kv_wide, kv_short, False, states[0], "prev")
    prev_sum = group_state(kv_wide, prevs, [], "prev_sum")

    far_first = after(far_first, prev_sum, states[0])
    run([], ((2, 0), (3, 0)), [far_first, swap(far_first, 1)], "grad_far")
    _, far, wide, short = run(
        [states[1], states[0]],
        ((2, split), (3, split)),
        [far_last, swap(far_last, 1)],
        "grad_last",
    )

    spots = tuple(places)
    query_part = query_products(place, ctx, key_rows, value_rows, prevs, grads, spots, own_rows)
    nexts = scan_states(wide, short, True, query_part, "next")
    payload = swap_state(ctx, half, prev_sum, wide, nexts)
    size = lax.axis_size("ctx")
    got = lax.ppermute(payload, "ctx", [(i, (i + size // 2) % size) for i in range(size)])
    key_part, value_part, grad_rows = later_products(
        place, ctx, query_rows, key_rows, value_rows, states[0], far, nexts, grads, spots, own_rows
    )
    parts = (query_part, key_part, value_part)
    return end_products(ctx, half, got, key_rows, value_rows, grad_rows, parts, own_rows)


def solution(mesh):
    placed = (
        P(("ctx", "head"), None),
        P(("ctx", "head"), None),
        P("head", None),
        P("ctx", "head"),
        P("ctx", "head"),
        P("ctx", "head"),
    )
    return jax.shard_map(
        per_device,
        mesh=mesh,
        in_specs=placed,
        out_specs=(P("ctx", "head"), P("ctx", "head"), P("ctx", "head")),
        check_vma=False,
    )
```

time: 66.2 us -> 59.4 us (0.90)
  waiting for transfers between devices: 18.8 us -> 13.3 us
  starting transfers between devices: 17.8 us -> 15.2 us
  local copies, waits for them, and re-layouts: 3.03 us -> 5.38 us
  Pallas kernels: 25.1 us -> 24.2 us
    ppermute x6 -> x5, waiting for transfers between devices: 17 us -> 9.97 us  [the longest x4 9.97 us: exchange(): return lax.ppermute(payload, 'ctx', pairs)]
    pallas_call x3 -> x5, Pallas kernels: 8.48 us -> 11.5 us  [the longest x1 5.26 us: later_products(): pl.pallas_call(functools.partial(later_body, places, sub, len(nexts)), ou...]
    ppermute x6 -> x5, starting transfers between devices: 13.7 us -> 11 us  [the longest x4 7.92 us: exchange(): return lax.ppermute(payload, 'ctx', pairs)]
    unnamed x26 -> x40, local copies, waits for them, and re-layouts: 3.03 us -> 5.38 us
    pallas_call x4 -> x3, Pallas kernels: 1.8 us -> 0.1 us  [group_state(): pl.pallas_call(functools.partial(group_body, len(received)), out_shape=ja...]
    ppermute x5 -> x8, waiting for transfers between devices: 1.84 us -> 3.34 us  [swap(): return lax.ppermute(array, 'head', [(i, i ^ distance) for i in range(size)])]
    pallas_call x1, Pallas kernels: 3.27 us -> 2.16 us  [end_products(): pl.pallas_call(functools.partial(end_body, sub), out_shape=(jax.ShapeDtyp...]
    pallas_call x1, Pallas kernels: 4.17 us -> 3.2 us  [query_products(): pl.pallas_call(functools.partial(query_body, places, sub, len(prevs)), ou...]
  transfers between devices with their start and end apart: 11 -> 13, of which waited for: 5 -> 6; matrix products, arithmetic and copies ran while one was open for 0% -> 0% of each run, Pallas kernels for 24% -> 29%
where the time goes in v3:
time: 59.4 us; the launch traced here: 59 us
  Pallas kernels  24.2 us (41%)
  starting transfers between devices  15.2 us (26%)
  waiting for transfers between devices  13.3 us (22%)
  local copies, waits for them, and re-layouts  5.38 us (9%)
  between operations  0.91 us (2%)
    ppermute x4, waiting for transfers between devices, exchange(): return lax.ppermute(payload, 'ctx', pairs)  9.97 us
    ppermute x4, starting transfers between devices, exchange(): return lax.ppermute(payload, 'ctx', pairs)  7.92 us
    pallas_call x3, Pallas kernels, grad_part(): pl.pallas_call(functools.partial(grad_body, pieces, sub, len(befores), la...  7.21 us
    unnamed x40, local copies, waits for them, and re-layouts  5.38 us
    pallas_call x1, Pallas kernels, later_products(): pl.pallas_call(functools.partial(later_body, places, sub, len(nexts)), ou...  5.26 us
    pallas_call x2, Pallas kernels, mask_rows(): pl.pallas_call(functools.partial(mask_body, row), out_shape=tuple((jax.Sh...  5.06 us
    ppermute x8, starting transfers between devices, swap(): return lax.ppermute(array, 'head', [(i, i ^ distance) for i in range(size)])  4.25 us
    ppermute x8, waiting for transfers between devices, swap(): return lax.ppermute(array, 'head', [(i, i ^ distance) for i in range(size)])  3.34 us
  transfers between devices with their start and end apart: 13, of which 6 were waited for; matrix products, arithmetic and copies ran while one was open for 0% of the time, Pallas kernels for 29%

profile of v3, /device:TPU:0, one launch (start us, length us, event | category | flops | bytes accessed | tf_op | source)
XLA Modules:
  0.0 59.0 jit_solution(10399175209170284884)
XLA Ops:
  0.6 2.6 %mask_first.1 = (bf16[144,2048]{1,0:T(8,128)(2,1)}, bf16[80,2048]{1,0:T(8,128)(2,1)}, bf16[64,2048]{1,0:T(8,128)(2,1)}) custom-call(bf16[256,2048]{1,0:T(8,128)(2,1)} %grad_ref.3, s32[256,2048]{1,0:T(8,128)} %keep_ref.3), custom_call_target="tpu_custom_call" | custom-call | flops 1 | bytes 1 | tf_op jit(solution)/shard_map/mask_first/pallas_call | solution.py:92
  3.3 3.0 %collective-permute-start.6 = (bf16[144,2048]{1,0:T(8,128)(2,1)}, bf16[144,2048]{1,0:T(8,128)(2,1)}, u32[]{:S(2)}, u32[]{:S(2)}) collective-permute-start(bf16[144,2048]{1,0:T(8,128)(2,1)} %get-tuple-element.28.refs_3_), channel_id=1, source_target_pairs={{0,2},{1,3},{2,0},{3,1},{4,6},{5,7},{6,4},{7,5},{8,10},{9,11},{10,... | collective-permute-start | bytes 1769480 | tf_op jit(solution)/shard_map/ppermute | solution.py:438
  6.3 2.4 %mask_last.1 = (bf16[112,2048]{1,0:T(8,128)(2,1)}, bf16[64,2048]{1,0:T(8,128)(2,1)}, bf16[48,2048]{1,0:T(8,128)(2,1)}) custom-call(bf16[256,2048]{1,0:T(8,128)(2,1)} %grad_ref.3, s32[256,2048]{1,0:T(8,128)} %keep_ref.3), custom_call_target="tpu_custom_call" | custom-call | flops 1 | bytes 1 | tf_op jit(solution)/shard_map/mask_last/pallas_call | solution.py:92
  8.8 0.5 collective-permute-start.4
  9.3 0.1 collective-permute-start.1
  9.4 0.4 collective-permute-start.2
  9.8 1.0 %collective-permute-done.4.refs_8_ = bf16[48,2048]{1,0:T(8,128)(2,1)S(1)} collective-permute-done((bf16[48,2048]{1,0:T(8,128)(2,1)}, bf16[48,2048]{1,0:T(8,128)(2,1)S(1)}, u32[]{:S(2)}, u32[]{:S(2)}) %collective-permute-start.4) | collective-permute-done | bytes 196640 | tf_op jit(solution)/shard_map/ppermute | solution.py:438
  10.8 0.2 collective-permute-start.8
  11.0 1.1 %kv_state.1 = (f32[4,128,128]{2,1,0:T(8,128)S(1)}, bf16[4,128,128]{2,1,0:T(8,128)(2,1)}) custom-call(bf16[1024,512]{1,0:T(8,128)(2,1)S(1)} %copy-done.2, bf16[1024,512]{1,0:T(8,128)(2,1)S(1)} %copy-done.4), custom_call_target="tpu_custom_call" | custom-call | flops 1 | bytes 1 | tf_op jit(solution)/shard_map/kv_state/pallas_call | solution.py:119
  12.1 0.7 %copy-done.12 = bf16[64,2048]{1,0:T(8,128)(2,1)} copy-done((bf16[64,2048]{1,0:T(8,128)(2,1)}, bf16[64,2048]{1,0:T(8,128)(2,1)S(1)}, u32[]{:S(2)}) %copy-start.12) | copy-done | bytes 262168
  12.8 2.2 %collective-permute-start = (bf16[4,128,128]{2,1,0:T(8,128)(2,1)}, bf16[4,128,128]{2,1,0:T(8,128)(2,1)S(1)}, u32[]{:S(2)}, u32[]{:S(2)}) collective-permute-start(bf16[4,128,128]{2,1,0:T(8,128)(2,1)} %get-tuple-element.27), channel_id=1, source_target_pairs={{0,4},{4,0},{8,12},{12,8},{16,20},{20,16},{24,28},{28,24},{1,5},{5... | collective-permute-start | bytes 393224 | tf_op jit(solution)/shard_map/ppermute | solution.py:415
  15.1 1.1 %copy-done.6 = bf16[144,2048]{1,0:T(8,128)(2,1)S(1)} copy-done((bf16[144,2048]{1,0:T(8,128)(2,1)S(1)}, bf16[144,2048]{1,0:T(8,128)(2,1)}, u32[]{:S(2)}) %copy-start.6) | copy-done | bytes 589848
  16.1 1.0 %copy-done.11 = bf16[112,2048]{1,0:T(8,128)(2,1)S(1)} copy-done((bf16[112,2048]{1,0:T(8,128)(2,1)S(1)}, bf16[112,2048]{1,0:T(8,128)(2,1)}, u32[]{:S(2)}) %copy-start.11) | copy-done | bytes 458776
  17.2 0.9 %copy-done.13 = bf16[64,2048]{1,0:T(8,128)(2,1)S(1)} copy-done((bf16[64,2048]{1,0:T(8,128)(2,1)S(1)}, bf16[64,2048]{1,0:T(8,128)(2,1)}, u32[]{:S(2)}) %copy-start.13) | copy-done | bytes 262168
  18.1 0.9 %copy-done.15 = bf16[48,2048]{1,0:T(8,128)(2,1)S(1)} copy-done((bf16[48,2048]{1,0:T(8,128)(2,1)S(1)}, bf16[48,2048]{1,0:T(8,128)(2,1)}, u32[]{:S(2)}) %copy-start.15) | copy-done | bytes 196632
  19.0 2.6 %grad_near.1 = (bf16[512,512]{1,0:T(8,128)(2,1)S(1)}, f32[2,4,128,128]{3,2,1,0:T(8,128)S(1)}) custom-call(s32[1]{0:T(128)} %bitcast.1.refs_0_.place_ref, bf16[1024,512]{1,0:T(8,128)(2,1)S(1)} %copy-done.1, bf16[512,2048]{1,0:T(8,128)(2,1)S(1)} %copy-done, bf16[144,2048]{1,0:T(8,128)(2,1)S(1)} %copy-done.6, bf16[112,2048]{1,0:T(8,128)(2,1)S(1)} %copy-done.11, ...), custom_call_target="tpu_custom_call" | custom-call | flops 1 | bytes 1 | tf_op jit(solution)/shard_map/grad_near/pallas_call | solution.py:224
  21.7 3.5 %collective-permute-start.5 = (bf16[4,128,128]{2,1,0:T(8,128)(2,1)S(1)}, bf16[4,128,128]{2,1,0:T(8,128)(2,1)S(1)}, u32[]{:S(2)}, u32[]{:S(2)}) collective-permute-start(bf16[4,128,128]{2,1,0:T(8,128)(2,1)S(1)} %prev_2.1), channel_id=1, source_target_pairs={{0,8},{4,12},{8,16},{12,20},{16,24},{20,28},{1,9},{5,13},{9,17},{1... | collective-permute-start | bytes 393224 | tf_op jit(solution)/shard_map/ppermute | solution.py:415
  25.2 2.5 %collective-permute-done.5.refs_1_ = bf16[4,128,128]{2,1,0:T(8,128)(2,1)S(1)} collective-permute-done((bf16[4,128,128]{2,1,0:T(8,128)(2,1)S(1)}, bf16[4,128,128]{2,1,0:T(8,128)(2,1)S(1)}, u32[]{:S(2)}, u32[]{:S(2)}) %collective-permute-start.5) | collective-permute-done | bytes 131104 | tf_op jit(solution)/shard_map/ppermute | solution.py:415
  27.8 0.6 %copy-done.7 = bf16[4,128,128]{2,1,0:T(8,128)(2,1)} copy-done((bf16[4,128,128]{2,1,0:T(8,128)(2,1)}, bf16[4,128,128]{2,1,0:T(8,128)(2,1)S(1)}, u32[]{:S(2)}) %copy-start.7) | copy-done | bytes 131096
  28.5 1.4 %collective-permute-done.8.refs_5_ = bf16[112,2048]{1,0:T(8,128)(2,1)} collective-permute-done((bf16[112,2048]{1,0:T(8,128)(2,1)}, bf16[112,2048]{1,0:T(8,128)(2,1)}, u32[]{:S(2)}, u32[]{:S(2)}) %collective-permute-start.8) | collective-permute-done | bytes 458784 | tf_op jit(solution)/shard_map/ppermute | solution.py:438
  29.8 1.0 %collective-permute-done.7.refs_4_ = bf16[144,2048]{1,0:T(8,128)(2,1)} collective-permute-done((bf16[144,2048]{1,0:T(8,128)(2,1)}, bf16[144,2048]{1,0:T(8,128)(2,1)}, u32[]{:S(2)}, u32[]{:S(2)}) %collective-permute-start.7) | collective-permute-done | bytes 589856 | tf_op jit(solution)/shard_map/ppermute | solution.py:438
  30.8 2.3 %grad_far.1 = (bf16[288,512]{1,0:T(8,128)(2,1)S(1)}, f32[2,4,128,128]{3,2,1,0:T(8,128)S(1)}) custom-call(s32[1]{0:T(128)} %bitcast.1.refs_0_.place_ref, bf16[1024,512]{1,0:T(8,128)(2,1)S(1)} %copy-done.1, bf16[512,2048]{1,0:T(8,128)(2,1)S(1)} %copy-done, bf16[144,2048]{1,0:T(8,128)(2,1)} %collective-permute-done.6.refs_3_, ...), custom_call_target="tpu_custom_call" | custom-call | flops 1 | bytes 1 | tf_op jit(solution)/shard_map/grad_far/pallas_call | solution.py:224
  33.2 2.3 %grad_last.1 = (bf16[224,512]{1,0:T(8,128)(2,1)S(1)}, f32[2,4,128,128]{3,2,1,0:T(8,128)S(1)}, f32[4,128,128]{2,1,0:T(8,128)S(1)}, bf16[4,128,128]{2,1,0:T(8,128)(2,1)S(1)}) custom-call(s32[1]{0:T(128)} %bitcast.1.refs_0_.place_ref, bf16[1024,512]{1,0:T(8,128)(2,1)S(1)} %copy-done.1, bf16[512,2048]{1,0:T(8,128)(2,1)S(1)} %copy-done, ...), custom_call_target="tpu_custom_call" | custom-call | flops 1 | bytes 1 | tf_op jit(solution)/shard_map/grad_last/pallas_call | solution.py:224
  35.5 0.9 %collective-permute-start.10 = (bf16[4,128,128]{2,1,0:T(8,128)(2,1)S(1)}, bf16[4,128,128]{2,1,0:T(8,128)(2,1)S(1)}, u32[]{:S(2)}, u32[]{:S(2)}) collective-permute-start(bf16[4,128,128]{2,1,0:T(8,128)(2,1)S(1)} %get-tuple-element.40), channel_id=1, source_target_pairs={{0,4},{4,0},{8,12},{12,8},{16,20},{20,16},{24,28},{28,24},{1,5},{5... | collective-permute-start | bytes 393224 | tf_op jit(solution)/shard_map/ppermute | solution.py:415
  36.4 3.2 %query_products.1.refs_0_ = f32[1024,512]{1,0:T(8,128)S(1)} custom-call(s32[1]{0:T(128)} %bitcast.1.refs_0_.place_ref, s32[1]{0:T(128)} %bitcast.ctx_ref, bf16[1024,512]{1,0:T(8,128)(2,1)S(1)} %copy-done.3, bf16[1024,512]{1,0:T(8,128)(2,1)S(1)} %copy-done.5, bf16[4,128,128]{2,1,0:T(8,128)(2,1)S(1)} %collective-permute-done.refs_0_, ...), custom_call_target="tpu_custom_call" | custom-call | flops 2147483648 | bytes 4194304 | tf_op jit(solution)/shard_map/query_products/pallas_call | solution.py:320
  39.6 1.4 %collective-permute-done.10.refs_0_.refs_2_ = bf16[4,128,128]{2,1,0:T(8,128)(2,1)S(1)} collective-permute-done((bf16[4,128,128]{2,1,0:T(8,128)(2,1)S(1)}, bf16[4,128,128]{2,1,0:T(8,128)(2,1)S(1)}, u32[]{:S(2)}, u32[]{:S(2)}) %collective-permute-start.10) | collective-permute-done | bytes 131104 | tf_op jit(solution)/shard_map/ppermute | solution.py:415
  41.1 1.3 %collective-permute-start.11 = (bf16[4,128,128]{2,1,0:T(8,128)(2,1)S(1)}, bf16[4,128,128]{2,1,0:T(8,128)(2,1)S(1)}, u32[]{:S(2)}, u32[]{:S(2)}) collective-permute-start(bf16[4,128,128]{2,1,0:T(8,128)(2,1)S(1)} %next_2.1), channel_id=1, source_target_pairs={{8,0},{12,4},{16,8},{20,12},{24,16},{28,20},{9,1},{13,5},{17,9},{2... | collective-permute-start | bytes 393224 | tf_op jit(solution)/shard_map/ppermute | solution.py:415
  42.4 6.0 %collective-permute-done.11.refs_1_.refs_3_ = bf16[4,128,128]{2,1,0:T(8,128)(2,1)S(1)} collective-permute-done((bf16[4,128,128]{2,1,0:T(8,128)(2,1)S(1)}, bf16[4,128,128]{2,1,0:T(8,128)(2,1)S(1)}, u32[]{:S(2)}, u32[]{:S(2)}) %collective-permute-start.11) | collective-permute-done | bytes 131104 | tf_op jit(solution)/shard_map/ppermute | solution.py:415
  48.4 0.1 swap_state.1
  48.5 3.1 %collective-permute-start.12 = (bf16[4,128,128]{2,1,0:T(8,128)(2,1)S(1)}, bf16[4,128,128]{2,1,0:T(8,128)(2,1)S(1)}, u32[]{:S(2)}, u32[]{:S(2)}) collective-permute-start(bf16[4,128,128]{2,1,0:T(8,128)(2,1)S(1)} %swap_state.1), channel_id=1, source_target_pairs={{0,16},{4,20},{8,24},{12,28},{16,0},{20,4},{24,8},{28,12},{1,17},{... | collective-permute-start | bytes 393224 | tf_op jit(solution)/shard_map/ppermute | solution.py:480
  51.6 5.3 %later_products.1 = (f32[1024,512]{1,0:T(8,128)S(1)}, f32[1024,512]{1,0:T(8,128)S(1)}, bf16[1024,512]{1,0:T(8,128)(2,1)S(1)}) custom-call(s32[1]{0:T(128)} %bitcast.1.refs_0_.place_ref, s32[1]{0:T(128)} %bitcast.ctx_ref, bf16[1024,512]{1,0:T(8,128)(2,1)S(1)} %copy-done.1, bf16[1024,512]{1,0:T(8,128)(2,1)S(1)} %copy-done.3, bf16[1024,512]{1,0:T(8,128)(2,1)S(1)} %copy-done.5, ...), custom_call_target="tpu_custom_call" | custom-call | flops 4294967296 | bytes 5242880 | tf_op jit(solution)/shard_map/later_products/pallas_call | solution.py:338
  56.9 2.2 %end_products.1 = (bf16[1024,512]{1,0:T(8,128)(2,1)}, bf16[1024,512]{1,0:T(8,128)(2,1)}, bf16[1024,512]{1,0:T(8,128)(2,1)}) custom-call(s32[1]{0:T(128)} %bitcast.ctx_ref, s32[1]{0:T(128)} %constant.9.clone.1.half_ref, bf16[4,128,128]{2,1,0:T(8,128)(2,1)S(1)} %collective-permute-done.12.got_ref, bf16[1024,512]{1,0:T(8,128)(2,1)S(1)} %copy-done.3, ...), custom_call_target="tpu_custom_call" | custom-call | flops 402653184 | bytes 8388608 | tf_op jit(solution)/shard_map/end_products/pallas_call | solution.py:392
  (47 shorter events, 0.3 us)
Async XLA Ops:
  3.3 7.7 %copy-start.2 = (bf16[1024,512]{1,0:T(8,128)(2,1)S(1)}, bf16[1024,512]{1,0:T(8,128)(2,1)}, u32[]{:S(2)}) copy-start(bf16[1024,512]{1,0:T(8,128)(2,1)} %key_ref.7) | copy-start | bytes 3145732
  3.3 7.7 %copy-start.4 = (bf16[1024,512]{1,0:T(8,128)(2,1)S(1)}, bf16[1024,512]{1,0:T(8,128)(2,1)}, u32[]{:S(2)}) copy-start(bf16[1024,512]{1,0:T(8,128)(2,1)} %value_ref.7) | copy-start | bytes 3145732
  3.3 11.8 %copy-start = (bf16[512,2048]{1,0:T(8,128)(2,1)S(1)}, bf16[512,2048]{1,0:T(8,128)(2,1)}, u32[]{:S(2)}) copy-start(bf16[512,2048]{1,0:T(8,128)(2,1)} %refs_2_.5) | copy-start | bytes 6291460
  3.3 11.7 %copy-start.1 = (bf16[1024,512]{1,0:T(8,128)(2,1)S(1)}, bf16[1024,512]{1,0:T(8,128)(2,1)}, u32[]{:S(2)}) copy-start(bf16[1024,512]{1,0:T(8,128)(2,1)} %query_ref.1) | copy-start | bytes 3145732
  3.3 25.1 %collective-permute-start.6 = (bf16[144,2048]{1,0:T(8,128)(2,1)}, bf16[144,2048]{1,0:T(8,128)(2,1)}, u32[]{:S(2)}, u32[]{:S(2)}) collective-permute-start(bf16[144,2048]{1,0:T(8,128)(2,1)} %get-tuple-element.28.refs_3_), channel_id=1, source_target_pairs={{0,2},{1,3},{2,0},{3,1},{4,6},{5,7},{6,4},{7,5},{8,10},{9,11},{10,... | collective-permute-start | bytes 1769480 | tf_op jit(solution)/shard_map/ppermute | solution.py:438
  8.8 3.4 %collective-permute-start.3 = (bf16[64,2048]{1,0:T(8,128)(2,1)}, bf16[64,2048]{1,0:T(8,128)(2,1)S(1)}, u32[]{:S(2)}, u32[]{:S(2)}) collective-permute-start(bf16[64,2048]{1,0:T(8,128)(2,1)} %get-tuple-element.32), channel_id=1, source_target_pairs={{0,1},{1,0},{2,3},{3,2},{4,5},{5,4},{6,7},{7,6},{8,9},{9,8},{10,11... | collective-permute-start | bytes 786440 | tf_op jit(solution)/shard_map/ppermute | solution.py:438
  8.8 2.0 %collective-permute-start.4 = (bf16[48,2048]{1,0:T(8,128)(2,1)}, bf16[48,2048]{1,0:T(8,128)(2,1)S(1)}, u32[]{:S(2)}, u32[]{:S(2)}) collective-permute-start(bf16[48,2048]{1,0:T(8,128)(2,1)} %get-tuple-element.33), channel_id=1, source_target_pairs={{0,1},{1,0},{2,3},{3,2},{4,5},{5,4},{6,7},{7,6},{8,9},{9,8},{10,11... | collective-permute-start | bytes 589832 | tf_op jit(solution)/shard_map/ppermute | solution.py:438
  9.3 5.7 %collective-permute-start.1 = (bf16[80,2048]{1,0:T(8,128)(2,1)}, bf16[80,2048]{1,0:T(8,128)(2,1)}, u32[]{:S(2)}, u32[]{:S(2)}) collective-permute-start(bf16[80,2048]{1,0:T(8,128)(2,1)} %get-tuple-element.30), channel_id=1, source_target_pairs={{0,1},{1,0},{2,3},{3,2},{4,5},{5,4},{6,7},{7,6},{8,9},{9,8},{10,11... | collective-permute-start | bytes 983048 | tf_op jit(solution)/shard_map/ppermute | solution.py:438
  9.4 5.6 %collective-permute-start.2 = (bf16[64,2048]{1,0:T(8,128)(2,1)}, bf16[64,2048]{1,0:T(8,128)(2,1)}, u32[]{:S(2)}, u32[]{:S(2)}) collective-permute-start(bf16[64,2048]{1,0:T(8,128)(2,1)} %get-tuple-element.31), channel_id=1, source_target_pairs={{0,1},{1,0},{2,3},{3,2},{4,5},{5,4},{6,7},{7,6},{8,9},{9,8},{10,11... | collective-permute-start | bytes 786440 | tf_op jit(solution)/shard_map/ppermute | solution.py:438
  10.8 1.3 %copy-start.14 = (bf16[48,2048]{1,0:T(8,128)(2,1)}, bf16[48,2048]{1,0:T(8,128)(2,1)S(1)}, u32[]{:S(2)}) copy-start(bf16[48,2048]{1,0:T(8,128)(2,1)S(1)} %collective-permute-done.4.refs_8_) | copy-start | bytes 589828
  10.8 19.0 %collective-permute-start.8 = (bf16[112,2048]{1,0:T(8,128)(2,1)}, bf16[112,2048]{1,0:T(8,128)(2,1)}, u32[]{:S(2)}, u32[]{:S(2)}) collective-permute-start(bf16[112,2048]{1,0:T(8,128)(2,1)} %get-tuple-element.29.refs_4_), channel_id=1, source_target_pairs={{0,2},{1,3},{2,0},{3,1},{4,6},{5,7},{6,4},{7,5},{8,10},{9,11},{10,... | collective-permute-start | bytes 1376264 | tf_op jit(solution)/shard_map/ppermute | solution.py:438
  12.1 0.7 %copy-start.12 = (bf16[64,2048]{1,0:T(8,128)(2,1)}, bf16[64,2048]{1,0:T(8,128)(2,1)S(1)}, u32[]{:S(2)}) copy-start(bf16[64,2048]{1,0:T(8,128)(2,1)S(1)} %collective-permute-done.3.refs_7_) | copy-start | bytes 786436
  12.8 8.8 %collective-permute-start = (bf16[4,128,128]{2,1,0:T(8,128)(2,1)}, bf16[4,128,128]{2,1,0:T(8,128)(2,1)S(1)}, u32[]{:S(2)}, u32[]{:S(2)}) collective-permute-start(bf16[4,128,128]{2,1,0:T(8,128)(2,1)} %get-tuple-element.27), channel_id=1, source_target_pairs={{0,4},{4,0},{8,12},{12,8},{16,20},{20,16},{24,28},{28,24},{1,5},{5... | collective-permute-start | bytes 393224 | tf_op jit(solution)/shard_map/ppermute | solution.py:415
  15.1 1.1 %copy-start.6 = (bf16[144,2048]{1,0:T(8,128)(2,1)S(1)}, bf16[144,2048]{1,0:T(8,128)(2,1)}, u32[]{:S(2)}) copy-start(bf16[144,2048]{1,0:T(8,128)(2,1)} %get-tuple-element.28.refs_3_) | copy-start | bytes 1769476
  16.1 1.0 %copy-start.11 = (bf16[112,2048]{1,0:T(8,128)(2,1)S(1)}, bf16[112,2048]{1,0:T(8,128)(2,1)}, u32[]{:S(2)}) copy-start(bf16[112,2048]{1,0:T(8,128)(2,1)} %get-tuple-element.29.refs_4_) | copy-start | bytes 1376260
  17.2 0.9 %copy-start.13 = (bf16[64,2048]{1,0:T(8,128)(2,1)S(1)}, bf16[64,2048]{1,0:T(8,128)(2,1)}, u32[]{:S(2)}) copy-start(bf16[64,2048]{1,0:T(8,128)(2,1)} %copy-done.12) | copy-start | bytes 786436
  18.1 0.9 %copy-start.15 = (bf16[48,2048]{1,0:T(8,128)(2,1)S(1)}, bf16[48,2048]{1,0:T(8,128)(2,1)}, u32[]{:S(2)}) copy-start(bf16[48,2048]{1,0:T(8,128)(2,1)} %copy-done.14) | copy-start | bytes 589828
  21.7 6.1 %copy-start.9 = (f32[2,4,128,128]{3,2,1,0:T(8,128)}, f32[2,4,128,128]{3,2,1,0:T(8,128)S(1)}, u32[]{:S(2)}) copy-start(f32[2,4,128,128]{3,2,1,0:T(8,128)S(1)} %get-tuple-element.35.refs_4_.refs_0_) | copy-start | bytes 1572868
  21.7 6.8 %copy-start.18 = (bf16[512,512]{1,0:T(8,128)(2,1)}, bf16[512,512]{1,0:T(8,128)(2,1)S(1)}, u32[]{:S(2)}) copy-start(bf16[512,512]{1,0:T(8,128)(2,1)S(1)} %get-tuple-element.41.refs_2_.refs_4_) | copy-start | bytes 1572868
  21.7 6.0 %collective-permute-start.5 = (bf16[4,128,128]{2,1,0:T(8,128)(2,1)S(1)}, bf16[4,128,128]{2,1,0:T(8,128)(2,1)S(1)}, u32[]{:S(2)}, u32[]{:S(2)}) collective-permute-start(bf16[4,128,128]{2,1,0:T(8,128)(2,1)S(1)} %prev_2.1), channel_id=1, source_target_pairs={{0,8},{4,12},{8,16},{12,20},{16,24},{20,28},{1,9},{5,13},{9,17},{1... | collective-permute-start | bytes 393224 | tf_op jit(solution)/shard_map/ppermute | solution.py:415
  27.7 0.7 %copy-start.16 = (bf16[4,128,128]{2,1,0:T(8,128)(2,1)}, bf16[4,128,128]{2,1,0:T(8,128)(2,1)S(1)}, u32[]{:S(2)}) copy-start(bf16[4,128,128]{2,1,0:T(8,128)(2,1)S(1)} %collective-permute-done.5.refs_1_) | copy-start | bytes 393220
  28.4 2.3 %collective-permute-start.7 = (bf16[144,2048]{1,0:T(8,128)(2,1)}, bf16[144,2048]{1,0:T(8,128)(2,1)}, u32[]{:S(2)}, u32[]{:S(2)}) collective-permute-start(bf16[144,2048]{1,0:T(8,128)(2,1)} %collective-permute-done.6.refs_3_), channel_id=1, source_target_pairs={{0,1},{1,0},{2,3},{3,2},{4,5},{5,4},{6,7},{7,6},{8,9},{9,8},{10,11... | collective-permute-start | bytes 1769480 | tf_op jit(solution)/shard_map/ppermute | solution.py:438
  29.8 3.3 %collective-permute-start.9 = (bf16[112,2048]{1,0:T(8,128)(2,1)}, bf16[112,2048]{1,0:T(8,128)(2,1)}, u32[]{:S(2)}, u32[]{:S(2)}) collective-permute-start(bf16[112,2048]{1,0:T(8,128)(2,1)} %collective-permute-done.8.refs_5_), channel_id=1, source_target_pairs={{0,1},{1,0},{2,3},{3,2},{4,5},{5,4},{6,7},{7,6},{8,9},{9,8},{10,11... | collective-permute-start | bytes 1376264 | tf_op jit(solution)/shard_map/ppermute | solution.py:438
  29.8 3.3 %copy-start.10 = (f32[2,4,128,128]{3,2,1,0:T(8,128)S(1)}, f32[2,4,128,128]{3,2,1,0:T(8,128)}, u32[]{:S(2)}) copy-start(f32[2,4,128,128]{3,2,1,0:T(8,128)} %copy-done.9) | copy-start | bytes 1572868
  33.1 3.3 %copy-start.3 = (bf16[1024,512]{1,0:T(8,128)(2,1)S(1)}, bf16[1024,512]{1,0:T(8,128)(2,1)}, u32[]{:S(2)}) copy-start(bf16[1024,512]{1,0:T(8,128)(2,1)} %key_ref.7) | copy-start | bytes 3145732
  33.1 3.3 %copy-start.5 = (bf16[1024,512]{1,0:T(8,128)(2,1)S(1)}, bf16[1024,512]{1,0:T(8,128)(2,1)}, u32[]{:S(2)}) copy-start(bf16[1024,512]{1,0:T(8,128)(2,1)} %value_ref.7) | copy-start | bytes 3145732
  33.2 3.3 %copy-start.17 = (bf16[4,128,128]{2,1,0:T(8,128)(2,1)S(1)}, bf16[4,128,128]{2,1,0:T(8,128)(2,1)}, u32[]{:S(2)}) copy-start(bf16[4,128,128]{2,1,0:T(8,128)(2,1)} %copy-done.16) | copy-start | bytes 393220
  33.2 3.2 %copy-start.19 = (bf16[512,512]{1,0:T(8,128)(2,1)S(1)}, bf16[512,512]{1,0:T(8,128)(2,1)}, u32[]{:S(2)}) copy-start(bf16[512,512]{1,0:T(8,128)(2,1)} %copy-done.18) | copy-start | bytes 1572868
  35.5 5.6 %collective-permute-start.10 = (bf16[4,128,128]{2,1,0:T(8,128)(2,1)S(1)}, bf16[4,128,128]{2,1,0:T(8,128)(2,1)S(1)}, u32[]{:S(2)}, u32[]{:S(2)}) collective-permute-start(bf16[4,128,128]{2,1,0:T(8,128)(2,1)S(1)} %get-tuple-element.40), channel_id=1, source_target_pairs={{0,4},{4,0},{8,12},{12,8},{16,20},{20,16},{24,28},{28,24},{1,5},{5... | collective-permute-start | bytes 393224 | tf_op jit(solution)/shard_map/ppermute | solution.py:415
  36.4 12.0 %copy-start.8 = (bf16[4,128,128]{2,1,0:T(8,128)(2,1)S(1)}, bf16[4,128,128]{2,1,0:T(8,128)(2,1)}, u32[]{:S(2)}) copy-start(bf16[4,128,128]{2,1,0:T(8,128)(2,1)} %copy-done.7) | copy-start | bytes 393220
  41.1 7.3 %collective-permute-start.11 = (bf16[4,128,128]{2,1,0:T(8,128)(2,1)S(1)}, bf16[4,128,128]{2,1,0:T(8,128)(2,1)S(1)}, u32[]{:S(2)}, u32[]{:S(2)}) collective-permute-start(bf16[4,128,128]{2,1,0:T(8,128)(2,1)S(1)} %next_2.1), channel_id=1, source_target_pairs={{8,0},{12,4},{16,8},{20,12},{24,16},{28,20},{9,1},{13,5},{17,9},{2... | collective-permute-start | bytes 393224 | tf_op jit(solution)/shard_map/ppermute | solution.py:415
  48.5 8.3 %collective-permute-start.12 = (bf16[4,128,128]{2,1,0:T(8,128)(2,1)S(1)}, bf16[4,128,128]{2,1,0:T(8,128)(2,1)S(1)}, u32[]{:S(2)}, u32[]{:S(2)}) collective-permute-start(bf16[4,128,128]{2,1,0:T(8,128)(2,1)S(1)} %swap_state.1), channel_id=1, source_target_pairs={{0,16},{4,20},{8,24},{12,28},{16,0},{20,4},{24,8},{28,12},{1,17},{... | collective-permute-start | bytes 393224 | tf_op jit(solution)/shard_map/ppermute | solution.py:480
  (1 other events, 0.7 us)

commit v4 on v3

--- a/solution.py
+++ b/solution.py
@@ -8,6 +8,7 @@
 from jax.sharding import PartitionSpec as P
 
 HEAD_DIM = 128
+QUAD = 4
 KEEP_SCALE = 1.0 / 0.9
 F32 = jnp.float32
 BF16 = jnp.bfloat16
@@ -177,12 +178,15 @@
     before_refs, refs = refs[:befores], refs[befores:]
     masked_refs, refs = refs[: len(pieces)], refs[len(pieces) :]
     grad_ref, state_ref = refs[:2]
-    masked, query = refs[-2:]
+    masked, query, sems = refs[-3:]
+    copies = []
     place = place_ref[0]
     spots, at = [], 0
     for ref, (flip, row) in zip(masked_refs, pieces):
         rows = ref.shape[0]
-        masked[at : at + rows, :] = ref[...]
+        copy = pltpu.make_async_copy(ref, masked.at[pl.ds(at, rows), :], sems.at[len(copies)])
+        copy.start()
+        copies.append(copy)
         start = pl.multiple_of(jnp.bitwise_xor(place, flip) * sub + row, 16)
         query[at : at + rows, :] = query_ref[pl.ds(start, rows), :]
         if spots and spots[-1][0] == flip:
@@ -191,6 +195,8 @@
             spots.append([flip, at, at + rows])
         at += rows
     spots = [slice(low, high) for _, low, high in spots]
+    for copy in copies:
+        copy.wait()
     grad = dot(masked[...], weight_ref[...], NT).astype(BF16)
     grad_ref[...] = grad
     for h in range(state_ref.shape[1]):
@@ -208,7 +214,7 @@
             short_ref[h] = total.astype(BF16)
 
 
-def grad_part(place, query_rows, out_weight, sub, befores, pieces, arrays, name):
+def grad_part(place, query_rows, out_weight, sub, befores, pieces, arrays, name, mib=20):
     width, model = out_weight.shape
     heads = width // HEAD_DIM
     rows = sum(a.shape[0] for a in arrays)
@@ -224,10 +230,14 @@
     return pl.pallas_call(
         functools.partial(grad_body, pieces, sub, len(befores), last),
         out_shape=tuple(out_shape),
-        in_specs=[smem()] + [vmem()] * (len(operands) - 1),
+        in_specs=[smem()] + [vmem()] * (2 + len(befores)) + [hbm()] * len(arrays),
         out_specs=tuple(vmem() for _ in out_shape),
-        scratch_shapes=[pltpu.VMEM((rows, model), BF16), pltpu.VMEM((rows, width), BF16)],
-        compiler_params=params(20),
+        scratch_shapes=[
+            pltpu.VMEM((rows, model), BF16),
+            pltpu.VMEM((rows, width), BF16),
+            pltpu.SemaphoreType.DMA((len(arrays),)),
+        ],
+        compiler_params=params(mib),
         cost_estimate=cost(1, 1),
         name=name,
     )(*operands)
@@ -247,14 +257,13 @@
     return col_id >= row_id if turned else row_id >= col_id
 
 
-def pair_state(ctx_ref, refs, reverse):
-    odd = jnp.bitwise_and(ctx_ref[0], 1) == 1
-    use = jnp.logical_not(odd) if reverse else odd
+def near_state(ctx_ref, refs, h, reverse):
     total = None
     for n, ref in enumerate(refs):
-        value = ref[0].astype(F32)
-        if n == 0:
-            value = value * use.astype(F32)
+        value = ref[h].astype(F32)
+        if n < QUAD - 1:
+            low = jnp.bitwise_and(ctx_ref[0], 1 if n == 0 else 2) == 0
+            value = jnp.where(low if reverse else jnp.logical_not(low), value, 0.0)
         total = value if total is None else total + value
     return total
 
@@ -265,95 +274,72 @@
     gather_grad(place_ref, grad_refs, places, sub, grad)
     keep = causal(sub, False)
     rows = [slice(at, at + sub) for at in range(0, key_ref.shape[0], sub)]
-    scores = [dot(grad[at, :], value_ref[at, :], NT) for at in rows]
-    states = [pair_state(ctx_ref, prev_refs, False)]
-    for at in rows[:-1]:
-        states.append(states[-1] + dot(key_ref[at, :], value_ref[at, :], TN))
-    totals = [dot(grad[at, :], state.astype(BF16), NT) for at, state in zip(rows, states)]
-    scores = [jnp.where(keep, score, 0.0).astype(BF16) for score in scores]
-    for at, score, total in zip(rows, scores, totals):
-        out_ref[at, :] = total + dot(score, key_ref[at, :], NN)
-
-
-def later_body(places, sub, parts, place_ref, ctx_ref, query_ref, key_ref, value_ref, *refs):
+    for h in range(key_ref.shape[1] // HEAD_DIM):
+        cols = head_cols(h)
+        scores = [dot(grad[at, cols], value_ref[at, cols], NT) for at in rows]
+        states = [near_state(ctx_ref, prev_refs, h, False)]
+        for at in rows[:-1]:
+            states.append(states[-1] + dot(key_ref[at, cols], value_ref[at, cols], TN))
+        totals = [dot(grad[at, cols], state.astype(BF16), NT) for at, state in zip(rows, states)]
+        scores = [jnp.where(keep, score, 0.0).astype(BF16) for score in scores]
+        for at, score, total in zip(rows, scores, totals):
+            out_ref[at, cols] = total + dot(score, key_ref[at, cols], NN)
+
+
+def later_body(sub, parts, place_ref, ctx_ref, query_ref, key_ref, value_ref, grad, *refs):
     near_ref, far_ref = refs[:2]
-    next_refs, refs = refs[2 : 2 + parts], refs[2 + parts :]
-    grad_refs, (key_out, value_out, grad_out, grad) = refs[: len(places)], refs[len(places) :]
-    gather_grad(place_ref, grad_refs, places, sub, grad)
-    grad_out[...] = grad[...]
+    next_refs, (key_out, value_out) = refs[2 : 2 + parts], refs[2 + parts :]
     place = place_ref[0]
     keep = causal(sub, True)
     rows = [slice(at, at + sub) for at in range(0, key_ref.shape[0], sub)]
     masked = lambda scores: [jnp.where(keep, score, 0.0).astype(BF16) for score in scores]
-    scores = [dot(value_ref[at, :], grad[at, :], NT) for at in rows]
-    attn = [dot(key_ref[at, :], query_ref[at, :], NT) for at in rows]
-    later = pair_state(ctx_ref, next_refs, True)
-    own = [near_ref[0, 0], near_ref[1, 0], far_ref[0, 0], far_ref[1, 0]]
-    states = []
-    for n in range(len(rows)):
-        total = later
-        for flip, state in enumerate(own):
-            total = total + jnp.where(jnp.bitwise_xor(place, flip) > n, state, 0.0)
-        states.append(total.astype(BF16))
-    scores = masked(scores)
-    for at, score, state in zip(rows, scores, states):
-        key_out[at, :] = dot(value_ref[at, :], state, NT) + dot(score, query_ref[at, :], NN)
-    attn = masked(attn)
-    for at, score, state in zip(rows, attn, states):
-        value_out[at, :] = dot(key_ref[at, :], state, NN) + dot(score, grad[at, :], NN)
-
-
-def column(rows):
-    return pl.BlockSpec((rows, HEAD_DIM), lambda h: (0, h))
-
-
-def head_state():
-    return pl.BlockSpec((1, HEAD_DIM, HEAD_DIM), lambda h: (h, 0, 0))
-
-
-def local_states(count):
-    return pl.BlockSpec((count, 1, HEAD_DIM, HEAD_DIM), lambda h: (0, h, 0, 0))
+    for h in range(key_ref.shape[1] // HEAD_DIM):
+        cols = head_cols(h)
+        scores = [dot(value_ref[at, cols], grad[at, cols], NT) for at in rows]
+        attn = [dot(key_ref[at, cols], query_ref[at, cols], NT) for at in rows]
+        later = near_state(ctx_ref, next_refs, h, True)
+        own = [near_ref[0, h], near_ref[1, h], far_ref[0, h], far_ref[1, h]]
+        states = []
+        for n in range(len(rows)):
+            total = later
+            for flip, state in enumerate(own):
+                total = total + jnp.where(jnp.bitwise_xor(place, flip) > n, state, 0.0)
+            states.append(total.astype(BF16))
+        scores = masked(scores)
+        for at, score, state in zip(rows, scores, states):
+            key_out[at, cols] = dot(value_ref[at, cols], state, NT) + dot(score, query_ref[at, cols], NN)
+        attn = masked(attn)
+        for at, score, state in zip(rows, attn, states):
+            value_out[at, cols] = dot(key_ref[at, cols], state, NN) + dot(score, grad[at, cols], NN)
 
 
 def query_products(place, ctx, key_rows, value_rows, prevs, grads, places, sub):
     tokens, width = key_rows.shape
     return pl.pallas_call(
         functools.partial(query_body, places, sub, len(prevs)),
-        out_shape=jax.ShapeDtypeStruct((tokens, width), F32),
-        grid=(width // HEAD_DIM,),
-        in_specs=[smem(), smem()]
-        + [column(tokens)] * 2
-        + [head_state()] * len(prevs)
-        + [column(g.shape[0]) for g in grads],
-        out_specs=column(tokens),
-        scratch_shapes=[pltpu.VMEM((tokens, HEAD_DIM), BF16)],
+        out_shape=(
+            jax.ShapeDtypeStruct((tokens, width), F32),
+            jax.ShapeDtypeStruct((tokens, width), BF16),
+        ),
+        in_specs=[smem(), smem()] + [vmem()] * (2 + len(prevs) + len(grads)),
+        out_specs=(vmem(), vmem()),
         compiler_params=params(16),
         cost_estimate=cost(4 * tokens * tokens * width, 8 * tokens * width),
         name="query_products",
     )(place, ctx, key_rows, value_rows, *prevs, *grads)
 
 
-def later_products(place, ctx, query_rows, key_rows, value_rows, near, far, nexts, grads, places, sub):
+def later_products(place, ctx, query_rows, key_rows, value_rows, grad_rows, near, far, nexts, sub):
     tokens, width = key_rows.shape
     return pl.pallas_call(
-        functools.partial(later_body, places, sub, len(nexts)),
-        out_shape=(
-            jax.ShapeDtypeStruct((tokens, width), F32),
-            jax.ShapeDtypeStruct((tokens, width), F32),
-            jax.ShapeDtypeStruct((tokens, width), BF16),
-        ),
-        grid=(width // HEAD_DIM,),
-        in_specs=[smem(), smem()]
-        + [column(tokens)] * 3
-        + [local_states(2), local_states(2)]
-        + [head_state()] * len(nexts)
-        + [column(g.shape[0]) for g in grads],
-        out_specs=(column(tokens),) * 3,
-        scratch_shapes=[pltpu.VMEM((tokens, HEAD_DIM), BF16)],
+        functools.partial(later_body, sub, len(nexts)),
+        out_shape=(jax.ShapeDtypeStruct((tokens, width), F32),) * 2,
+        in_specs=[smem(), smem()] + [vmem()] * (6 + len(nexts)),
+        out_specs=(vmem(), vmem()),
         compiler_params=params(16),
         cost_estimate=cost(8 * tokens * tokens * width, 10 * tokens * width),
         name="later_products",
-    )(place, ctx, query_rows, key_rows, value_rows, near, far, *nexts, *grads)
+    )(place, ctx, query_rows, key_rows, value_rows, grad_rows, near, far, *nexts)
 
 
 def end_body(sub, ctx_ref, half_ref, got_ref, key_ref, value_ref, grad_ref, *refs):
@@ -404,23 +390,18 @@
     )(ctx, half, got, key_rows, value_rows, grad_rows, *parts)
 
 
-def exchange(payload, reach, reverse):
+def scan_states(wide, short, reverse, ties, name):
     size = lax.axis_size("ctx")
-    if reach == 1:
-        pairs = [(i, i ^ 1) for i in range(size)]
-    elif reverse:
-        pairs = [(i + reach, i) for i in range(size - reach)]
-    else:
-        pairs = [(i, i + reach) for i in range(size - reach)]
-    return lax.ppermute(payload, "ctx", pairs)
-
-
-def scan_states(wide, short, reverse, tie, name):
-    received, reach, payload = [], 1, short
-    while reach < lax.axis_size("ctx") // 2:
-        if reach > 1:
-            payload = group_state(wide, received, [tie] if reach == 2 else [], "%s_%d" % (name, reach))
-        received.append(exchange(payload, reach, reverse))
+    send = lambda payload, pairs: lax.ppermute(payload, "ctx", pairs)
+    received = [send(short, [(i, i ^ k) for i in range(size)]) for k in range(1, QUAD)]
+    reach = QUAD
+    while reach < size // 2:
+        payload = group_state(wide, received, ties if reach == QUAD else [], "%s_%d" % (name, reach))
+        if reverse:
+            pairs = [(i + reach, i) for i in range(size - reach)]
+        else:
+            pairs = [(i, i + reach) for i in range(size - reach)]
+        received.append(send(payload, pairs))
         reach *= 2
     return received
 
@@ -440,14 +421,15 @@
     first, *near_first = mask_rows(out_grad, keep_mask, 0, (5 * unit, 4 * unit), "mask_first")
     last, *near_last = mask_rows(out_grad, keep_mask, split, (4 * unit, 3 * unit), "mask_last")
     far_first, far_last = swap(first, 2), swap(last, 2)
+    kv_wide, kv_short = kv_state(key_rows, value_rows)
+    prevs = scan_states(kv_wide, kv_short, False, [], "prev")
     near = [swap(piece, 1) for piece in near_first + near_last]
-    kv_wide, kv_short = kv_state(key_rows, value_rows)
 
     part = functools.partial(grad_part, place, query_rows, out_weight, own_rows)
     grads, places, states = [], [], []
 
-    def run(befores, pieces, arrays, name):
-        got = part(befores, pieces, arrays, name)
+    def run(befores, pieces, arrays, name, mib=20):
+        got = part(befores, pieces, arrays, name, mib)
         at, spots = 0, []
         for (flip, row), array in zip(pieces, arrays):
             spots.append((at, array.shape[0], flip, row))
@@ -458,10 +440,9 @@
         return got
 
     pieces = ((0, 0), (0, split), (1, 0), (1, 5 * unit), (1, split), (1, split + 4 * unit))
-    run([], pieces, [first, last] + near[:-1] + [after(near[-1], kv_short)], "grad_near")
-
-    prevs = scan_states(kv_wide, kv_short, False, states[0], "prev")
-    prev_sum = group_state(kv_wide, prevs, [], "prev_sum")
+    run([], pieces, [first, last] + near, "grad_near", 60)
+
+    prev_sum = group_state(kv_wide, prevs, [states[0]], "prev_sum")
 
     far_first = after(far_first, prev_sum, states[0])
     run([], ((2, 0), (3, 0)), [far_first, swap(far_first, 1)], "grad_far")
@@ -473,13 +454,14 @@
     )
 
     spots = tuple(places)
-    query_part = query_products(place, ctx, key_rows, value_rows, prevs, grads, spots, own_rows)
-    nexts = scan_states(wide, short, True, query_part, "next")
+    query_part, grad_rows = query_products(place, ctx, key_rows, value_rows, prevs, grads, spots, own_rows)
+    nexts = scan_states(wide, short, True, [query_part], "next")
+    nexts[-1] = after(nexts[-1], query_part)
     payload = swap_state(ctx, half, prev_sum, wide, nexts)
     size = lax.axis_size("ctx")
     got = lax.ppermute(payload, "ctx", [(i, (i + size // 2) % size) for i in range(size)])
-    key_part, value_part, grad_rows = later_products(
-        place, ctx, query_rows, key_rows, value_rows, states[0], far, nexts, grads, spots, own_rows
+    key_part, value_part = later_products(
+        place, ctx, query_rows, key_rows, value_rows, grad_rows, states[0], far, nexts, own_rows
     )
     parts = (query_part, key_part, value_part)
     return end_products(ctx, half, got, key_rows, value_rows, grad_rows, parts, own_rows)

time: 59.4 us -> 56.2 us (0.946)
  local copies, waits for them, and re-layouts: 5.38 us -> 3 us
  Pallas kernels: 24.2 us -> 26.2 us
  waiting for transfers between devices: 13.3 us -> 11.8 us
  starting transfers between devices: 15.2 us -> 14.1 us
    ppermute x4 -> x6, waiting for transfers between devices: 9.97 us -> 3.53 us  [scan_states(): send = lambda payload, pairs: lax.ppermute(payload, 'ctx', pairs)]
    pallas_call x3, Pallas kernels: 7.21 us -> 10.6 us  [grad_part(): pl.pallas_call(functools.partial(grad_body, pieces, sub, len(befores), la...]
    ppermute x1, waiting for transfers between devices: 0.01 us -> 3.28 us  [per_device(): lax.ppermute(payload, 'ctx', [(i, (i + size // 2) % size) for i in range(...]
    unnamed x40 -> x30, local copies, waits for them, and re-layouts: 5.38 us -> 3 us
    pallas_call x1, Pallas kernels: 5.26 us -> 3.1 us  [later_products(): pl.pallas_call(functools.partial(later_body, sub, len(nexts)), out_shape=...]
    ppermute x8, waiting for transfers between devices: 3.34 us -> 4.98 us  [swap(): return lax.ppermute(array, 'head', [(i, i ^ distance) for i in range(size)])]
    pallas_call x3 -> x1, Pallas kernels: 0.1 us -> 1.03 us  [group_state(): pl.pallas_call(functools.partial(group_body, len(received)), out_shape=ja...]
    ppermute x4 -> x6, starting transfers between devices: 7.92 us -> 7.19 us  [scan_states(): send = lambda payload, pairs: lax.ppermute(payload, 'ctx', pairs)]
  transfers between devices with their start and end apart: 13 -> 15, of which waited for: 6 -> 5; matrix products, arithmetic and copies ran while one was open for 0% -> 0% of each run, Pallas kernels for 29% -> 34%
where the time goes in v4:
time: 56.2 us; the launch traced here: 56 us
  Pallas kernels  26.2 us (47%)
  starting transfers between devices  14.1 us (25%)
  waiting for transfers between devices  11.8 us (21%)
  local copies, waits for them, and re-layouts  3 us (5%)
  between operations  0.86 us (2%)
    pallas_call x3, Pallas kernels, grad_part(): pl.pallas_call(functools.partial(grad_body, pieces, sub, len(befores), la...  10.6 us
    ppermute x6, starting transfers between devices, scan_states(): send = lambda payload, pairs: lax.ppermute(payload, 'ctx', pairs)  7.19 us
    pallas_call x2, Pallas kernels, mask_rows(): pl.pallas_call(functools.partial(mask_body, row), out_shape=tuple((jax.Sh...  5.07 us
    ppermute x8, waiting for transfers between devices, swap(): return lax.ppermute(array, 'head', [(i, i ^ distance) for i in range(size)])  4.98 us
    ppermute x8, starting transfers between devices, swap(): return lax.ppermute(array, 'head', [(i, i ^ distance) for i in range(size)])  4.31 us
    ppermute x6, waiting for transfers between devices, scan_states(): send = lambda payload, pairs: lax.ppermute(payload, 'ctx', pairs)  3.53 us
    ppermute x1, waiting for transfers between devices, per_device(): lax.ppermute(payload, 'ctx', [(i, (i + size // 2) % size) for i in range(...  3.28 us
    pallas_call x1, Pallas kernels, later_products(): pl.pallas_call(functools.partial(later_body, sub, len(nexts)), out_shape=...  3.1 us
  transfers between devices with their start and end apart: 15, of which 5 were waited for; matrix products, arithmetic and copies ran while one was open for 0% of the time, Pallas kernels for 34%

profile of v4, /device:TPU:0, one launch (start us, length us, event | category | flops | bytes accessed | tf_op | source)
XLA Modules:
  0.0 56.0 jit_solution(12019381797723697938)
XLA Ops:
  0.6 2.6 %mask_first.1 = (bf16[144,2048]{1,0:T(8,128)(2,1)}, bf16[80,2048]{1,0:T(8,128)(2,1)}, bf16[64,2048]{1,0:T(8,128)(2,1)}) custom-call(bf16[256,2048]{1,0:T(8,128)(2,1)} %grad_ref.3, s32[256,2048]{1,0:T(8,128)} %keep_ref.3), custom_call_target="tpu_custom_call" | custom-call | flops 1 | bytes 1 | tf_op jit(solution)/shard_map/mask_first/pallas_call | solution.py:93
  3.3 3.0 %collective-permute-start.7 = (bf16[144,2048]{1,0:T(8,128)(2,1)}, bf16[144,2048]{1,0:T(8,128)(2,1)}, u32[]{:S(2)}, u32[]{:S(2)}) collective-permute-start(bf16[144,2048]{1,0:T(8,128)(2,1)} %get-tuple-element.28.refs_3_), channel_id=1, source_target_pairs={{0,2},{1,3},{2,0},{3,1},{4,6},{5,7},{6,4},{7,5},{8,10},{9,11},{10,... | collective-permute-start | bytes 1769480 | tf_op jit(solution)/shard_map/ppermute | solution.py:419
  6.3 2.4 %mask_last.1 = (bf16[112,2048]{1,0:T(8,128)(2,1)}, bf16[64,2048]{1,0:T(8,128)(2,1)}, bf16[48,2048]{1,0:T(8,128)(2,1)}) custom-call(bf16[256,2048]{1,0:T(8,128)(2,1)} %grad_ref.3, s32[256,2048]{1,0:T(8,128)} %keep_ref.3), custom_call_target="tpu_custom_call" | custom-call | flops 1 | bytes 1 | tf_op jit(solution)/shard_map/mask_last/pallas_call | solution.py:93
  8.9 0.5 collective-permute-start.3
  9.3 0.1 collective-permute-start.5
  9.4 0.4 collective-permute-start.4
  9.9 0.6 %collective-permute-done.6.refs_8_ = bf16[48,2048]{1,0:T(8,128)(2,1)S(1)} collective-permute-done((bf16[48,2048]{1,0:T(8,128)(2,1)}, bf16[48,2048]{1,0:T(8,128)(2,1)S(1)}, u32[]{:S(2)}, u32[]{:S(2)}) %collective-permute-start.6) | collective-permute-done | bytes 196640 | tf_op jit(solution)/shard_map/ppermute | solution.py:419
  10.5 0.7 %copy-done.12 = bf16[48,2048]{1,0:T(8,128)(2,1)} copy-done((bf16[48,2048]{1,0:T(8,128)(2,1)}, bf16[48,2048]{1,0:T(8,128)(2,1)S(1)}, u32[]{:S(2)}) %copy-start.12) | copy-done | bytes 196632
  11.2 0.2 collective-permute-start.9
  11.3 1.1 %kv_state.1 = (f32[4,128,128]{2,1,0:T(8,128)S(1)}, bf16[4,128,128]{2,1,0:T(8,128)(2,1)}) custom-call(bf16[1024,512]{1,0:T(8,128)(2,1)S(1)} %copy-done.2, bf16[1024,512]{1,0:T(8,128)(2,1)S(1)} %copy-done.4), custom_call_target="tpu_custom_call" | custom-call | flops 1 | bytes 1 | tf_op jit(solution)/shard_map/kv_state/pallas_call | solution.py:120
  12.5 0.7 %copy-done.11 = bf16[64,2048]{1,0:T(8,128)(2,1)} copy-done((bf16[64,2048]{1,0:T(8,128)(2,1)}, bf16[64,2048]{1,0:T(8,128)(2,1)S(1)}, u32[]{:S(2)}) %copy-start.11) | copy-done | bytes 262168
  13.2 3.1 %collective-permute-start.2 = (bf16[4,128,128]{2,1,0:T(8,128)(2,1)}, bf16[4,128,128]{2,1,0:T(8,128)(2,1)S(1)}, u32[]{:S(2)}, u32[]{:S(2)}) collective-permute-start(bf16[4,128,128]{2,1,0:T(8,128)(2,1)} %get-tuple-element.27), channel_id=1, source_target_pairs={{0,12},{4,8},{8,4},{12,0},{16,28},{20,24},{24,20},{28,16},{1,13},{... | collective-permute-start | bytes 393224 | tf_op jit(solution)/shard_map/ppermute | solution.py:395
  16.3 0.4 collective-permute-start.1
  16.7 0.1 collective-permute-start
  16.8 5.9 %grad_near.1 = (bf16[512,512]{1,0:T(8,128)(2,1)}, f32[2,4,128,128]{3,2,1,0:T(8,128)}) custom-call(s32[1]{0:T(128)} %bitcast.1.refs_0_.place_ref, bf16[1024,512]{1,0:T(8,128)(2,1)} %query_ref.1, bf16[512,2048]{1,0:T(8,128)(2,1)} %refs_2_.5, bf16[144,2048]{1,0:T(8,128)(2,1)} %get-tuple-element.28.refs_3_, bf16[112,2048]{1,0:T(8,128)(2,1)} %get-tuple-element.29.refs_4_, ...), custom_call_target="tpu_custom_call" | custom-call | flops 1 | bytes 1 | tf_op jit(solution)/shard_map/grad_near/pallas_call | solution.py:230
  22.8 0.6 %copy-done.7 = bf16[4,128,128]{2,1,0:T(8,128)(2,1)} copy-done((bf16[4,128,128]{2,1,0:T(8,128)(2,1)}, bf16[4,128,128]{2,1,0:T(8,128)(2,1)S(1)}, u32[]{:S(2)}) %copy-start.7) | copy-done | bytes 131096
  23.5 0.9 %copy-done.8 = bf16[4,128,128]{2,1,0:T(8,128)(2,1)S(1)} copy-done((bf16[4,128,128]{2,1,0:T(8,128)(2,1)S(1)}, bf16[4,128,128]{2,1,0:T(8,128)(2,1)}, u32[]{:S(2)}) %copy-start.8) | copy-done | bytes 131096
  24.4 1.0 %prev_sum.1.prev_ref = bf16[4,128,128]{2,1,0:T(8,128)(2,1)S(1)} custom-call(f32[4,128,128]{2,1,0:T(8,128)S(1)} %get-tuple-element.26.wide_ref, bf16[4,128,128]{2,1,0:T(8,128)(2,1)} %collective-permute-done.refs_0_, bf16[4,128,128]{2,1,0:T(8,128)(2,1)} %collective-permute-done.1.refs_1_, bf16[4,128,128]{2,1,0:T(8,128)(2,1)S(1)} %copy-done.8), custom_call_target="tpu_custom_call" | custom-call | flops 1 | bytes 1 | tf_op jit(solution)/shard_map/prev_sum/pallas_call | solution.py:144
  25.5 4.3 %collective-permute-done.9.refs_5_ = bf16[112,2048]{1,0:T(8,128)(2,1)} collective-permute-done((bf16[112,2048]{1,0:T(8,128)(2,1)}, bf16[112,2048]{1,0:T(8,128)(2,1)}, u32[]{:S(2)}, u32[]{:S(2)}) %collective-permute-start.9) | collective-permute-done | bytes 458784 | tf_op jit(solution)/shard_map/ppermute | solution.py:419
  29.8 2.4 %grad_far.1 = (bf16[288,512]{1,0:T(8,128)(2,1)S(1)}, f32[2,4,128,128]{3,2,1,0:T(8,128)S(1)}) custom-call(s32[1]{0:T(128)} %bitcast.1.refs_0_.place_ref, bf16[1024,512]{1,0:T(8,128)(2,1)S(1)} %copy-done.1, bf16[512,2048]{1,0:T(8,128)(2,1)S(1)} %copy-done, bf16[144,2048]{1,0:T(8,128)(2,1)} %collective-permute-done.7.refs_3_, ...), custom_call_target="tpu_custom_call" | custom-call | flops 1 | bytes 1 | tf_op jit(solution)/shard_map/grad_far/pallas_call | solution.py:230
  32.3 2.3 %grad_last.1 = (bf16[224,512]{1,0:T(8,128)(2,1)S(1)}, f32[2,4,128,128]{3,2,1,0:T(8,128)S(1)}, f32[4,128,128]{2,1,0:T(8,128)S(1)}, bf16[4,128,128]{2,1,0:T(8,128)(2,1)S(1)}) custom-call(s32[1]{0:T(128)} %bitcast.1.refs_0_.place_ref, bf16[1024,512]{1,0:T(8,128)(2,1)S(1)} %copy-done.1, bf16[512,2048]{1,0:T(8,128)(2,1)S(1)} %copy-done, ...), custom_call_target="tpu_custom_call" | custom-call | flops 1 | bytes 1 | tf_op jit(solution)/shard_map/grad_last/pallas_call | solution.py:230
  34.6 2.8 %collective-permute-start.13 = (bf16[4,128,128]{2,1,0:T(8,128)(2,1)S(1)}, bf16[4,128,128]{2,1,0:T(8,128)(2,1)S(1)}, u32[]{:S(2)}, u32[]{:S(2)}) collective-permute-start(bf16[4,128,128]{2,1,0:T(8,128)(2,1)S(1)} %get-tuple-element.39), channel_id=1, source_target_pairs={{0,12},{4,8},{8,4},{12,0},{16,28},{20,24},{24,20},{28,16},{1,13},{... | collective-permute-start | bytes 393224 | tf_op jit(solution)/shard_map/ppermute | solution.py:395
  37.5 0.4 collective-permute-start.12
  37.9 0.3 collective-permute-start.11
  38.2 2.9 %query_products.1 = (f32[1024,512]{1,0:T(8,128)S(1)}, bf16[1024,512]{1,0:T(8,128)(2,1)S(1)}) custom-call(s32[1]{0:T(128)} %bitcast.1.refs_0_.place_ref, s32[1]{0:T(128)} %bitcast.ctx_ref, bf16[1024,512]{1,0:T(8,128)(2,1)S(1)} %copy-done.3, bf16[1024,512]{1,0:T(8,128)(2,1)S(1)} %copy-done.5, bf16[4,128,128]{2,1,0:T(8,128)(2,1)} %collective-permute-done.refs_0_, ...), custom_call_target="tpu_custom_call" | custom-call | flops 2147483648 | bytes 4194304 | tf_op jit(solution)/shard_map/query_products/pallas_call | solution.py:318
  41.1 0.8 %collective-permute-done.13.refs_2_.refs_4_ = bf16[4,128,128]{2,1,0:T(8,128)(2,1)S(1)} collective-permute-done((bf16[4,128,128]{2,1,0:T(8,128)(2,1)S(1)}, bf16[4,128,128]{2,1,0:T(8,128)(2,1)S(1)}, u32[]{:S(2)}, u32[]{:S(2)}) %collective-permute-start.13) | collective-permute-done | bytes 131104 | tf_op jit(solution)/shard_map/ppermute | solution.py:395
  42.0 2.7 %collective-permute-done.12.refs_1_.refs_3_ = bf16[4,128,128]{2,1,0:T(8,128)(2,1)S(1)} collective-permute-done((bf16[4,128,128]{2,1,0:T(8,128)(2,1)S(1)}, bf16[4,128,128]{2,1,0:T(8,128)(2,1)S(1)}, u32[]{:S(2)}, u32[]{:S(2)}) %collective-permute-start.12) | collective-permute-done | bytes 131104 | tf_op jit(solution)/shard_map/ppermute | solution.py:395
  44.7 0.1 swap_state.1
  44.7 2.6 %collective-permute-start.14 = (bf16[4,128,128]{2,1,0:T(8,128)(2,1)S(1)}, bf16[4,128,128]{2,1,0:T(8,128)(2,1)S(1)}, u32[]{:S(2)}, u32[]{:S(2)}) collective-permute-start(bf16[4,128,128]{2,1,0:T(8,128)(2,1)S(1)} %swap_state.1), channel_id=1, source_target_pairs={{0,16},{4,20},{8,24},{12,28},{16,0},{20,4},{24,8},{28,12},{1,17},{... | collective-permute-start | bytes 393224 | tf_op jit(solution)/shard_map/ppermute | solution.py:462
  47.4 3.1 %later_products.1 = (f32[1024,512]{1,0:T(8,128)S(1)}, f32[1024,512]{1,0:T(8,128)S(1)}) custom-call(s32[1]{0:T(128)} %bitcast.1.refs_0_.place_ref, s32[1]{0:T(128)} %bitcast.ctx_ref, bf16[1024,512]{1,0:T(8,128)(2,1)S(1)} %copy-done.1, bf16[1024,512]{1,0:T(8,128)(2,1)S(1)} %copy-done.3, bf16[1024,512]{1,0:T(8,128)(2,1)S(1)} %copy-done.5, ...), custom_call_target="tpu_custom_call" | custom-call | flops 4294967296 | bytes 5242880 | tf_op jit(solution)/shard_map/later_products/pallas_call | solution.py:334
  50.5 3.3 %collective-permute-done.14.got_ref = bf16[4,128,128]{2,1,0:T(8,128)(2,1)S(1)} collective-permute-done((bf16[4,128,128]{2,1,0:T(8,128)(2,1)S(1)}, bf16[4,128,128]{2,1,0:T(8,128)(2,1)S(1)}, u32[]{:S(2)}, u32[]{:S(2)}) %collective-permute-start.14) | collective-permute-done | bytes 131104 | tf_op jit(solution)/shard_map/ppermute | solution.py:462
  53.8 2.2 %end_products.1 = (bf16[1024,512]{1,0:T(8,128)(2,1)}, bf16[1024,512]{1,0:T(8,128)(2,1)}, bf16[1024,512]{1,0:T(8,128)(2,1)}) custom-call(s32[1]{0:T(128)} %bitcast.ctx_ref, s32[1]{0:T(128)} %constant.9.clone.1.half_ref, bf16[4,128,128]{2,1,0:T(8,128)(2,1)S(1)} %collective-permute-done.14.got_ref, bf16[1024,512]{1,0:T(8,128)(2,1)S(1)} %copy-done.3, ...), custom_call_target="tpu_custom_call" | custom-call | flops 402653184 | bytes 8388608 | tf_op jit(solution)/shard_map/end_products/pallas_call | solution.py:378
  (39 shorter events, 0.2 us)
Async XLA Ops:
  3.3 5.6 %copy-start.13 = (bf16[80,2048]{1,0:T(8,128)(2,1)S(1)}, bf16[80,2048]{1,0:T(8,128)(2,1)}, u32[]{:S(2)}) copy-start(bf16[80,2048]{1,0:T(8,128)(2,1)} %get-tuple-element.30) | copy-start | bytes 983044
  3.3 6.1 %copy-start.14 = (bf16[64,2048]{1,0:T(8,128)(2,1)S(1)}, bf16[64,2048]{1,0:T(8,128)(2,1)}, u32[]{:S(2)}) copy-start(bf16[64,2048]{1,0:T(8,128)(2,1)} %get-tuple-element.31) | copy-start | bytes 786436
  3.3 8.0 %copy-start.2 = (bf16[1024,512]{1,0:T(8,128)(2,1)S(1)}, bf16[1024,512]{1,0:T(8,128)(2,1)}, u32[]{:S(2)}) copy-start(bf16[1024,512]{1,0:T(8,128)(2,1)} %key_ref.7) | copy-start | bytes 3145732
  3.3 8.0 %copy-start.4 = (bf16[1024,512]{1,0:T(8,128)(2,1)S(1)}, bf16[1024,512]{1,0:T(8,128)(2,1)}, u32[]{:S(2)}) copy-start(bf16[1024,512]{1,0:T(8,128)(2,1)} %value_ref.7) | copy-start | bytes 3145732
  3.3 22.1 %collective-permute-start.7 = (bf16[144,2048]{1,0:T(8,128)(2,1)}, bf16[144,2048]{1,0:T(8,128)(2,1)}, u32[]{:S(2)}, u32[]{:S(2)}) collective-permute-start(bf16[144,2048]{1,0:T(8,128)(2,1)} %get-tuple-element.28.refs_3_), channel_id=1, source_target_pairs={{0,2},{1,3},{2,0},{3,1},{4,6},{5,7},{6,4},{7,5},{8,10},{9,11},{10,... | collective-permute-start | bytes 1769480 | tf_op jit(solution)/shard_map/ppermute | solution.py:419
  8.8 1.7 %collective-permute-start.6 = (bf16[48,2048]{1,0:T(8,128)(2,1)}, bf16[48,2048]{1,0:T(8,128)(2,1)S(1)}, u32[]{:S(2)}, u32[]{:S(2)}) collective-permute-start(bf16[48,2048]{1,0:T(8,128)(2,1)} %get-tuple-element.33), channel_id=1, source_target_pairs={{0,1},{1,0},{2,3},{3,2},{4,5},{5,4},{6,7},{7,6},{8,9},{9,8},{10,11... | collective-permute-start | bytes 589832 | tf_op jit(solution)/shard_map/ppermute | solution.py:419
  8.9 7.9 %collective-permute-start.3 = (bf16[80,2048]{1,0:T(8,128)(2,1)S(1)}, bf16[80,2048]{1,0:T(8,128)(2,1)}, u32[]{:S(2)}, u32[]{:S(2)}) collective-permute-start(bf16[80,2048]{1,0:T(8,128)(2,1)S(1)} %copy-done.13), channel_id=1, source_target_pairs={{0,1},{1,0},{2,3},{3,2},{4,5},{5,4},{6,7},{7,6},{8,9},{9,8},{10,11... | collective-permute-start | bytes 983048 | tf_op jit(solution)/shard_map/ppermute | solution.py:419
  9.3 3.2 %collective-permute-start.5 = (bf16[64,2048]{1,0:T(8,128)(2,1)}, bf16[64,2048]{1,0:T(8,128)(2,1)S(1)}, u32[]{:S(2)}, u32[]{:S(2)}) collective-permute-start(bf16[64,2048]{1,0:T(8,128)(2,1)} %get-tuple-element.32), channel_id=1, source_target_pairs={{0,1},{1,0},{2,3},{3,2},{4,5},{5,4},{6,7},{7,6},{8,9},{9,8},{10,11... | collective-permute-start | bytes 786440 | tf_op jit(solution)/shard_map/ppermute | solution.py:419
  9.4 6.8 %collective-permute-start.4 = (bf16[64,2048]{1,0:T(8,128)(2,1)S(1)}, bf16[64,2048]{1,0:T(8,128)(2,1)}, u32[]{:S(2)}, u32[]{:S(2)}) collective-permute-start(bf16[64,2048]{1,0:T(8,128)(2,1)S(1)} %copy-done.14), channel_id=1, source_target_pairs={{0,1},{1,0},{2,3},{3,2},{4,5},{5,4},{6,7},{7,6},{8,9},{9,8},{10,11... | collective-permute-start | bytes 786440 | tf_op jit(solution)/shard_map/ppermute | solution.py:419
  10.5 0.7 %copy-start.12 = (bf16[48,2048]{1,0:T(8,128)(2,1)}, bf16[48,2048]{1,0:T(8,128)(2,1)S(1)}, u32[]{:S(2)}) copy-start(bf16[48,2048]{1,0:T(8,128)(2,1)S(1)} %collective-permute-done.6.refs_8_) | copy-start | bytes 589828
  11.2 18.6 %collective-permute-start.9 = (bf16[112,2048]{1,0:T(8,128)(2,1)}, bf16[112,2048]{1,0:T(8,128)(2,1)}, u32[]{:S(2)}, u32[]{:S(2)}) collective-permute-start(bf16[112,2048]{1,0:T(8,128)(2,1)} %get-tuple-element.29.refs_4_), channel_id=1, source_target_pairs={{0,2},{1,3},{2,0},{3,1},{4,6},{5,7},{6,4},{7,5},{8,10},{9,11},{10,... | collective-permute-start | bytes 1376264 | tf_op jit(solution)/shard_map/ppermute | solution.py:419
  12.5 0.7 %copy-start.11 = (bf16[64,2048]{1,0:T(8,128)(2,1)}, bf16[64,2048]{1,0:T(8,128)(2,1)S(1)}, u32[]{:S(2)}) copy-start(bf16[64,2048]{1,0:T(8,128)(2,1)S(1)} %collective-permute-done.5.refs_7_) | copy-start | bytes 786436
  13.2 9.6 %collective-permute-start.2 = (bf16[4,128,128]{2,1,0:T(8,128)(2,1)}, bf16[4,128,128]{2,1,0:T(8,128)(2,1)S(1)}, u32[]{:S(2)}, u32[]{:S(2)}) collective-permute-start(bf16[4,128,128]{2,1,0:T(8,128)(2,1)} %get-tuple-element.27), channel_id=1, source_target_pairs={{0,12},{4,8},{8,4},{12,0},{16,28},{20,24},{24,20},{28,16},{1,13},{... | collective-permute-start | bytes 393224 | tf_op jit(solution)/shard_map/ppermute | solution.py:395
  16.3 7.2 %collective-permute-start.1 = (bf16[4,128,128]{2,1,0:T(8,128)(2,1)}, bf16[4,128,128]{2,1,0:T(8,128)(2,1)}, u32[]{:S(2)}, u32[]{:S(2)}) collective-permute-start(bf16[4,128,128]{2,1,0:T(8,128)(2,1)} %get-tuple-element.27), channel_id=1, source_target_pairs={{0,8},{4,12},{8,0},{12,4},{16,24},{20,28},{24,16},{28,20},{1,9},{5... | collective-permute-start | bytes 393224 | tf_op jit(solution)/shard_map/ppermute | solution.py:395
  16.7 6.7 %collective-permute-start = (bf16[4,128,128]{2,1,0:T(8,128)(2,1)}, bf16[4,128,128]{2,1,0:T(8,128)(2,1)}, u32[]{:S(2)}, u32[]{:S(2)}) collective-permute-start(bf16[4,128,128]{2,1,0:T(8,128)(2,1)} %get-tuple-element.27), channel_id=1, source_target_pairs={{0,4},{4,0},{8,12},{12,8},{16,20},{20,16},{24,28},{28,24},{1,5},{5... | collective-permute-start | bytes 393224 | tf_op jit(solution)/shard_map/ppermute | solution.py:395
  16.8 13.0 %copy-start = (bf16[512,2048]{1,0:T(8,128)(2,1)S(1)}, bf16[512,2048]{1,0:T(8,128)(2,1)}, u32[]{:S(2)}) copy-start(bf16[512,2048]{1,0:T(8,128)(2,1)} %refs_2_.5) | copy-start | bytes 6291460
  16.8 13.0 %copy-start.1 = (bf16[1024,512]{1,0:T(8,128)(2,1)S(1)}, bf16[1024,512]{1,0:T(8,128)(2,1)}, u32[]{:S(2)}) copy-start(bf16[1024,512]{1,0:T(8,128)(2,1)} %query_ref.1) | copy-start | bytes 3145732
  22.8 0.7 %copy-start.7 = (bf16[4,128,128]{2,1,0:T(8,128)(2,1)}, bf16[4,128,128]{2,1,0:T(8,128)(2,1)S(1)}, u32[]{:S(2)}) copy-start(bf16[4,128,128]{2,1,0:T(8,128)(2,1)S(1)} %collective-permute-done.2.refs_2_) | copy-start | bytes 393220
  23.4 0.9 %copy-start.8 = (bf16[4,128,128]{2,1,0:T(8,128)(2,1)S(1)}, bf16[4,128,128]{2,1,0:T(8,128)(2,1)}, u32[]{:S(2)}) copy-start(bf16[4,128,128]{2,1,0:T(8,128)(2,1)} %copy-done.7) | copy-start | bytes 393220
  25.4 4.4 %collective-permute-start.8 = (bf16[144,2048]{1,0:T(8,128)(2,1)}, bf16[144,2048]{1,0:T(8,128)(2,1)}, u32[]{:S(2)}, u32[]{:S(2)}) collective-permute-start(bf16[144,2048]{1,0:T(8,128)(2,1)} %collective-permute-done.7.refs_3_), channel_id=1, source_target_pairs={{0,1},{1,0},{2,3},{3,2},{4,5},{5,4},{6,7},{7,6},{8,9},{9,8},{10,11... | collective-permute-start | bytes 1769480 | tf_op jit(solution)/shard_map/ppermute | solution.py:419
  29.8 2.4 %collective-permute-start.10 = (bf16[112,2048]{1,0:T(8,128)(2,1)}, bf16[112,2048]{1,0:T(8,128)(2,1)}, u32[]{:S(2)}, u32[]{:S(2)}) collective-permute-start(bf16[112,2048]{1,0:T(8,128)(2,1)} %collective-permute-done.9.refs_5_), channel_id=1, source_target_pairs={{0,1},{1,0},{2,3},{3,2},{4,5},{5,4},{6,7},{7,6},{8,9},{9,8},{10,11... | collective-permute-start | bytes 1376264 | tf_op jit(solution)/shard_map/ppermute | solution.py:419
  29.8 2.4 %copy-start.6 = (f32[2,4,128,128]{3,2,1,0:T(8,128)S(1)}, f32[2,4,128,128]{3,2,1,0:T(8,128)}, u32[]{:S(2)}) copy-start(f32[2,4,128,128]{3,2,1,0:T(8,128)} %get-tuple-element.34.refs_4_.refs_0_) | copy-start | bytes 1572868
  32.3 5.9 %copy-start.3 = (bf16[1024,512]{1,0:T(8,128)(2,1)S(1)}, bf16[1024,512]{1,0:T(8,128)(2,1)}, u32[]{:S(2)}) copy-start(bf16[1024,512]{1,0:T(8,128)(2,1)} %key_ref.7) | copy-start | bytes 3145732
  32.3 5.9 %copy-start.5 = (bf16[1024,512]{1,0:T(8,128)(2,1)S(1)}, bf16[1024,512]{1,0:T(8,128)(2,1)}, u32[]{:S(2)}) copy-start(bf16[1024,512]{1,0:T(8,128)(2,1)} %value_ref.7) | copy-start | bytes 3145732
  32.3 5.9 %copy-start.9 = (bf16[4,128,128]{2,1,0:T(8,128)(2,1)S(1)}, bf16[4,128,128]{2,1,0:T(8,128)(2,1)}, u32[]{:S(2)}) copy-start(bf16[4,128,128]{2,1,0:T(8,128)(2,1)} %copy-done.7) | copy-start | bytes 393220
  32.3 5.9 %copy-start.10 = (bf16[512,512]{1,0:T(8,128)(2,1)S(1)}, bf16[512,512]{1,0:T(8,128)(2,1)}, u32[]{:S(2)}) copy-start(bf16[512,512]{1,0:T(8,128)(2,1)} %get-tuple-element.40.refs_3_) | copy-start | bytes 1572868
  34.6 7.3 %collective-permute-start.13 = (bf16[4,128,128]{2,1,0:T(8,128)(2,1)S(1)}, bf16[4,128,128]{2,1,0:T(8,128)(2,1)S(1)}, u32[]{:S(2)}, u32[]{:S(2)}) collective-permute-start(bf16[4,128,128]{2,1,0:T(8,128)(2,1)S(1)} %get-tuple-element.39), channel_id=1, source_target_pairs={{0,12},{4,8},{8,4},{12,0},{16,28},{20,24},{24,20},{28,16},{1,13},{... | collective-permute-start | bytes 393224 | tf_op jit(solution)/shard_map/ppermute | solution.py:395
  37.5 7.2 %collective-permute-start.12 = (bf16[4,128,128]{2,1,0:T(8,128)(2,1)S(1)}, bf16[4,128,128]{2,1,0:T(8,128)(2,1)S(1)}, u32[]{:S(2)}, u32[]{:S(2)}) collective-permute-start(bf16[4,128,128]{2,1,0:T(8,128)(2,1)S(1)} %get-tuple-element.39), channel_id=1, source_target_pairs={{0,8},{4,12},{8,0},{12,4},{16,24},{20,28},{24,16},{28,20},{1,9},{5... | collective-permute-start | bytes 393224 | tf_op jit(solution)/shard_map/ppermute | solution.py:395
  37.9 6.7 %collective-permute-start.11 = (bf16[4,128,128]{2,1,0:T(8,128)(2,1)S(1)}, bf16[4,128,128]{2,1,0:T(8,128)(2,1)S(1)}, u32[]{:S(2)}, u32[]{:S(2)}) collective-permute-start(bf16[4,128,128]{2,1,0:T(8,128)(2,1)S(1)} %get-tuple-element.39), channel_id=1, source_target_pairs={{0,4},{4,0},{8,12},{12,8},{16,20},{20,16},{24,28},{28,24},{1,5},{5... | collective-permute-start | bytes 393224 | tf_op jit(solution)/shard_map/ppermute | solution.py:395
  44.7 9.0 %collective-permute-start.14 = (bf16[4,128,128]{2,1,0:T(8,128)(2,1)S(1)}, bf16[4,128,128]{2,1,0:T(8,128)(2,1)S(1)}, u32[]{:S(2)}, u32[]{:S(2)}) collective-permute-start(bf16[4,128,128]{2,1,0:T(8,128)(2,1)S(1)} %swap_state.1), channel_id=1, source_target_pairs={{0,16},{4,20},{8,24},{12,28},{16,0},{20,4},{24,8},{28,12},{1,17},{... | collective-permute-start | bytes 393224 | tf_op jit(solution)/shard_map/ppermute | solution.py:462

commit v5 on v4

--- a/solution.py
+++ b/solution.py
@@ -89,7 +89,7 @@
 def mask_rows(out_grad, keep_mask, row, split, name):
     model = out_grad.shape[1]
     rows = sum(split)
-    pieces = rows // 16
+    pieces = rows // 16 if rows % 48 else rows // 48
     return pl.pallas_call(
         functools.partial(mask_body, row),
         out_shape=tuple(jax.ShapeDtypeStruct((n, model), BF16) for n in [rows] + list(split)),
@@ -270,7 +270,7 @@
 
 def query_body(places, sub, parts, place_ref, ctx_ref, key_ref, value_ref, *refs):
     prev_refs, refs = refs[:parts], refs[parts:]
-    grad_refs, (out_ref, grad) = refs[: len(places)], refs[len(places) :]
+    grad_refs, (out_ref, done_ref, grad) = refs[: len(places)], refs[len(places) :]
     gather_grad(place_ref, grad_refs, places, sub, grad)
     keep = causal(sub, False)
     rows = [slice(at, at + sub) for at in range(0, key_ref.shape[0], sub)]
@@ -283,12 +283,14 @@
         totals = [dot(grad[at, cols], state.astype(BF16), NT) for at, state in zip(rows, states)]
         scores = [jnp.where(keep, score, 0.0).astype(BF16) for score in scores]
         for at, score, total in zip(rows, scores, totals):
-            out_ref[at, cols] = total + dot(score, key_ref[at, cols], NN)
+            total = total + dot(score, key_ref[at, cols], NN)
+            out_ref[at, cols] = total
+            done_ref[at, cols] = total.astype(BF16)
 
 
 def later_body(sub, parts, place_ref, ctx_ref, query_ref, key_ref, value_ref, grad, *refs):
     near_ref, far_ref = refs[:2]
-    next_refs, (key_out, value_out) = refs[2 : 2 + parts], refs[2 + parts :]
+    next_refs, (key_out, value_out, key_done, value_done) = refs[2 : 2 + parts], refs[2 + parts :]
     place = place_ref[0]
     keep = causal(sub, True)
     rows = [slice(at, at + sub) for at in range(0, key_ref.shape[0], sub)]
@@ -307,10 +309,14 @@
             states.append(total.astype(BF16))
         scores = masked(scores)
         for at, score, state in zip(rows, scores, states):
-            key_out[at, cols] = dot(value_ref[at, cols], state, NT) + dot(score, query_ref[at, cols], NN)
+            total = dot(value_ref[at, cols], state, NT) + dot(score, query_ref[at, cols], NN)
+            key_out[at, cols] = total
+            key_done[at, cols] = total.astype(BF16)
         attn = masked(attn)
         for at, score, state in zip(rows, attn, states):
-            value_out[at, cols] = dot(key_ref[at, cols], state, NN) + dot(score, grad[at, cols], NN)
+            total = dot(key_ref[at, cols], state, NN) + dot(score, grad[at, cols], NN)
+            value_out[at, cols] = total
+            value_done[at, cols] = total.astype(BF16)
 
 
 def query_products(place, ctx, key_rows, value_rows, prevs, grads, places, sub):
@@ -320,9 +326,10 @@
         out_shape=(
             jax.ShapeDtypeStruct((tokens, width), F32),
             jax.ShapeDtypeStruct((tokens, width), BF16),
+            jax.ShapeDtypeStruct((tokens, width), BF16),
         ),
         in_specs=[smem(), smem()] + [vmem()] * (2 + len(prevs) + len(grads)),
-        out_specs=(vmem(), vmem()),
+        out_specs=(vmem(),) * 3,
         compiler_params=params(16),
         cost_estimate=cost(4 * tokens * tokens * width, 8 * tokens * width),
         name="query_products",
@@ -333,9 +340,10 @@
     tokens, width = key_rows.shape
     return pl.pallas_call(
         functools.partial(later_body, sub, len(nexts)),
-        out_shape=(jax.ShapeDtypeStruct((tokens, width), F32),) * 2,
+        out_shape=(jax.ShapeDtypeStruct((tokens, width), F32),) * 2
+        + (jax.ShapeDtypeStruct((tokens, width), BF16),) * 2,
         in_specs=[smem(), smem()] + [vmem()] * (6 + len(nexts)),
-        out_specs=(vmem(), vmem()),
+        out_specs=(vmem(),) * 4,
         compiler_params=params(16),
         cost_estimate=cost(8 * tokens * tokens * width, 10 * tokens * width),
         name="later_products",
@@ -343,51 +351,54 @@
 
 
 def end_body(sub, ctx_ref, half_ref, got_ref, key_ref, value_ref, grad_ref, *refs):
-    part_refs, out_refs, (done, sems) = refs[:3], refs[3:6], refs[6:]
+    part_refs, (out_refs, done, sems) = refs[:3], (refs[-5:-2], refs[-2], refs[-1])
     upper = ctx_ref[0] >= half_ref[0]
-    heads = got_ref.shape[0]
-    copies = []
-    for n in range(key_ref.shape[0] // sub):
-        rows = slice(n * sub, (n + 1) * sub)
-        for h in range(heads):
-            cols = head_cols(h)
-            got = got_ref[h].astype(F32)
-            down = jnp.where(upper, 0.0, got).astype(BF16)
-            up = jnp.where(upper, got, 0.0).astype(BF16)
-            adds = (
-                dot(grad_ref[rows, cols], up, NT),
-                dot(value_ref[rows, cols], down, NT),
-                dot(key_ref[rows, cols], down, NN),
-            )
-            for k in range(3):
-                done[k, rows, cols] = (part_refs[k][rows, cols] + adds[k]).astype(BF16)
-        for k in range(3):
-            copy = pltpu.make_async_copy(
-                done.at[k, pl.ds(n * sub, sub), :],
-                out_refs[k].at[pl.ds(n * sub, sub), :],
-                sems.at[k, n],
-            )
-            copy.start()
-            copies.append(copy)
-    for copy in copies:
-        copy.wait()
-
-
-def end_products(ctx, half, got, key_rows, value_rows, grad_rows, parts, sub):
+    lefts, dims = (grad_ref, value_ref, key_ref), (NT, NT, NN)
+
+    def renew(which):
+        copies = []
+        for n in range(key_ref.shape[0] // sub):
+            rows = slice(n * sub, (n + 1) * sub)
+            for k in which:
+                for h in range(got_ref.shape[0]):
+                    cols = head_cols(h)
+                    add = dot(lefts[k][rows, cols], got_ref[h], dims[k])
+                    done[k, rows, cols] = (part_refs[k][rows, cols] + add).astype(BF16)
+                copy = pltpu.make_async_copy(
+                    done.at[k, pl.ds(n * sub, sub), :],
+                    out_refs[k].at[pl.ds(n * sub, sub), :],
+                    sems.at[k, n],
+                )
+                copy.start()
+                copies.append(copy)
+        for copy in copies:
+            copy.wait()
+
+    @pl.when(upper)
+    def _():
+        renew((0,))
+
+    @pl.when(jnp.logical_not(upper))
+    def _():
+        renew((1, 2))
+
+
+def end_products(ctx, half, got, key_rows, value_rows, grad_rows, parts, dones, sub):
     tokens, width = key_rows.shape
     return pl.pallas_call(
         functools.partial(end_body, sub),
         out_shape=(jax.ShapeDtypeStruct((tokens, width), BF16),) * 3,
-        in_specs=[smem(), smem()] + [vmem()] * 7,
+        in_specs=[smem(), smem()] + [vmem()] * 7 + [hbm()] * 3,
         out_specs=(hbm(),) * 3,
         scratch_shapes=[
             pltpu.VMEM((3, tokens, width), BF16),
             pltpu.SemaphoreType.DMA((3, tokens // sub)),
         ],
+        input_output_aliases={9 + k: k for k in range(3)},
         compiler_params=params(16),
         cost_estimate=cost(6 * tokens * width * HEAD_DIM, 16 * tokens * width),
         name="end_products",
-    )(ctx, half, got, key_rows, value_rows, grad_rows, *parts)
+    )(ctx, half, got, key_rows, value_rows, grad_rows, *parts, *dones)
 
 
 def scan_states(wide, short, reverse, ties, name):
@@ -454,17 +465,18 @@
     )
 
     spots = tuple(places)
-    query_part, grad_rows = query_products(place, ctx, key_rows, value_rows, prevs, grads, spots, own_rows)
+    query_part, query_done, grad_rows = query_products(place, ctx, key_rows, value_rows, prevs, grads, spots, own_rows)
     nexts = scan_states(wide, short, True, [query_part], "next")
     nexts[-1] = after(nexts[-1], query_part)
     payload = swap_state(ctx, half, prev_sum, wide, nexts)
     size = lax.axis_size("ctx")
     got = lax.ppermute(payload, "ctx", [(i, (i + size // 2) % size) for i in range(size)])
-    key_part, value_part = later_products(
+    key_part, value_part, key_done, value_done = later_products(
         place, ctx, query_rows, key_rows, value_rows, grad_rows, states[0], far, nexts, own_rows
     )
     parts = (query_part, key_part, value_part)
-    return end_products(ctx, half, got, key_rows, value_rows, grad_rows, parts, own_rows)
+    dones = (query_done, key_done, value_done)
+    return end_products(ctx, half, got, key_rows, value_rows, grad_rows, parts, dones, own_rows)
 
 
 def solution(mesh):

time: 56.2 us -> 55.5 us (0.988)
  waiting for transfers between devices: 11.8 us -> 9.72 us
  Pallas kernels: 26.2 us -> 27.6 us
    ppermute x1, waiting for transfers between devices: 3.28 us -> 2.19 us  [per_device(): lax.ppermute(payload, 'ctx', [(i, (i + size // 2) % size) for i in range(...]
    pallas_call x1, Pallas kernels: 3.1 us -> 4.19 us  [later_products(): pl.pallas_call(functools.partial(later_body, sub, len(nexts)), out_shape=...]
    pallas_call x1, Pallas kernels: 2.93 us -> 3.91 us  [query_products(): pl.pallas_call(functools.partial(query_body, places, sub, len(prevs)), ou...]
    ppermute x6, waiting for transfers between devices: 3.53 us -> 2.56 us  [scan_states(): send = lambda payload, pairs: lax.ppermute(payload, 'ctx', pairs)]
  transfers between devices with their start and end apart: 15 -> 15, of which waited for: 5 -> 4; matrix products, arithmetic and copies ran while one was open for 0% -> 0% of each run, Pallas kernels for 34% -> 38%
where the time goes in v5:
time: 55.5 us; the launch traced here: 55.3 us
  Pallas kernels  27.6 us (50%)
  starting transfers between devices  14.1 us (25%)
  waiting for transfers between devices  9.72 us (18%)
  local copies, waits for them, and re-layouts  3 us (5%)
  between operations  0.85 us (2%)
    pallas_call x3, Pallas kernels, grad_part(): pl.pallas_call(functools.partial(grad_body, pieces, sub, len(befores), la...  10.6 us
    ppermute x6, starting transfers between devices, scan_states(): send = lambda payload, pairs: lax.ppermute(payload, 'ctx', pairs)  7.19 us
    ppermute x8, waiting for transfers between devices, swap(): return lax.ppermute(array, 'head', [(i, i ^ distance) for i in range(size)])  4.98 us
    pallas_call x2, Pallas kernels, mask_rows(): pl.pallas_call(functools.partial(mask_body, row), out_shape=tuple((jax.Sh...  4.91 us
    ppermute x8, starting transfers between devices, swap(): return lax.ppermute(array, 'head', [(i, i ^ distance) for i in range(size)])  4.31 us
    pallas_call x1, Pallas kernels, later_products(): pl.pallas_call(functools.partial(later_body, sub, len(nexts)), out_shape=...  4.19 us
    pallas_call x1, Pallas kernels, query_products(): pl.pallas_call(functools.partial(query_body, places, sub, len(prevs)), ou...  3.91 us
    unnamed x30, local copies, waits for them, and re-layouts  3 us
  transfers between devices with their start and end apart: 15, of which 4 were waited for; matrix products, arithmetic and copies ran while one was open for 0% of the time, Pallas kernels for 38%

profile of v5, /device:TPU:0, one launch (start us, length us, event | category | flops | bytes accessed | tf_op | source)
XLA Modules:
  0.0 55.3 jit_solution(15382356824545106257)
XLA Ops:
  0.6 2.5 %mask_first.1 = (bf16[144,2048]{1,0:T(8,128)(2,1)}, bf16[80,2048]{1,0:T(8,128)(2,1)}, bf16[64,2048]{1,0:T(8,128)(2,1)}) custom-call(bf16[256,2048]{1,0:T(8,128)(2,1)} %grad_ref.3, s32[256,2048]{1,0:T(8,128)} %keep_ref.3), custom_call_target="tpu_custom_call" | custom-call | flops 1 | bytes 1 | tf_op jit(solution)/shard_map/mask_first/pallas_call | solution.py:93
  3.2 3.0 %collective-permute-start.7 = (bf16[144,2048]{1,0:T(8,128)(2,1)}, bf16[144,2048]{1,0:T(8,128)(2,1)}, u32[]{:S(2)}, u32[]{:S(2)}) collective-permute-start(bf16[144,2048]{1,0:T(8,128)(2,1)} %get-tuple-element.31.refs_3_), channel_id=1, source_target_pairs={{0,2},{1,3},{2,0},{3,1},{4,6},{5,7},{6,4},{7,5},{8,10},{9,11},{10,... | collective-permute-start | bytes 1769480 | tf_op jit(solution)/shard_map/ppermute | solution.py:430
  6.2 2.4 %mask_last.1 = (bf16[112,2048]{1,0:T(8,128)(2,1)}, bf16[64,2048]{1,0:T(8,128)(2,1)}, bf16[48,2048]{1,0:T(8,128)(2,1)}) custom-call(bf16[256,2048]{1,0:T(8,128)(2,1)} %grad_ref.3, s32[256,2048]{1,0:T(8,128)} %keep_ref.3), custom_call_target="tpu_custom_call" | custom-call | flops 1 | bytes 1 | tf_op jit(solution)/shard_map/mask_last/pallas_call | solution.py:93
  8.7 0.5 collective-permute-start.3
  9.2 0.1 collective-permute-start.5
  9.3 0.4 collective-permute-start.4
  9.7 0.6 %collective-permute-done.6.refs_8_ = bf16[48,2048]{1,0:T(8,128)(2,1)S(1)} collective-permute-done((bf16[48,2048]{1,0:T(8,128)(2,1)}, bf16[48,2048]{1,0:T(8,128)(2,1)S(1)}, u32[]{:S(2)}, u32[]{:S(2)}) %collective-permute-start.6) | collective-permute-done | bytes 196640 | tf_op jit(solution)/shard_map/ppermute | solution.py:430
  10.3 0.7 %copy-done.12 = bf16[48,2048]{1,0:T(8,128)(2,1)} copy-done((bf16[48,2048]{1,0:T(8,128)(2,1)}, bf16[48,2048]{1,0:T(8,128)(2,1)S(1)}, u32[]{:S(2)}) %copy-start.12) | copy-done | bytes 196632
  11.0 0.2 collective-permute-start.9
  11.2 1.1 %kv_state.1 = (f32[4,128,128]{2,1,0:T(8,128)S(1)}, bf16[4,128,128]{2,1,0:T(8,128)(2,1)}) custom-call(bf16[1024,512]{1,0:T(8,128)(2,1)S(1)} %copy-done.2, bf16[1024,512]{1,0:T(8,128)(2,1)S(1)} %copy-done.4), custom_call_target="tpu_custom_call" | custom-call | flops 1 | bytes 1 | tf_op jit(solution)/shard_map/kv_state/pallas_call | solution.py:120
  12.3 0.7 %copy-done.11 = bf16[64,2048]{1,0:T(8,128)(2,1)} copy-done((bf16[64,2048]{1,0:T(8,128)(2,1)}, bf16[64,2048]{1,0:T(8,128)(2,1)S(1)}, u32[]{:S(2)}) %copy-start.11) | copy-done | bytes 262168
  13.0 3.1 %collective-permute-start.2 = (bf16[4,128,128]{2,1,0:T(8,128)(2,1)}, bf16[4,128,128]{2,1,0:T(8,128)(2,1)S(1)}, u32[]{:S(2)}, u32[]{:S(2)}) collective-permute-start(bf16[4,128,128]{2,1,0:T(8,128)(2,1)} %get-tuple-element.30), channel_id=1, source_target_pairs={{0,12},{4,8},{8,4},{12,0},{16,28},{20,24},{24,20},{28,16},{1,13},{... | collective-permute-start | bytes 393224 | tf_op jit(solution)/shard_map/ppermute | solution.py:406
  16.1 0.5 collective-permute-start.1
  16.6 0.1 collective-permute-start
  16.7 5.9 %grad_near.1 = (bf16[512,512]{1,0:T(8,128)(2,1)}, f32[2,4,128,128]{3,2,1,0:T(8,128)}) custom-call(s32[1]{0:T(128)} %bitcast.1.refs_0_.place_ref, bf16[1024,512]{1,0:T(8,128)(2,1)} %query_ref.1, bf16[512,2048]{1,0:T(8,128)(2,1)} %refs_2_.5, bf16[144,2048]{1,0:T(8,128)(2,1)} %get-tuple-element.31.refs_3_, bf16[112,2048]{1,0:T(8,128)(2,1)} %get-tuple-element.32.refs_4_, ...), custom_call_target="tpu_custom_call" | custom-call | flops 1 | bytes 1 | tf_op jit(solution)/shard_map/grad_near/pallas_call | solution.py:230
  22.6 0.6 %copy-done.7 = bf16[4,128,128]{2,1,0:T(8,128)(2,1)} copy-done((bf16[4,128,128]{2,1,0:T(8,128)(2,1)}, bf16[4,128,128]{2,1,0:T(8,128)(2,1)S(1)}, u32[]{:S(2)}) %copy-start.7) | copy-done | bytes 131096
  23.3 0.9 %copy-done.8 = bf16[4,128,128]{2,1,0:T(8,128)(2,1)S(1)} copy-done((bf16[4,128,128]{2,1,0:T(8,128)(2,1)S(1)}, bf16[4,128,128]{2,1,0:T(8,128)(2,1)}, u32[]{:S(2)}) %copy-start.8) | copy-done | bytes 131096
  24.2 1.0 %prev_sum.1.prev_ref = bf16[4,128,128]{2,1,0:T(8,128)(2,1)S(1)} custom-call(f32[4,128,128]{2,1,0:T(8,128)S(1)} %get-tuple-element.29.wide_ref, bf16[4,128,128]{2,1,0:T(8,128)(2,1)} %collective-permute-done.refs_0_, bf16[4,128,128]{2,1,0:T(8,128)(2,1)} %collective-permute-done.1.refs_1_, bf16[4,128,128]{2,1,0:T(8,128)(2,1)S(1)} %copy-done.8), custom_call_target="tpu_custom_call" | custom-call | flops 1 | bytes 1 | tf_op jit(solution)/shard_map/prev_sum/pallas_call | solution.py:144
  25.2 0.1 collective-permute-start.8
  25.3 4.3 %collective-permute-done.9.refs_5_ = bf16[112,2048]{1,0:T(8,128)(2,1)} collective-permute-done((bf16[112,2048]{1,0:T(8,128)(2,1)}, bf16[112,2048]{1,0:T(8,128)(2,1)}, u32[]{:S(2)}, u32[]{:S(2)}) %collective-permute-start.9) | collective-permute-done | bytes 458784 | tf_op jit(solution)/shard_map/ppermute | solution.py:430
  29.7 2.4 %grad_far.1 = (bf16[288,512]{1,0:T(8,128)(2,1)S(1)}, f32[2,4,128,128]{3,2,1,0:T(8,128)S(1)}) custom-call(s32[1]{0:T(128)} %bitcast.1.refs_0_.place_ref, bf16[1024,512]{1,0:T(8,128)(2,1)S(1)} %copy-done.1, bf16[512,2048]{1,0:T(8,128)(2,1)S(1)} %copy-done, bf16[144,2048]{1,0:T(8,128)(2,1)} %collective-permute-done.7.refs_3_, ...), custom_call_target="tpu_custom_call" | custom-call | flops 1 | bytes 1 | tf_op jit(solution)/shard_map/grad_far/pallas_call | solution.py:230
  32.2 2.3 %grad_last.1 = (bf16[224,512]{1,0:T(8,128)(2,1)S(1)}, f32[2,4,128,128]{3,2,1,0:T(8,128)S(1)}, f32[4,128,128]{2,1,0:T(8,128)S(1)}, bf16[4,128,128]{2,1,0:T(8,128)(2,1)S(1)}) custom-call(s32[1]{0:T(128)} %bitcast.1.refs_0_.place_ref, bf16[1024,512]{1,0:T(8,128)(2,1)S(1)} %copy-done.1, bf16[512,2048]{1,0:T(8,128)(2,1)S(1)} %copy-done, ...), custom_call_target="tpu_custom_call" | custom-call | flops 1 | bytes 1 | tf_op jit(solution)/shard_map/grad_last/pallas_call | solution.py:230
  34.5 2.8 %collective-permute-start.13 = (bf16[4,128,128]{2,1,0:T(8,128)(2,1)S(1)}, bf16[4,128,128]{2,1,0:T(8,128)(2,1)S(1)}, u32[]{:S(2)}, u32[]{:S(2)}) collective-permute-start(bf16[4,128,128]{2,1,0:T(8,128)(2,1)S(1)} %get-tuple-element.42), channel_id=1, source_target_pairs={{0,12},{4,8},{8,4},{12,0},{16,28},{20,24},{24,20},{28,16},{1,13},{... | collective-permute-start | bytes 393224 | tf_op jit(solution)/shard_map/ppermute | solution.py:406
  37.3 0.5 collective-permute-start.12
  37.8 0.3 collective-permute-start.11
  38.0 3.9 %query_products.1 = (f32[1024,512]{1,0:T(8,128)S(1)}, bf16[1024,512]{1,0:T(8,128)(2,1)}, bf16[1024,512]{1,0:T(8,128)(2,1)S(1)}) custom-call(s32[1]{0:T(128)} %bitcast.1.refs_0_.place_ref, s32[1]{0:T(128)} %bitcast.ctx_ref, bf16[1024,512]{1,0:T(8,128)(2,1)S(1)} %copy-done.3, bf16[1024,512]{1,0:T(8,128)(2,1)S(1)} %copy-done.5, ...), custom_call_target="tpu_custom_call" | custom-call | flops 2147483648 | bytes 4194304 | tf_op jit(solution)/shard_map/query_products/pallas_call | solution.py:324
  42.0 2.5 %collective-permute-done.12.refs_1_.refs_3_ = bf16[4,128,128]{2,1,0:T(8,128)(2,1)S(1)} collective-permute-done((bf16[4,128,128]{2,1,0:T(8,128)(2,1)S(1)}, bf16[4,128,128]{2,1,0:T(8,128)(2,1)S(1)}, u32[]{:S(2)}, u32[]{:S(2)}) %collective-permute-start.12) | collective-permute-done | bytes 131104 | tf_op jit(solution)/shard_map/ppermute | solution.py:406
  44.5 0.1 swap_state.1
  44.6 2.6 %collective-permute-start.14 = (bf16[4,128,128]{2,1,0:T(8,128)(2,1)S(1)}, bf16[4,128,128]{2,1,0:T(8,128)(2,1)S(1)}, u32[]{:S(2)}, u32[]{:S(2)}) collective-permute-start(bf16[4,128,128]{2,1,0:T(8,128)(2,1)S(1)} %swap_state.1), channel_id=1, source_target_pairs={{0,16},{4,20},{8,24},{12,28},{16,0},{20,4},{24,8},{28,12},{1,17},{... | collective-permute-start | bytes 393224 | tf_op jit(solution)/shard_map/ppermute | solution.py:473
  47.2 4.2 %later_products.1 = (f32[1024,512]{1,0:T(8,128)S(1)}, f32[1024,512]{1,0:T(8,128)S(1)}, bf16[1024,512]{1,0:T(8,128)(2,1)}, bf16[1024,512]{1,0:T(8,128)(2,1)}) custom-call(s32[1]{0:T(128)} %bitcast.1.refs_0_.place_ref, s32[1]{0:T(128)} %bitcast.ctx_ref, bf16[1024,512]{1,0:T(8,128)(2,1)S(1)} %copy-done.1, bf16[1024,512]{1,0:T(8,128)(2,1)S(1)} %copy-done.3, ...), custom_call_target="tpu_custom_call" | custom-call | flops 4294967296 | bytes 5242880 | tf_op jit(solution)/shard_map/later_products/pallas_call | solution.py:341
  51.4 2.2 %collective-permute-done.14.got_ref = bf16[4,128,128]{2,1,0:T(8,128)(2,1)S(1)} collective-permute-done((bf16[4,128,128]{2,1,0:T(8,128)(2,1)S(1)}, bf16[4,128,128]{2,1,0:T(8,128)(2,1)S(1)}, u32[]{:S(2)}, u32[]{:S(2)}) %collective-permute-start.14) | collective-permute-done | bytes 131104 | tf_op jit(solution)/shard_map/ppermute | solution.py:473
  53.6 1.7 %end_products.1 = (bf16[1024,512]{1,0:T(8,128)(2,1)}, bf16[1024,512]{1,0:T(8,128)(2,1)}, bf16[1024,512]{1,0:T(8,128)(2,1)}) custom-call(s32[1]{0:T(128)} %bitcast.ctx_ref, s32[1]{0:T(128)} %constant.9.clone.1.half_ref, bf16[4,128,128]{2,1,0:T(8,128)(2,1)S(1)} %collective-permute-done.14.got_ref, ...), custom_call_target="tpu_custom_call", output_to_operand_aliasing={{0}: (9, {}), {1}: (10, {}), {2}: (11, {})} | custom-call | flops 402653184 | bytes 8388608 | tf_op jit(solution)/shard_map/end_products/pallas_call | solution.py:388
  (39 shorter events, 0.2 us)
Async XLA Ops:
  3.1 5.6 %copy-start.13 = (bf16[80,2048]{1,0:T(8,128)(2,1)S(1)}, bf16[80,2048]{1,0:T(8,128)(2,1)}, u32[]{:S(2)}) copy-start(bf16[80,2048]{1,0:T(8,128)(2,1)} %get-tuple-element.33) | copy-start | bytes 983044
  3.1 6.1 %copy-start.14 = (bf16[64,2048]{1,0:T(8,128)(2,1)S(1)}, bf16[64,2048]{1,0:T(8,128)(2,1)}, u32[]{:S(2)}) copy-start(bf16[64,2048]{1,0:T(8,128)(2,1)} %get-tuple-element.34) | copy-start | bytes 786436
  3.2 8.0 %copy-start.2 = (bf16[1024,512]{1,0:T(8,128)(2,1)S(1)}, bf16[1024,512]{1,0:T(8,128)(2,1)}, u32[]{:S(2)}) copy-start(bf16[1024,512]{1,0:T(8,128)(2,1)} %key_ref.7) | copy-start | bytes 3145732
  3.2 8.0 %copy-start.4 = (bf16[1024,512]{1,0:T(8,128)(2,1)S(1)}, bf16[1024,512]{1,0:T(8,128)(2,1)}, u32[]{:S(2)}) copy-start(bf16[1024,512]{1,0:T(8,128)(2,1)} %value_ref.7) | copy-start | bytes 3145732
  3.2 22.1 %collective-permute-start.7 = (bf16[144,2048]{1,0:T(8,128)(2,1)}, bf16[144,2048]{1,0:T(8,128)(2,1)}, u32[]{:S(2)}, u32[]{:S(2)}) collective-permute-start(bf16[144,2048]{1,0:T(8,128)(2,1)} %get-tuple-element.31.refs_3_), channel_id=1, source_target_pairs={{0,2},{1,3},{2,0},{3,1},{4,6},{5,7},{6,4},{7,5},{8,10},{9,11},{10,... | collective-permute-start | bytes 1769480 | tf_op jit(solution)/shard_map/ppermute | solution.py:430
  8.6 1.7 %collective-permute-start.6 = (bf16[48,2048]{1,0:T(8,128)(2,1)}, bf16[48,2048]{1,0:T(8,128)(2,1)S(1)}, u32[]{:S(2)}, u32[]{:S(2)}) collective-permute-start(bf16[48,2048]{1,0:T(8,128)(2,1)} %get-tuple-element.36), channel_id=1, source_target_pairs={{0,1},{1,0},{2,3},{3,2},{4,5},{5,4},{6,7},{7,6},{8,9},{9,8},{10,11... | collective-permute-start | bytes 589832 | tf_op jit(solution)/shard_map/ppermute | solution.py:430
  8.7 7.9 %collective-permute-start.3 = (bf16[80,2048]{1,0:T(8,128)(2,1)S(1)}, bf16[80,2048]{1,0:T(8,128)(2,1)}, u32[]{:S(2)}, u32[]{:S(2)}) collective-permute-start(bf16[80,2048]{1,0:T(8,128)(2,1)S(1)} %copy-done.13), channel_id=1, source_target_pairs={{0,1},{1,0},{2,3},{3,2},{4,5},{5,4},{6,7},{7,6},{8,9},{9,8},{10,11... | collective-permute-start | bytes 983048 | tf_op jit(solution)/shard_map/ppermute | solution.py:430
  9.2 3.1 %collective-permute-start.5 = (bf16[64,2048]{1,0:T(8,128)(2,1)}, bf16[64,2048]{1,0:T(8,128)(2,1)S(1)}, u32[]{:S(2)}, u32[]{:S(2)}) collective-permute-start(bf16[64,2048]{1,0:T(8,128)(2,1)} %get-tuple-element.35), channel_id=1, source_target_pairs={{0,1},{1,0},{2,3},{3,2},{4,5},{5,4},{6,7},{7,6},{8,9},{9,8},{10,11... | collective-permute-start | bytes 786440 | tf_op jit(solution)/shard_map/ppermute | solution.py:430
  9.3 6.8 %collective-permute-start.4 = (bf16[64,2048]{1,0:T(8,128)(2,1)S(1)}, bf16[64,2048]{1,0:T(8,128)(2,1)}, u32[]{:S(2)}, u32[]{:S(2)}) collective-permute-start(bf16[64,2048]{1,0:T(8,128)(2,1)S(1)} %copy-done.14), channel_id=1, source_target_pairs={{0,1},{1,0},{2,3},{3,2},{4,5},{5,4},{6,7},{7,6},{8,9},{9,8},{10,11... | collective-permute-start | bytes 786440 | tf_op jit(solution)/shard_map/ppermute | solution.py:430
  10.3 0.7 %copy-start.12 = (bf16[48,2048]{1,0:T(8,128)(2,1)}, bf16[48,2048]{1,0:T(8,128)(2,1)S(1)}, u32[]{:S(2)}) copy-start(bf16[48,2048]{1,0:T(8,128)(2,1)S(1)} %collective-permute-done.6.refs_8_) | copy-start | bytes 589828
  11.0 18.6 %collective-permute-start.9 = (bf16[112,2048]{1,0:T(8,128)(2,1)}, bf16[112,2048]{1,0:T(8,128)(2,1)}, u32[]{:S(2)}, u32[]{:S(2)}) collective-permute-start(bf16[112,2048]{1,0:T(8,128)(2,1)} %get-tuple-element.32.refs_4_), channel_id=1, source_target_pairs={{0,2},{1,3},{2,0},{3,1},{4,6},{5,7},{6,4},{7,5},{8,10},{9,11},{10,... | collective-permute-start | bytes 1376264 | tf_op jit(solution)/shard_map/ppermute | solution.py:430
  12.3 0.7 %copy-start.11 = (bf16[64,2048]{1,0:T(8,128)(2,1)}, bf16[64,2048]{1,0:T(8,128)(2,1)S(1)}, u32[]{:S(2)}) copy-start(bf16[64,2048]{1,0:T(8,128)(2,1)S(1)} %collective-permute-done.5.refs_7_) | copy-start | bytes 786436
  13.0 9.6 %collective-permute-start.2 = (bf16[4,128,128]{2,1,0:T(8,128)(2,1)}, bf16[4,128,128]{2,1,0:T(8,128)(2,1)S(1)}, u32[]{:S(2)}, u32[]{:S(2)}) collective-permute-start(bf16[4,128,128]{2,1,0:T(8,128)(2,1)} %get-tuple-element.30), channel_id=1, source_target_pairs={{0,12},{4,8},{8,4},{12,0},{16,28},{20,24},{24,20},{28,16},{1,13},{... | collective-permute-start | bytes 393224 | tf_op jit(solution)/shard_map/ppermute | solution.py:406
  16.1 7.2 %collective-permute-start.1 = (bf16[4,128,128]{2,1,0:T(8,128)(2,1)}, bf16[4,128,128]{2,1,0:T(8,128)(2,1)}, u32[]{:S(2)}, u32[]{:S(2)}) collective-permute-start(bf16[4,128,128]{2,1,0:T(8,128)(2,1)} %get-tuple-element.30), channel_id=1, source_target_pairs={{0,8},{4,12},{8,0},{12,4},{16,24},{20,28},{24,16},{28,20},{1,9},{5... | collective-permute-start | bytes 393224 | tf_op jit(solution)/shard_map/ppermute | solution.py:406
  16.6 6.7 %collective-permute-start = (bf16[4,128,128]{2,1,0:T(8,128)(2,1)}, bf16[4,128,128]{2,1,0:T(8,128)(2,1)}, u32[]{:S(2)}, u32[]{:S(2)}) collective-permute-start(bf16[4,128,128]{2,1,0:T(8,128)(2,1)} %get-tuple-element.30), channel_id=1, source_target_pairs={{0,4},{4,0},{8,12},{12,8},{16,20},{20,16},{24,28},{28,24},{1,5},{5... | collective-permute-start | bytes 393224 | tf_op jit(solution)/shard_map/ppermute | solution.py:406
  16.7 13.0 %copy-start = (bf16[512,2048]{1,0:T(8,128)(2,1)S(1)}, bf16[512,2048]{1,0:T(8,128)(2,1)}, u32[]{:S(2)}) copy-start(bf16[512,2048]{1,0:T(8,128)(2,1)} %refs_2_.5) | copy-start | bytes 6291460
  16.7 13.0 %copy-start.1 = (bf16[1024,512]{1,0:T(8,128)(2,1)S(1)}, bf16[1024,512]{1,0:T(8,128)(2,1)}, u32[]{:S(2)}) copy-start(bf16[1024,512]{1,0:T(8,128)(2,1)} %query_ref.1) | copy-start | bytes 3145732
  22.6 0.7 %copy-start.7 = (bf16[4,128,128]{2,1,0:T(8,128)(2,1)}, bf16[4,128,128]{2,1,0:T(8,128)(2,1)S(1)}, u32[]{:S(2)}) copy-start(bf16[4,128,128]{2,1,0:T(8,128)(2,1)S(1)} %collective-permute-done.2.refs_2_) | copy-start | bytes 393220
  23.3 0.9 %copy-start.8 = (bf16[4,128,128]{2,1,0:T(8,128)(2,1)S(1)}, bf16[4,128,128]{2,1,0:T(8,128)(2,1)}, u32[]{:S(2)}) copy-start(bf16[4,128,128]{2,1,0:T(8,128)(2,1)} %copy-done.7) | copy-start | bytes 393220
  25.2 4.4 %collective-permute-start.8 = (bf16[144,2048]{1,0:T(8,128)(2,1)}, bf16[144,2048]{1,0:T(8,128)(2,1)}, u32[]{:S(2)}, u32[]{:S(2)}) collective-permute-start(bf16[144,2048]{1,0:T(8,128)(2,1)} %collective-permute-done.7.refs_3_), channel_id=1, source_target_pairs={{0,1},{1,0},{2,3},{3,2},{4,5},{5,4},{6,7},{7,6},{8,9},{9,8},{10,11... | collective-permute-start | bytes 1769480 | tf_op jit(solution)/shard_map/ppermute | solution.py:430
  29.7 2.4 %collective-permute-start.10 = (bf16[112,2048]{1,0:T(8,128)(2,1)}, bf16[112,2048]{1,0:T(8,128)(2,1)}, u32[]{:S(2)}, u32[]{:S(2)}) collective-permute-start(bf16[112,2048]{1,0:T(8,128)(2,1)} %collective-permute-done.9.refs_5_), channel_id=1, source_target_pairs={{0,1},{1,0},{2,3},{3,2},{4,5},{5,4},{6,7},{7,6},{8,9},{9,8},{10,11... | collective-permute-start | bytes 1376264 | tf_op jit(solution)/shard_map/ppermute | solution.py:430
  29.7 2.4 %copy-start.6 = (f32[2,4,128,128]{3,2,1,0:T(8,128)S(1)}, f32[2,4,128,128]{3,2,1,0:T(8,128)}, u32[]{:S(2)}) copy-start(f32[2,4,128,128]{3,2,1,0:T(8,128)} %get-tuple-element.37.refs_4_.refs_0_) | copy-start | bytes 1572868
  32.1 5.9 %copy-start.3 = (bf16[1024,512]{1,0:T(8,128)(2,1)S(1)}, bf16[1024,512]{1,0:T(8,128)(2,1)}, u32[]{:S(2)}) copy-start(bf16[1024,512]{1,0:T(8,128)(2,1)} %key_ref.7) | copy-start | bytes 3145732
  32.1 5.9 %copy-start.5 = (bf16[1024,512]{1,0:T(8,128)(2,1)S(1)}, bf16[1024,512]{1,0:T(8,128)(2,1)}, u32[]{:S(2)}) copy-start(bf16[1024,512]{1,0:T(8,128)(2,1)} %value_ref.7) | copy-start | bytes 3145732
  32.1 5.9 %copy-start.9 = (bf16[4,128,128]{2,1,0:T(8,128)(2,1)S(1)}, bf16[4,128,128]{2,1,0:T(8,128)(2,1)}, u32[]{:S(2)}) copy-start(bf16[4,128,128]{2,1,0:T(8,128)(2,1)} %copy-done.7) | copy-start | bytes 393220
  32.1 5.9 %copy-start.10 = (bf16[512,512]{1,0:T(8,128)(2,1)S(1)}, bf16[512,512]{1,0:T(8,128)(2,1)}, u32[]{:S(2)}) copy-start(bf16[512,512]{1,0:T(8,128)(2,1)} %get-tuple-element.43.refs_3_) | copy-start | bytes 1572868
  34.5 7.5 %collective-permute-start.13 = (bf16[4,128,128]{2,1,0:T(8,128)(2,1)S(1)}, bf16[4,128,128]{2,1,0:T(8,128)(2,1)S(1)}, u32[]{:S(2)}, u32[]{:S(2)}) collective-permute-start(bf16[4,128,128]{2,1,0:T(8,128)(2,1)S(1)} %get-tuple-element.42), channel_id=1, source_target_pairs={{0,12},{4,8},{8,4},{12,0},{16,28},{20,24},{24,20},{28,16},{1,13},{... | collective-permute-start | bytes 393224 | tf_op jit(solution)/shard_map/ppermute | solution.py:406
  37.3 7.2 %collective-permute-start.12 = (bf16[4,128,128]{2,1,0:T(8,128)(2,1)S(1)}, bf16[4,128,128]{2,1,0:T(8,128)(2,1)S(1)}, u32[]{:S(2)}, u32[]{:S(2)}) collective-permute-start(bf16[4,128,128]{2,1,0:T(8,128)(2,1)S(1)} %get-tuple-element.42), channel_id=1, source_target_pairs={{0,8},{4,12},{8,0},{12,4},{16,24},{20,28},{24,16},{28,20},{1,9},{5... | collective-permute-start | bytes 393224 | tf_op jit(solution)/shard_map/ppermute | solution.py:406
  37.8 6.7 %collective-permute-start.11 = (bf16[4,128,128]{2,1,0:T(8,128)(2,1)S(1)}, bf16[4,128,128]{2,1,0:T(8,128)(2,1)S(1)}, u32[]{:S(2)}, u32[]{:S(2)}) collective-permute-start(bf16[4,128,128]{2,1,0:T(8,128)(2,1)S(1)} %get-tuple-element.42), channel_id=1, source_target_pairs={{0,4},{4,0},{8,12},{12,8},{16,20},{20,16},{24,28},{28,24},{1,5},{5... | collective-permute-start | bytes 393224 | tf_op jit(solution)/shard_map/ppermute | solution.py:406
  44.6 9.0 %collective-permute-start.14 = (bf16[4,128,128]{2,1,0:T(8,128)(2,1)S(1)}, bf16[4,128,128]{2,1,0:T(8,128)(2,1)S(1)}, u32[]{:S(2)}, u32[]{:S(2)}) collective-permute-start(bf16[4,128,128]{2,1,0:T(8,128)(2,1)S(1)} %swap_state.1), channel_id=1, source_target_pairs={{0,16},{4,20},{8,24},{12,28},{16,0},{20,4},{24,8},{28,12},{1,17},{... | collective-permute-start | bytes 393224 | tf_op jit(solution)/shard_map/ppermute | solution.py:473

commit v6 on v5

--- a/solution.py
+++ b/solution.py
@@ -65,25 +65,34 @@
 
 
 def mask_body(row, grad_ref, keep_ref, *refs):
-    out_refs, (grad, keep, grad_sems, keep_sems) = refs[:-4], refs[-4:]
+    out_refs, (grad, keep, masked, grad_sems, keep_sems, out_sems) = refs[:-6], refs[-6:]
     rows = grad.shape[0]
     pieces = keep_sems.shape[0]
     size = rows // pieces
     keep_copies = fetch(keep_ref, keep, keep_sems, row, rows, pieces)
     grad_copies = fetch(grad_ref, grad, grad_sems, row, rows, pieces)
+    copies = []
+
+    def send(at, count, target):
+        copy = pltpu.make_async_copy(masked.at[pl.ds(at, count), :], target, out_sems.at[len(copies)])
+        copy.start()
+        copies.append(copy)
+
+    waiting, at = [], 0
+    for ref in out_refs[1:]:
+        waiting.append((at, ref))
+        at += ref.shape[0]
     for n in range(pieces):
         keep_copies[n].wait()
         grad_copies[n].wait()
         low, high = n * size, (n + 1) * size
-        value = masked_rows(grad[low:high, :], keep[low:high, :])
-        out_refs[0][low:high, :] = value
-        at = 0
-        for ref in out_refs[1:]:
-            end = at + ref.shape[0]
-            top, bottom = max(low, at), min(high, end)
-            if top < bottom:
-                ref[top - at : bottom - at, :] = value[top - low : bottom - low, :]
-            at = end
+        masked[low:high, :] = masked_rows(grad[low:high, :], keep[low:high, :])
+        send(low, size, out_refs[0].at[pl.ds(low, size), :])
+        while waiting and waiting[0][0] + waiting[0][1].shape[0] <= high:
+            at, ref = waiting.pop(0)
+            send(at, ref.shape[0], ref)
+    for copy in copies:
+        copy.wait()
 
 
 def mask_rows(out_grad, keep_mask, row, split, name):
@@ -94,12 +103,14 @@
         functools.partial(mask_body, row),
         out_shape=tuple(jax.ShapeDtypeStruct((n, model), BF16) for n in [rows] + list(split)),
         in_specs=[hbm(), hbm()],
-        out_specs=(vmem(),) * (1 + len(split)),
+        out_specs=(hbm(),) * (1 + len(split)),
         scratch_shapes=[
             pltpu.VMEM((rows, model), BF16),
             pltpu.VMEM((rows, model), jnp.int32),
+            pltpu.VMEM((rows, model), BF16),
             pltpu.SemaphoreType.DMA((pieces,)),
             pltpu.SemaphoreType.DMA((pieces,)),
+            pltpu.SemaphoreType.DMA((pieces + len(split),)),
         ],
         compiler_params=params(56),
         cost_estimate=cost(1, 1),

time: 55.5 us -> 55.4 us (level)
  no operation moved by 1% of the time
where the time goes in v6:
time: 55.4 us; the launch traced here: 55.1 us
  Pallas kernels  27.3 us (49%)
  starting transfers between devices  14.2 us (26%)
  waiting for transfers between devices  9.86 us (18%)
  local copies, waits for them, and re-layouts  3 us (5%)
  between operations  0.85 us (2%)
    pallas_call x3, Pallas kernels, grad_part(): pl.pallas_call(functools.partial(grad_body, pieces, sub, len(befores), la...  10.6 us
    ppermute x6, starting transfers between devices, scan_states(): send = lambda payload, pairs: lax.ppermute(payload, 'ctx', pairs)  7.19 us
    ppermute x8, waiting for transfers between devices, swap(): return lax.ppermute(array, 'head', [(i, i ^ distance) for i in range(size)])  5.1 us
    pallas_call x2, Pallas kernels, mask_rows(): pl.pallas_call(functools.partial(mask_body, row), out_shape=tuple((jax.Sh...  4.65 us
    ppermute x8, starting transfers between devices, swap(): return lax.ppermute(array, 'head', [(i, i ^ distance) for i in range(size)])  4.31 us
    pallas_call x1, Pallas kernels, later_products(): pl.pallas_call(functools.partial(later_body, sub, len(nexts)), out_shape=...  4.19 us
    pallas_call x1, Pallas kernels, query_products(): pl.pallas_call(functools.partial(query_body, places, sub, len(prevs)), ou...  3.91 us
    unnamed x30, local copies, waits for them, and re-layouts  3 us
  transfers between devices with their start and end apart: 15, of which 4 were waited for; matrix products, arithmetic and copies ran while one was open for 0% of the time, Pallas kernels for 38%

profile of v6, /device:TPU:0, one launch (start us, length us, event | category | flops | bytes accessed | tf_op | source)
XLA Modules:
  0.0 55.1 jit_solution(10030984792765767411)
XLA Ops:
  0.6 2.4 %mask_first.1 = (bf16[144,2048]{1,0:T(8,128)(2,1)}, bf16[80,2048]{1,0:T(8,128)(2,1)}, bf16[64,2048]{1,0:T(8,128)(2,1)}) custom-call(bf16[256,2048]{1,0:T(8,128)(2,1)} %grad_ref.3, s32[256,2048]{1,0:T(8,128)} %keep_ref.3), custom_call_target="tpu_custom_call" | custom-call | flops 1 | bytes 1 | tf_op jit(solution)/shard_map/mask_first/pallas_call | solution.py:102
  3.0 3.0 %collective-permute-start.7 = (bf16[144,2048]{1,0:T(8,128)(2,1)}, bf16[144,2048]{1,0:T(8,128)(2,1)}, u32[]{:S(2)}, u32[]{:S(2)}) collective-permute-start(bf16[144,2048]{1,0:T(8,128)(2,1)} %get-tuple-element.31.refs_3_), channel_id=1, source_target_pairs={{0,2},{1,3},{2,0},{3,1},{4,6},{5,7},{6,4},{7,5},{8,10},{9,11},{10,... | collective-permute-start | bytes 1769480 | tf_op jit(solution)/shard_map/ppermute | solution.py:441
  6.0 2.3 %mask_last.1 = (bf16[112,2048]{1,0:T(8,128)(2,1)}, bf16[64,2048]{1,0:T(8,128)(2,1)}, bf16[48,2048]{1,0:T(8,128)(2,1)}) custom-call(bf16[256,2048]{1,0:T(8,128)(2,1)} %grad_ref.3, s32[256,2048]{1,0:T(8,128)} %keep_ref.3), custom_call_target="tpu_custom_call" | custom-call | flops 1 | bytes 1 | tf_op jit(solution)/shard_map/mask_last/pallas_call | solution.py:102
  8.4 0.5 collective-permute-start.3
  8.9 0.1 collective-permute-start.5
  9.0 0.4 collective-permute-start.4
  9.4 0.6 %collective-permute-done.6.refs_8_ = bf16[48,2048]{1,0:T(8,128)(2,1)S(1)} collective-permute-done((bf16[48,2048]{1,0:T(8,128)(2,1)}, bf16[48,2048]{1,0:T(8,128)(2,1)S(1)}, u32[]{:S(2)}, u32[]{:S(2)}) %collective-permute-start.6) | collective-permute-done | bytes 196640 | tf_op jit(solution)/shard_map/ppermute | solution.py:441
  10.1 0.7 %copy-done.12 = bf16[48,2048]{1,0:T(8,128)(2,1)} copy-done((bf16[48,2048]{1,0:T(8,128)(2,1)}, bf16[48,2048]{1,0:T(8,128)(2,1)S(1)}, u32[]{:S(2)}) %copy-start.12) | copy-done | bytes 196632
  10.8 0.2 collective-permute-start.9
  10.9 1.1 %kv_state.1 = (f32[4,128,128]{2,1,0:T(8,128)S(1)}, bf16[4,128,128]{2,1,0:T(8,128)(2,1)}) custom-call(bf16[1024,512]{1,0:T(8,128)(2,1)S(1)} %copy-done.2, bf16[1024,512]{1,0:T(8,128)(2,1)S(1)} %copy-done.4), custom_call_target="tpu_custom_call" | custom-call | flops 1 | bytes 1 | tf_op jit(solution)/shard_map/kv_state/pallas_call | solution.py:131
  12.1 0.7 %copy-done.11 = bf16[64,2048]{1,0:T(8,128)(2,1)} copy-done((bf16[64,2048]{1,0:T(8,128)(2,1)}, bf16[64,2048]{1,0:T(8,128)(2,1)S(1)}, u32[]{:S(2)}) %copy-start.11) | copy-done | bytes 262168
  12.8 3.1 %collective-permute-start.2 = (bf16[4,128,128]{2,1,0:T(8,128)(2,1)}, bf16[4,128,128]{2,1,0:T(8,128)(2,1)S(1)}, u32[]{:S(2)}, u32[]{:S(2)}) collective-permute-start(bf16[4,128,128]{2,1,0:T(8,128)(2,1)} %get-tuple-element.30), channel_id=1, source_target_pairs={{0,12},{4,8},{8,4},{12,0},{16,28},{20,24},{24,20},{28,16},{1,13},{... | collective-permute-start | bytes 393224 | tf_op jit(solution)/shard_map/ppermute | solution.py:417
  15.8 0.5 collective-permute-start.1
  16.3 0.1 collective-permute-start
  16.4 5.9 %grad_near.1 = (bf16[512,512]{1,0:T(8,128)(2,1)}, f32[2,4,128,128]{3,2,1,0:T(8,128)}) custom-call(s32[1]{0:T(128)} %bitcast.1.refs_0_.place_ref, bf16[1024,512]{1,0:T(8,128)(2,1)} %query_ref.1, bf16[512,2048]{1,0:T(8,128)(2,1)} %refs_2_.5, bf16[144,2048]{1,0:T(8,128)(2,1)} %get-tuple-element.31.refs_3_, bf16[112,2048]{1,0:T(8,128)(2,1)} %get-tuple-element.32.refs_4_, ...), custom_call_target="tpu_custom_call" | custom-call | flops 1 | bytes 1 | tf_op jit(solution)/shard_map/grad_near/pallas_call | solution.py:241
  22.4 0.6 %copy-done.7 = bf16[4,128,128]{2,1,0:T(8,128)(2,1)} copy-done((bf16[4,128,128]{2,1,0:T(8,128)(2,1)}, bf16[4,128,128]{2,1,0:T(8,128)(2,1)S(1)}, u32[]{:S(2)}) %copy-start.7) | copy-done | bytes 131096
  23.0 0.9 %copy-done.8 = bf16[4,128,128]{2,1,0:T(8,128)(2,1)S(1)} copy-done((bf16[4,128,128]{2,1,0:T(8,128)(2,1)S(1)}, bf16[4,128,128]{2,1,0:T(8,128)(2,1)}, u32[]{:S(2)}) %copy-start.8) | copy-done | bytes 131096
  23.9 1.0 %prev_sum.1.prev_ref = bf16[4,128,128]{2,1,0:T(8,128)(2,1)S(1)} custom-call(f32[4,128,128]{2,1,0:T(8,128)S(1)} %get-tuple-element.29.wide_ref, bf16[4,128,128]{2,1,0:T(8,128)(2,1)} %collective-permute-done.refs_0_, bf16[4,128,128]{2,1,0:T(8,128)(2,1)} %collective-permute-done.1.refs_1_, bf16[4,128,128]{2,1,0:T(8,128)(2,1)S(1)} %copy-done.8), custom_call_target="tpu_custom_call" | custom-call | flops 1 | bytes 1 | tf_op jit(solution)/shard_map/prev_sum/pallas_call | solution.py:155
  25.0 0.1 collective-permute-start.8
  25.1 4.5 %collective-permute-done.9.refs_5_ = bf16[112,2048]{1,0:T(8,128)(2,1)} collective-permute-done((bf16[112,2048]{1,0:T(8,128)(2,1)}, bf16[112,2048]{1,0:T(8,128)(2,1)}, u32[]{:S(2)}, u32[]{:S(2)}) %collective-permute-start.9) | collective-permute-done | bytes 458784 | tf_op jit(solution)/shard_map/ppermute | solution.py:441
  29.6 2.4 %grad_far.1 = (bf16[288,512]{1,0:T(8,128)(2,1)S(1)}, f32[2,4,128,128]{3,2,1,0:T(8,128)S(1)}) custom-call(s32[1]{0:T(128)} %bitcast.1.refs_0_.place_ref, bf16[1024,512]{1,0:T(8,128)(2,1)S(1)} %copy-done.1, bf16[512,2048]{1,0:T(8,128)(2,1)S(1)} %copy-done, bf16[144,2048]{1,0:T(8,128)(2,1)} %collective-permute-done.7.refs_3_, ...), custom_call_target="tpu_custom_call" | custom-call | flops 1 | bytes 1 | tf_op jit(solution)/shard_map/grad_far/pallas_call | solution.py:241
  32.0 2.3 %grad_last.1 = (bf16[224,512]{1,0:T(8,128)(2,1)S(1)}, f32[2,4,128,128]{3,2,1,0:T(8,128)S(1)}, f32[4,128,128]{2,1,0:T(8,128)S(1)}, bf16[4,128,128]{2,1,0:T(8,128)(2,1)S(1)}) custom-call(s32[1]{0:T(128)} %bitcast.1.refs_0_.place_ref, bf16[1024,512]{1,0:T(8,128)(2,1)S(1)} %copy-done.1, bf16[512,2048]{1,0:T(8,128)(2,1)S(1)} %copy-done, ...), custom_call_target="tpu_custom_call" | custom-call | flops 1 | bytes 1 | tf_op jit(solution)/shard_map/grad_last/pallas_call | solution.py:241
  34.3 2.9 %collective-permute-start.13 = (bf16[4,128,128]{2,1,0:T(8,128)(2,1)S(1)}, bf16[4,128,128]{2,1,0:T(8,128)(2,1)S(1)}, u32[]{:S(2)}, u32[]{:S(2)}) collective-permute-start(bf16[4,128,128]{2,1,0:T(8,128)(2,1)S(1)} %get-tuple-element.42), channel_id=1, source_target_pairs={{0,12},{4,8},{8,4},{12,0},{16,28},{20,24},{24,20},{28,16},{1,13},{... | collective-permute-start | bytes 393224 | tf_op jit(solution)/shard_map/ppermute | solution.py:417
  37.2 0.4 collective-permute-start.12
  37.6 0.3 collective-permute-start.11
  37.9 3.9 %query_products.1 = (f32[1024,512]{1,0:T(8,128)S(1)}, bf16[1024,512]{1,0:T(8,128)(2,1)}, bf16[1024,512]{1,0:T(8,128)(2,1)S(1)}) custom-call(s32[1]{0:T(128)} %bitcast.1.refs_0_.place_ref, s32[1]{0:T(128)} %bitcast.ctx_ref, bf16[1024,512]{1,0:T(8,128)(2,1)S(1)} %copy-done.3, bf16[1024,512]{1,0:T(8,128)(2,1)S(1)} %copy-done.5, ...), custom_call_target="tpu_custom_call" | custom-call | flops 2147483648 | bytes 4194304 | tf_op jit(solution)/shard_map/query_products/pallas_call | solution.py:335
  41.8 2.6 %collective-permute-done.12.refs_1_.refs_3_ = bf16[4,128,128]{2,1,0:T(8,128)(2,1)S(1)} collective-permute-done((bf16[4,128,128]{2,1,0:T(8,128)(2,1)S(1)}, bf16[4,128,128]{2,1,0:T(8,128)(2,1)S(1)}, u32[]{:S(2)}, u32[]{:S(2)}) %collective-permute-start.12) | collective-permute-done | bytes 131104 | tf_op jit(solution)/shard_map/ppermute | solution.py:417
  44.4 0.1 swap_state.1
  44.5 2.6 %collective-permute-start.14 = (bf16[4,128,128]{2,1,0:T(8,128)(2,1)S(1)}, bf16[4,128,128]{2,1,0:T(8,128)(2,1)S(1)}, u32[]{:S(2)}, u32[]{:S(2)}) collective-permute-start(bf16[4,128,128]{2,1,0:T(8,128)(2,1)S(1)} %swap_state.1), channel_id=1, source_target_pairs={{0,16},{4,20},{8,24},{12,28},{16,0},{20,4},{24,8},{28,12},{1,17},{... | collective-permute-start | bytes 393224 | tf_op jit(solution)/shard_map/ppermute | solution.py:484
  47.1 4.2 %later_products.1 = (f32[1024,512]{1,0:T(8,128)S(1)}, f32[1024,512]{1,0:T(8,128)S(1)}, bf16[1024,512]{1,0:T(8,128)(2,1)}, bf16[1024,512]{1,0:T(8,128)(2,1)}) custom-call(s32[1]{0:T(128)} %bitcast.1.refs_0_.place_ref, s32[1]{0:T(128)} %bitcast.ctx_ref, bf16[1024,512]{1,0:T(8,128)(2,1)S(1)} %copy-done.1, bf16[1024,512]{1,0:T(8,128)(2,1)S(1)} %copy-done.3, ...), custom_call_target="tpu_custom_call" | custom-call | flops 4294967296 | bytes 5242880 | tf_op jit(solution)/shard_map/later_products/pallas_call | solution.py:352
  51.3 2.2 %collective-permute-done.14.got_ref = bf16[4,128,128]{2,1,0:T(8,128)(2,1)S(1)} collective-permute-done((bf16[4,128,128]{2,1,0:T(8,128)(2,1)S(1)}, bf16[4,128,128]{2,1,0:T(8,128)(2,1)S(1)}, u32[]{:S(2)}, u32[]{:S(2)}) %collective-permute-start.14) | collective-permute-done | bytes 131104 | tf_op jit(solution)/shard_map/ppermute | solution.py:484
  53.5 1.7 %end_products.1 = (bf16[1024,512]{1,0:T(8,128)(2,1)}, bf16[1024,512]{1,0:T(8,128)(2,1)}, bf16[1024,512]{1,0:T(8,128)(2,1)}) custom-call(s32[1]{0:T(128)} %bitcast.ctx_ref, s32[1]{0:T(128)} %constant.9.clone.1.half_ref, bf16[4,128,128]{2,1,0:T(8,128)(2,1)S(1)} %collective-permute-done.14.got_ref, ...), custom_call_target="tpu_custom_call", output_to_operand_aliasing={{0}: (9, {}), {1}: (10, {}), {2}: (11, {})} | custom-call | flops 402653184 | bytes 8388608 | tf_op jit(solution)/shard_map/end_products/pallas_call | solution.py:399
  (39 shorter events, 0.2 us)
Async XLA Ops:
  3.0 5.4 %copy-start.13 = (bf16[80,2048]{1,0:T(8,128)(2,1)S(1)}, bf16[80,2048]{1,0:T(8,128)(2,1)}, u32[]{:S(2)}) copy-start(bf16[80,2048]{1,0:T(8,128)(2,1)} %get-tuple-element.33) | copy-start | bytes 983044
  3.0 6.0 %copy-start.14 = (bf16[64,2048]{1,0:T(8,128)(2,1)S(1)}, bf16[64,2048]{1,0:T(8,128)(2,1)}, u32[]{:S(2)}) copy-start(bf16[64,2048]{1,0:T(8,128)(2,1)} %get-tuple-element.34) | copy-start | bytes 786436
  3.0 7.9 %copy-start.2 = (bf16[1024,512]{1,0:T(8,128)(2,1)S(1)}, bf16[1024,512]{1,0:T(8,128)(2,1)}, u32[]{:S(2)}) copy-start(bf16[1024,512]{1,0:T(8,128)(2,1)} %key_ref.7) | copy-start | bytes 3145732
  3.0 7.9 %copy-start.4 = (bf16[1024,512]{1,0:T(8,128)(2,1)S(1)}, bf16[1024,512]{1,0:T(8,128)(2,1)}, u32[]{:S(2)}) copy-start(bf16[1024,512]{1,0:T(8,128)(2,1)} %value_ref.7) | copy-start | bytes 3145732
  3.0 21.9 %collective-permute-start.7 = (bf16[144,2048]{1,0:T(8,128)(2,1)}, bf16[144,2048]{1,0:T(8,128)(2,1)}, u32[]{:S(2)}, u32[]{:S(2)}) collective-permute-start(bf16[144,2048]{1,0:T(8,128)(2,1)} %get-tuple-element.31.refs_3_), channel_id=1, source_target_pairs={{0,2},{1,3},{2,0},{3,1},{4,6},{5,7},{6,4},{7,5},{8,10},{9,11},{10,... | collective-permute-start | bytes 1769480 | tf_op jit(solution)/shard_map/ppermute | solution.py:441
  8.3 1.7 %collective-permute-start.6 = (bf16[48,2048]{1,0:T(8,128)(2,1)}, bf16[48,2048]{1,0:T(8,128)(2,1)S(1)}, u32[]{:S(2)}, u32[]{:S(2)}) collective-permute-start(bf16[48,2048]{1,0:T(8,128)(2,1)} %get-tuple-element.36), channel_id=1, source_target_pairs={{0,1},{1,0},{2,3},{3,2},{4,5},{5,4},{6,7},{7,6},{8,9},{9,8},{10,11... | collective-permute-start | bytes 589832 | tf_op jit(solution)/shard_map/ppermute | solution.py:441
  8.4 7.9 %collective-permute-start.3 = (bf16[80,2048]{1,0:T(8,128)(2,1)S(1)}, bf16[80,2048]{1,0:T(8,128)(2,1)}, u32[]{:S(2)}, u32[]{:S(2)}) collective-permute-start(bf16[80,2048]{1,0:T(8,128)(2,1)S(1)} %copy-done.13), channel_id=1, source_target_pairs={{0,1},{1,0},{2,3},{3,2},{4,5},{5,4},{6,7},{7,6},{8,9},{9,8},{10,11... | collective-permute-start | bytes 983048 | tf_op jit(solution)/shard_map/ppermute | solution.py:441
  8.9 3.1 %collective-permute-start.5 = (bf16[64,2048]{1,0:T(8,128)(2,1)}, bf16[64,2048]{1,0:T(8,128)(2,1)S(1)}, u32[]{:S(2)}, u32[]{:S(2)}) collective-permute-start(bf16[64,2048]{1,0:T(8,128)(2,1)} %get-tuple-element.35), channel_id=1, source_target_pairs={{0,1},{1,0},{2,3},{3,2},{4,5},{5,4},{6,7},{7,6},{8,9},{9,8},{10,11... | collective-permute-start | bytes 786440 | tf_op jit(solution)/shard_map/ppermute | solution.py:441
  9.0 6.8 %collective-permute-start.4 = (bf16[64,2048]{1,0:T(8,128)(2,1)S(1)}, bf16[64,2048]{1,0:T(8,128)(2,1)}, u32[]{:S(2)}, u32[]{:S(2)}) collective-permute-start(bf16[64,2048]{1,0:T(8,128)(2,1)S(1)} %copy-done.14), channel_id=1, source_target_pairs={{0,1},{1,0},{2,3},{3,2},{4,5},{5,4},{6,7},{7,6},{8,9},{9,8},{10,11... | collective-permute-start | bytes 786440 | tf_op jit(solution)/shard_map/ppermute | solution.py:441
  10.1 0.7 %copy-start.12 = (bf16[48,2048]{1,0:T(8,128)(2,1)}, bf16[48,2048]{1,0:T(8,128)(2,1)S(1)}, u32[]{:S(2)}) copy-start(bf16[48,2048]{1,0:T(8,128)(2,1)S(1)} %collective-permute-done.6.refs_8_) | copy-start | bytes 589828
  10.8 18.8 %collective-permute-start.9 = (bf16[112,2048]{1,0:T(8,128)(2,1)}, bf16[112,2048]{1,0:T(8,128)(2,1)}, u32[]{:S(2)}, u32[]{:S(2)}) collective-permute-start(bf16[112,2048]{1,0:T(8,128)(2,1)} %get-tuple-element.32.refs_4_), channel_id=1, source_target_pairs={{0,2},{1,3},{2,0},{3,1},{4,6},{5,7},{6,4},{7,5},{8,10},{9,11},{10,... | collective-permute-start | bytes 1376264 | tf_op jit(solution)/shard_map/ppermute | solution.py:441
  12.1 0.7 %copy-start.11 = (bf16[64,2048]{1,0:T(8,128)(2,1)}, bf16[64,2048]{1,0:T(8,128)(2,1)S(1)}, u32[]{:S(2)}) copy-start(bf16[64,2048]{1,0:T(8,128)(2,1)S(1)} %collective-permute-done.5.refs_7_) | copy-start | bytes 786436
  12.8 9.6 %collective-permute-start.2 = (bf16[4,128,128]{2,1,0:T(8,128)(2,1)}, bf16[4,128,128]{2,1,0:T(8,128)(2,1)S(1)}, u32[]{:S(2)}, u32[]{:S(2)}) collective-permute-start(bf16[4,128,128]{2,1,0:T(8,128)(2,1)} %get-tuple-element.30), channel_id=1, source_target_pairs={{0,12},{4,8},{8,4},{12,0},{16,28},{20,24},{24,20},{28,16},{1,13},{... | collective-permute-start | bytes 393224 | tf_op jit(solution)/shard_map/ppermute | solution.py:417
  15.8 7.2 %collective-permute-start.1 = (bf16[4,128,128]{2,1,0:T(8,128)(2,1)}, bf16[4,128,128]{2,1,0:T(8,128)(2,1)}, u32[]{:S(2)}, u32[]{:S(2)}) collective-permute-start(bf16[4,128,128]{2,1,0:T(8,128)(2,1)} %get-tuple-element.30), channel_id=1, source_target_pairs={{0,8},{4,12},{8,0},{12,4},{16,24},{20,28},{24,16},{28,20},{1,9},{5... | collective-permute-start | bytes 393224 | tf_op jit(solution)/shard_map/ppermute | solution.py:417
  16.3 6.7 %collective-permute-start = (bf16[4,128,128]{2,1,0:T(8,128)(2,1)}, bf16[4,128,128]{2,1,0:T(8,128)(2,1)}, u32[]{:S(2)}, u32[]{:S(2)}) collective-permute-start(bf16[4,128,128]{2,1,0:T(8,128)(2,1)} %get-tuple-element.30), channel_id=1, source_target_pairs={{0,4},{4,0},{8,12},{12,8},{16,20},{20,16},{24,28},{28,24},{1,5},{5... | collective-permute-start | bytes 393224 | tf_op jit(solution)/shard_map/ppermute | solution.py:417
  16.4 13.1 %copy-start = (bf16[512,2048]{1,0:T(8,128)(2,1)S(1)}, bf16[512,2048]{1,0:T(8,128)(2,1)}, u32[]{:S(2)}) copy-start(bf16[512,2048]{1,0:T(8,128)(2,1)} %refs_2_.5) | copy-start | bytes 6291460
  16.4 13.1 %copy-start.1 = (bf16[1024,512]{1,0:T(8,128)(2,1)S(1)}, bf16[1024,512]{1,0:T(8,128)(2,1)}, u32[]{:S(2)}) copy-start(bf16[1024,512]{1,0:T(8,128)(2,1)} %query_ref.1) | copy-start | bytes 3145732
  22.4 0.7 %copy-start.7 = (bf16[4,128,128]{2,1,0:T(8,128)(2,1)}, bf16[4,128,128]{2,1,0:T(8,128)(2,1)S(1)}, u32[]{:S(2)}) copy-start(bf16[4,128,128]{2,1,0:T(8,128)(2,1)S(1)} %collective-permute-done.2.refs_2_) | copy-start | bytes 393220
  23.0 0.9 %copy-start.8 = (bf16[4,128,128]{2,1,0:T(8,128)(2,1)S(1)}, bf16[4,128,128]{2,1,0:T(8,128)(2,1)}, u32[]{:S(2)}) copy-start(bf16[4,128,128]{2,1,0:T(8,128)(2,1)} %copy-done.7) | copy-start | bytes 393220
  25.0 4.5 %collective-permute-start.8 = (bf16[144,2048]{1,0:T(8,128)(2,1)}, bf16[144,2048]{1,0:T(8,128)(2,1)}, u32[]{:S(2)}, u32[]{:S(2)}) collective-permute-start(bf16[144,2048]{1,0:T(8,128)(2,1)} %collective-permute-done.7.refs_3_), channel_id=1, source_target_pairs={{0,1},{1,0},{2,3},{3,2},{4,5},{5,4},{6,7},{7,6},{8,9},{9,8},{10,11... | collective-permute-start | bytes 1769480 | tf_op jit(solution)/shard_map/ppermute | solution.py:441
  29.5 2.4 %collective-permute-start.10 = (bf16[112,2048]{1,0:T(8,128)(2,1)}, bf16[112,2048]{1,0:T(8,128)(2,1)}, u32[]{:S(2)}, u32[]{:S(2)}) collective-permute-start(bf16[112,2048]{1,0:T(8,128)(2,1)} %collective-permute-done.9.refs_5_), channel_id=1, source_target_pairs={{0,1},{1,0},{2,3},{3,2},{4,5},{5,4},{6,7},{7,6},{8,9},{9,8},{10,11... | collective-permute-start | bytes 1376264 | tf_op jit(solution)/shard_map/ppermute | solution.py:441
  29.5 2.4 %copy-start.6 = (f32[2,4,128,128]{3,2,1,0:T(8,128)S(1)}, f32[2,4,128,128]{3,2,1,0:T(8,128)}, u32[]{:S(2)}) copy-start(f32[2,4,128,128]{3,2,1,0:T(8,128)} %get-tuple-element.37.refs_4_.refs_0_) | copy-start | bytes 1572868
  32.0 5.9 %copy-start.3 = (bf16[1024,512]{1,0:T(8,128)(2,1)S(1)}, bf16[1024,512]{1,0:T(8,128)(2,1)}, u32[]{:S(2)}) copy-start(bf16[1024,512]{1,0:T(8,128)(2,1)} %key_ref.7) | copy-start | bytes 3145732
  32.0 5.9 %copy-start.5 = (bf16[1024,512]{1,0:T(8,128)(2,1)S(1)}, bf16[1024,512]{1,0:T(8,128)(2,1)}, u32[]{:S(2)}) copy-start(bf16[1024,512]{1,0:T(8,128)(2,1)} %value_ref.7) | copy-start | bytes 3145732
  32.0 5.9 %copy-start.9 = (bf16[4,128,128]{2,1,0:T(8,128)(2,1)S(1)}, bf16[4,128,128]{2,1,0:T(8,128)(2,1)}, u32[]{:S(2)}) copy-start(bf16[4,128,128]{2,1,0:T(8,128)(2,1)} %copy-done.7) | copy-start | bytes 393220
  32.0 5.9 %copy-start.10 = (bf16[512,512]{1,0:T(8,128)(2,1)S(1)}, bf16[512,512]{1,0:T(8,128)(2,1)}, u32[]{:S(2)}) copy-start(bf16[512,512]{1,0:T(8,128)(2,1)} %get-tuple-element.43.refs_3_) | copy-start | bytes 1572868
  34.3 7.5 %collective-permute-start.13 = (bf16[4,128,128]{2,1,0:T(8,128)(2,1)S(1)}, bf16[4,128,128]{2,1,0:T(8,128)(2,1)S(1)}, u32[]{:S(2)}, u32[]{:S(2)}) collective-permute-start(bf16[4,128,128]{2,1,0:T(8,128)(2,1)S(1)} %get-tuple-element.42), channel_id=1, source_target_pairs={{0,12},{4,8},{8,4},{12,0},{16,28},{20,24},{24,20},{28,16},{1,13},{... | collective-permute-start | bytes 393224 | tf_op jit(solution)/shard_map/ppermute | solution.py:417
  37.2 7.2 %collective-permute-start.12 = (bf16[4,128,128]{2,1,0:T(8,128)(2,1)S(1)}, bf16[4,128,128]{2,1,0:T(8,128)(2,1)S(1)}, u32[]{:S(2)}, u32[]{:S(2)}) collective-permute-start(bf16[4,128,128]{2,1,0:T(8,128)(2,1)S(1)} %get-tuple-element.42), channel_id=1, source_target_pairs={{0,8},{4,12},{8,0},{12,4},{16,24},{20,28},{24,16},{28,20},{1,9},{5... | collective-permute-start | bytes 393224 | tf_op jit(solution)/shard_map/ppermute | solution.py:417
  37.6 6.7 %collective-permute-start.11 = (bf16[4,128,128]{2,1,0:T(8,128)(2,1)S(1)}, bf16[4,128,128]{2,1,0:T(8,128)(2,1)S(1)}, u32[]{:S(2)}, u32[]{:S(2)}) collective-permute-start(bf16[4,128,128]{2,1,0:T(8,128)(2,1)S(1)} %get-tuple-element.42), channel_id=1, source_target_pairs={{0,4},{4,0},{8,12},{12,8},{16,20},{20,16},{24,28},{28,24},{1,5},{5... | collective-permute-start | bytes 393224 | tf_op jit(solution)/shard_map/ppermute | solution.py:417
  44.5 9.0 %collective-permute-start.14 = (bf16[4,128,128]{2,1,0:T(8,128)(2,1)S(1)}, bf16[4,128,128]{2,1,0:T(8,128)(2,1)S(1)}, u32[]{:S(2)}, u32[]{:S(2)}) collective-permute-start(bf16[4,128,128]{2,1,0:T(8,128)(2,1)S(1)} %swap_state.1), channel_id=1, source_target_pairs={{0,16},{4,20},{8,24},{12,28},{16,0},{20,4},{24,8},{28,12},{1,17},{... | collective-permute-start | bytes 393224 | tf_op jit(solution)/shard_map/ppermute | solution.py:484

commit v7 on v5

--- a/solution.py
+++ b/solution.py
@@ -476,7 +476,7 @@
     )
     parts = (query_part, key_part, value_part)
     dones = (query_done, key_done, value_done)
-    return end_products(ctx, half, got, key_rows, value_rows, grad_rows, parts, dones, own_rows)
+    return end_products(ctx, half, got, key_rows, value_rows, grad_rows, parts, dones, own_rows // 2)
 
 
 def solution(mesh):

time: 55.5 us -> 56.1 us (1.011)
  no operation moved by 1% of the time
where the time goes in v7:
time: 56.1 us; the launch traced here: 55.8 us
  Pallas kernels  28.1 us (50%)
  starting transfers between devices  14.1 us (25%)
  waiting for transfers between devices  9.72 us (17%)
  local copies, waits for them, and re-layouts  3 us (5%)
  between operations  0.85 us (2%)
    pallas_call x3, Pallas kernels, grad_part(): pl.pallas_call(functools.partial(grad_body, pieces, sub, len(befores), la...  10.6 us
    ppermute x6, starting transfers between devices, scan_states(): send = lambda payload, pairs: lax.ppermute(payload, 'ctx', pairs)  7.19 us
    ppermute x8, waiting for transfers between devices, swap(): return lax.ppermute(array, 'head', [(i, i ^ distance) for i in range(size)])  4.98 us
    pallas_call x2, Pallas kernels, mask_rows(): pl.pallas_call(functools.partial(mask_body, row), out_shape=tuple((jax.Sh...  4.91 us
    ppermute x8, starting transfers between devices, swap(): return lax.ppermute(array, 'head', [(i, i ^ distance) for i in range(size)])  4.31 us
    pallas_call x1, Pallas kernels, later_products(): pl.pallas_call(functools.partial(later_body, sub, len(nexts)), out_shape=...  4.19 us
    pallas_call x1, Pallas kernels, query_products(): pl.pallas_call(functools.partial(query_body, places, sub, len(prevs)), ou...  3.91 us
    unnamed x30, local copies, waits for them, and re-layouts  3 us
  transfers between devices with their start and end apart: 15, of which 4 were waited for; matrix products, arithmetic and copies ran while one was open for 0% of the time, Pallas kernels for 38%

profile of v7, /device:TPU:0, one launch (start us, length us, event | category | flops | bytes accessed | tf_op | source)
XLA Modules:
  0.0 55.8 jit_solution(2924434058026716890)
XLA Ops:
  0.6 2.5 %mask_first.1 = (bf16[144,2048]{1,0:T(8,128)(2,1)}, bf16[80,2048]{1,0:T(8,128)(2,1)}, bf16[64,2048]{1,0:T(8,128)(2,1)}) custom-call(bf16[256,2048]{1,0:T(8,128)(2,1)} %grad_ref.3, s32[256,2048]{1,0:T(8,128)} %keep_ref.3), custom_call_target="tpu_custom_call" | custom-call | flops 1 | bytes 1 | tf_op jit(solution)/shard_map/mask_first/pallas_call | solution.py:93
  3.2 3.0 %collective-permute-start.7 = (bf16[144,2048]{1,0:T(8,128)(2,1)}, bf16[144,2048]{1,0:T(8,128)(2,1)}, u32[]{:S(2)}, u32[]{:S(2)}) collective-permute-start(bf16[144,2048]{1,0:T(8,128)(2,1)} %get-tuple-element.31.refs_3_), channel_id=1, source_target_pairs={{0,2},{1,3},{2,0},{3,1},{4,6},{5,7},{6,4},{7,5},{8,10},{9,11},{10,... | collective-permute-start | bytes 1769480 | tf_op jit(solution)/shard_map/ppermute | solution.py:430
  6.2 2.4 %mask_last.1 = (bf16[112,2048]{1,0:T(8,128)(2,1)}, bf16[64,2048]{1,0:T(8,128)(2,1)}, bf16[48,2048]{1,0:T(8,128)(2,1)}) custom-call(bf16[256,2048]{1,0:T(8,128)(2,1)} %grad_ref.3, s32[256,2048]{1,0:T(8,128)} %keep_ref.3), custom_call_target="tpu_custom_call" | custom-call | flops 1 | bytes 1 | tf_op jit(solution)/shard_map/mask_last/pallas_call | solution.py:93
  8.7 0.5 collective-permute-start.3
  9.2 0.1 collective-permute-start.5
  9.3 0.4 collective-permute-start.4
  9.7 0.6 %collective-permute-done.6.refs_8_ = bf16[48,2048]{1,0:T(8,128)(2,1)S(1)} collective-permute-done((bf16[48,2048]{1,0:T(8,128)(2,1)}, bf16[48,2048]{1,0:T(8,128)(2,1)S(1)}, u32[]{:S(2)}, u32[]{:S(2)}) %collective-permute-start.6) | collective-permute-done | bytes 196640 | tf_op jit(solution)/shard_map/ppermute | solution.py:430
  10.3 0.7 %copy-done.12 = bf16[48,2048]{1,0:T(8,128)(2,1)} copy-done((bf16[48,2048]{1,0:T(8,128)(2,1)}, bf16[48,2048]{1,0:T(8,128)(2,1)S(1)}, u32[]{:S(2)}) %copy-start.12) | copy-done | bytes 196632
  11.0 0.2 collective-permute-start.9
  11.2 1.1 %kv_state.1 = (f32[4,128,128]{2,1,0:T(8,128)S(1)}, bf16[4,128,128]{2,1,0:T(8,128)(2,1)}) custom-call(bf16[1024,512]{1,0:T(8,128)(2,1)S(1)} %copy-done.2, bf16[1024,512]{1,0:T(8,128)(2,1)S(1)} %copy-done.4), custom_call_target="tpu_custom_call" | custom-call | flops 1 | bytes 1 | tf_op jit(solution)/shard_map/kv_state/pallas_call | solution.py:120
  12.3 0.7 %copy-done.11 = bf16[64,2048]{1,0:T(8,128)(2,1)} copy-done((bf16[64,2048]{1,0:T(8,128)(2,1)}, bf16[64,2048]{1,0:T(8,128)(2,1)S(1)}, u32[]{:S(2)}) %copy-start.11) | copy-done | bytes 262168
  13.0 3.1 %collective-permute-start.2 = (bf16[4,128,128]{2,1,0:T(8,128)(2,1)}, bf16[4,128,128]{2,1,0:T(8,128)(2,1)S(1)}, u32[]{:S(2)}, u32[]{:S(2)}) collective-permute-start(bf16[4,128,128]{2,1,0:T(8,128)(2,1)} %get-tuple-element.30), channel_id=1, source_target_pairs={{0,12},{4,8},{8,4},{12,0},{16,28},{20,24},{24,20},{28,16},{1,13},{... | collective-permute-start | bytes 393224 | tf_op jit(solution)/shard_map/ppermute | solution.py:406
  16.1 0.5 collective-permute-start.1
  16.6 0.1 collective-permute-start
  16.7 5.9 %grad_near.1 = (bf16[512,512]{1,0:T(8,128)(2,1)}, f32[2,4,128,128]{3,2,1,0:T(8,128)}) custom-call(s32[1]{0:T(128)} %bitcast.1.refs_0_.place_ref, bf16[1024,512]{1,0:T(8,128)(2,1)} %query_ref.1, bf16[512,2048]{1,0:T(8,128)(2,1)} %refs_2_.5, bf16[144,2048]{1,0:T(8,128)(2,1)} %get-tuple-element.31.refs_3_, bf16[112,2048]{1,0:T(8,128)(2,1)} %get-tuple-element.32.refs_4_, ...), custom_call_target="tpu_custom_call" | custom-call | flops 1 | bytes 1 | tf_op jit(solution)/shard_map/grad_near/pallas_call | solution.py:230
  22.6 0.6 %copy-done.7 = bf16[4,128,128]{2,1,0:T(8,128)(2,1)} copy-done((bf16[4,128,128]{2,1,0:T(8,128)(2,1)}, bf16[4,128,128]{2,1,0:T(8,128)(2,1)S(1)}, u32[]{:S(2)}) %copy-start.7) | copy-done | bytes 131096
  23.3 0.9 %copy-done.8 = bf16[4,128,128]{2,1,0:T(8,128)(2,1)S(1)} copy-done((bf16[4,128,128]{2,1,0:T(8,128)(2,1)S(1)}, bf16[4,128,128]{2,1,0:T(8,128)(2,1)}, u32[]{:S(2)}) %copy-start.8) | copy-done | bytes 131096
  24.2 1.0 %prev_sum.1.prev_ref = bf16[4,128,128]{2,1,0:T(8,128)(2,1)S(1)} custom-call(f32[4,128,128]{2,1,0:T(8,128)S(1)} %get-tuple-element.29.wide_ref, bf16[4,128,128]{2,1,0:T(8,128)(2,1)} %collective-permute-done.refs_0_, bf16[4,128,128]{2,1,0:T(8,128)(2,1)} %collective-permute-done.1.refs_1_, bf16[4,128,128]{2,1,0:T(8,128)(2,1)S(1)} %copy-done.8), custom_call_target="tpu_custom_call" | custom-call | flops 1 | bytes 1 | tf_op jit(solution)/shard_map/prev_sum/pallas_call | solution.py:144
  25.2 0.1 collective-permute-start.8
  25.3 4.3 %collective-permute-done.9.refs_5_ = bf16[112,2048]{1,0:T(8,128)(2,1)} collective-permute-done((bf16[112,2048]{1,0:T(8,128)(2,1)}, bf16[112,2048]{1,0:T(8,128)(2,1)}, u32[]{:S(2)}, u32[]{:S(2)}) %collective-permute-start.9) | collective-permute-done | bytes 458784 | tf_op jit(solution)/shard_map/ppermute | solution.py:430
  29.7 2.4 %grad_far.1 = (bf16[288,512]{1,0:T(8,128)(2,1)S(1)}, f32[2,4,128,128]{3,2,1,0:T(8,128)S(1)}) custom-call(s32[1]{0:T(128)} %bitcast.1.refs_0_.place_ref, bf16[1024,512]{1,0:T(8,128)(2,1)S(1)} %copy-done.1, bf16[512,2048]{1,0:T(8,128)(2,1)S(1)} %copy-done, bf16[144,2048]{1,0:T(8,128)(2,1)} %collective-permute-done.7.refs_3_, ...), custom_call_target="tpu_custom_call" | custom-call | flops 1 | bytes 1 | tf_op jit(solution)/shard_map/grad_far/pallas_call | solution.py:230
  32.2 2.3 %grad_last.1 = (bf16[224,512]{1,0:T(8,128)(2,1)S(1)}, f32[2,4,128,128]{3,2,1,0:T(8,128)S(1)}, f32[4,128,128]{2,1,0:T(8,128)S(1)}, bf16[4,128,128]{2,1,0:T(8,128)(2,1)S(1)}) custom-call(s32[1]{0:T(128)} %bitcast.1.refs_0_.place_ref, bf16[1024,512]{1,0:T(8,128)(2,1)S(1)} %copy-done.1, bf16[512,2048]{1,0:T(8,128)(2,1)S(1)} %copy-done, ...), custom_call_target="tpu_custom_call" | custom-call | flops 1 | bytes 1 | tf_op jit(solution)/shard_map/grad_last/pallas_call | solution.py:230
  34.5 2.8 %collective-permute-start.13 = (bf16[4,128,128]{2,1,0:T(8,128)(2,1)S(1)}, bf16[4,128,128]{2,1,0:T(8,128)(2,1)S(1)}, u32[]{:S(2)}, u32[]{:S(2)}) collective-permute-start(bf16[4,128,128]{2,1,0:T(8,128)(2,1)S(1)} %get-tuple-element.42), channel_id=1, source_target_pairs={{0,12},{4,8},{8,4},{12,0},{16,28},{20,24},{24,20},{28,16},{1,13},{... | collective-permute-start | bytes 393224 | tf_op jit(solution)/shard_map/ppermute | solution.py:406
  37.3 0.5 collective-permute-start.12
  37.8 0.3 collective-permute-start.11
  38.0 3.9 %query_products.1 = (f32[1024,512]{1,0:T(8,128)S(1)}, bf16[1024,512]{1,0:T(8,128)(2,1)}, bf16[1024,512]{1,0:T(8,128)(2,1)S(1)}) custom-call(s32[1]{0:T(128)} %bitcast.1.refs_0_.place_ref, s32[1]{0:T(128)} %bitcast.ctx_ref, bf16[1024,512]{1,0:T(8,128)(2,1)S(1)} %copy-done.3, bf16[1024,512]{1,0:T(8,128)(2,1)S(1)} %copy-done.5, ...), custom_call_target="tpu_custom_call" | custom-call | flops 2147483648 | bytes 4194304 | tf_op jit(solution)/shard_map/query_products/pallas_call | solution.py:324
  42.0 2.5 %collective-permute-done.12.refs_1_.refs_3_ = bf16[4,128,128]{2,1,0:T(8,128)(2,1)S(1)} collective-permute-done((bf16[4,128,128]{2,1,0:T(8,128)(2,1)S(1)}, bf16[4,128,128]{2,1,0:T(8,128)(2,1)S(1)}, u32[]{:S(2)}, u32[]{:S(2)}) %collective-permute-start.12) | collective-permute-done | bytes 131104 | tf_op jit(solution)/shard_map/ppermute | solution.py:406
  44.5 0.1 swap_state.1
  44.6 2.6 %collective-permute-start.14 = (bf16[4,128,128]{2,1,0:T(8,128)(2,1)S(1)}, bf16[4,128,128]{2,1,0:T(8,128)(2,1)S(1)}, u32[]{:S(2)}, u32[]{:S(2)}) collective-permute-start(bf16[4,128,128]{2,1,0:T(8,128)(2,1)S(1)} %swap_state.1), channel_id=1, source_target_pairs={{0,16},{4,20},{8,24},{12,28},{16,0},{20,4},{24,8},{28,12},{1,17},{... | collective-permute-start | bytes 393224 | tf_op jit(solution)/shard_map/ppermute | solution.py:473
  47.2 4.2 %later_products.1 = (f32[1024,512]{1,0:T(8,128)S(1)}, f32[1024,512]{1,0:T(8,128)S(1)}, bf16[1024,512]{1,0:T(8,128)(2,1)}, bf16[1024,512]{1,0:T(8,128)(2,1)}) custom-call(s32[1]{0:T(128)} %bitcast.1.refs_0_.place_ref, s32[1]{0:T(128)} %bitcast.ctx_ref, bf16[1024,512]{1,0:T(8,128)(2,1)S(1)} %copy-done.1, bf16[1024,512]{1,0:T(8,128)(2,1)S(1)} %copy-done.3, ...), custom_call_target="tpu_custom_call" | custom-call | flops 4294967296 | bytes 5242880 | tf_op jit(solution)/shard_map/later_products/pallas_call | solution.py:341
  51.4 2.2 %collective-permute-done.14.got_ref = bf16[4,128,128]{2,1,0:T(8,128)(2,1)S(1)} collective-permute-done((bf16[4,128,128]{2,1,0:T(8,128)(2,1)S(1)}, bf16[4,128,128]{2,1,0:T(8,128)(2,1)S(1)}, u32[]{:S(2)}, u32[]{:S(2)}) %collective-permute-start.14) | collective-permute-done | bytes 131104 | tf_op jit(solution)/shard_map/ppermute | solution.py:473
  53.6 2.2 %end_products.1 = (bf16[1024,512]{1,0:T(8,128)(2,1)}, bf16[1024,512]{1,0:T(8,128)(2,1)}, bf16[1024,512]{1,0:T(8,128)(2,1)}) custom-call(s32[1]{0:T(128)} %bitcast.ctx_ref, s32[1]{0:T(128)} %constant.9.clone.1.half_ref, bf16[4,128,128]{2,1,0:T(8,128)(2,1)S(1)} %collective-permute-done.14.got_ref, ...), custom_call_target="tpu_custom_call", output_to_operand_aliasing={{0}: (9, {}), {1}: (10, {}), {2}: (11, {})} | custom-call | flops 402653184 | bytes 8388608 | tf_op jit(solution)/shard_map/end_products/pallas_call | solution.py:388
  (39 shorter events, 0.2 us)
Async XLA Ops:
  3.1 5.6 %copy-start.13 = (bf16[80,2048]{1,0:T(8,128)(2,1)S(1)}, bf16[80,2048]{1,0:T(8,128)(2,1)}, u32[]{:S(2)}) copy-start(bf16[80,2048]{1,0:T(8,128)(2,1)} %get-tuple-element.33) | copy-start | bytes 983044
  3.1 6.1 %copy-start.14 = (bf16[64,2048]{1,0:T(8,128)(2,1)S(1)}, bf16[64,2048]{1,0:T(8,128)(2,1)}, u32[]{:S(2)}) copy-start(bf16[64,2048]{1,0:T(8,128)(2,1)} %get-tuple-element.34) | copy-start | bytes 786436
  3.2 8.0 %copy-start.2 = (bf16[1024,512]{1,0:T(8,128)(2,1)S(1)}, bf16[1024,512]{1,0:T(8,128)(2,1)}, u32[]{:S(2)}) copy-start(bf16[1024,512]{1,0:T(8,128)(2,1)} %key_ref.7) | copy-start | bytes 3145732
  3.2 8.0 %copy-start.4 = (bf16[1024,512]{1,0:T(8,128)(2,1)S(1)}, bf16[1024,512]{1,0:T(8,128)(2,1)}, u32[]{:S(2)}) copy-start(bf16[1024,512]{1,0:T(8,128)(2,1)} %value_ref.7) | copy-start | bytes 3145732
  3.2 22.1 %collective-permute-start.7 = (bf16[144,2048]{1,0:T(8,128)(2,1)}, bf16[144,2048]{1,0:T(8,128)(2,1)}, u32[]{:S(2)}, u32[]{:S(2)}) collective-permute-start(bf16[144,2048]{1,0:T(8,128)(2,1)} %get-tuple-element.31.refs_3_), channel_id=1, source_target_pairs={{0,2},{1,3},{2,0},{3,1},{4,6},{5,7},{6,4},{7,5},{8,10},{9,11},{10,... | collective-permute-start | bytes 1769480 | tf_op jit(solution)/shard_map/ppermute | solution.py:430
  8.6 1.7 %collective-permute-start.6 = (bf16[48,2048]{1,0:T(8,128)(2,1)}, bf16[48,2048]{1,0:T(8,128)(2,1)S(1)}, u32[]{:S(2)}, u32[]{:S(2)}) collective-permute-start(bf16[48,2048]{1,0:T(8,128)(2,1)} %get-tuple-element.36), channel_id=1, source_target_pairs={{0,1},{1,0},{2,3},{3,2},{4,5},{5,4},{6,7},{7,6},{8,9},{9,8},{10,11... | collective-permute-start | bytes 589832 | tf_op jit(solution)/shard_map/ppermute | solution.py:430
  8.7 7.9 %collective-permute-start.3 = (bf16[80,2048]{1,0:T(8,128)(2,1)S(1)}, bf16[80,2048]{1,0:T(8,128)(2,1)}, u32[]{:S(2)}, u32[]{:S(2)}) collective-permute-start(bf16[80,2048]{1,0:T(8,128)(2,1)S(1)} %copy-done.13), channel_id=1, source_target_pairs={{0,1},{1,0},{2,3},{3,2},{4,5},{5,4},{6,7},{7,6},{8,9},{9,8},{10,11... | collective-permute-start | bytes 983048 | tf_op jit(solution)/shard_map/ppermute | solution.py:430
  9.2 3.1 %collective-permute-start.5 = (bf16[64,2048]{1,0:T(8,128)(2,1)}, bf16[64,2048]{1,0:T(8,128)(2,1)S(1)}, u32[]{:S(2)}, u32[]{:S(2)}) collective-permute-start(bf16[64,2048]{1,0:T(8,128)(2,1)} %get-tuple-element.35), channel_id=1, source_target_pairs={{0,1},{1,0},{2,3},{3,2},{4,5},{5,4},{6,7},{7,6},{8,9},{9,8},{10,11... | collective-permute-start | bytes 786440 | tf_op jit(solution)/shard_map/ppermute | solution.py:430
  9.3 6.8 %collective-permute-start.4 = (bf16[64,2048]{1,0:T(8,128)(2,1)S(1)}, bf16[64,2048]{1,0:T(8,128)(2,1)}, u32[]{:S(2)}, u32[]{:S(2)}) collective-permute-start(bf16[64,2048]{1,0:T(8,128)(2,1)S(1)} %copy-done.14), channel_id=1, source_target_pairs={{0,1},{1,0},{2,3},{3,2},{4,5},{5,4},{6,7},{7,6},{8,9},{9,8},{10,11... | collective-permute-start | bytes 786440 | tf_op jit(solution)/shard_map/ppermute | solution.py:430
  10.3 0.7 %copy-start.12 = (bf16[48,2048]{1,0:T(8,128)(2,1)}, bf16[48,2048]{1,0:T(8,128)(2,1)S(1)}, u32[]{:S(2)}) copy-start(bf16[48,2048]{1,0:T(8,128)(2,1)S(1)} %collective-permute-done.6.refs_8_) | copy-start | bytes 589828
  11.0 18.6 %collective-permute-start.9 = (bf16[112,2048]{1,0:T(8,128)(2,1)}, bf16[112,2048]{1,0:T(8,128)(2,1)}, u32[]{:S(2)}, u32[]{:S(2)}) collective-permute-start(bf16[112,2048]{1,0:T(8,128)(2,1)} %get-tuple-element.32.refs_4_), channel_id=1, source_target_pairs={{0,2},{1,3},{2,0},{3,1},{4,6},{5,7},{6,4},{7,5},{8,10},{9,11},{10,... | collective-permute-start | bytes 1376264 | tf_op jit(solution)/shard_map/ppermute | solution.py:430
  12.3 0.7 %copy-start.11 = (bf16[64,2048]{1,0:T(8,128)(2,1)}, bf16[64,2048]{1,0:T(8,128)(2,1)S(1)}, u32[]{:S(2)}) copy-start(bf16[64,2048]{1,0:T(8,128)(2,1)S(1)} %collective-permute-done.5.refs_7_) | copy-start | bytes 786436
  13.0 9.6 %collective-permute-start.2 = (bf16[4,128,128]{2,1,0:T(8,128)(2,1)}, bf16[4,128,128]{2,1,0:T(8,128)(2,1)S(1)}, u32[]{:S(2)}, u32[]{:S(2)}) collective-permute-start(bf16[4,128,128]{2,1,0:T(8,128)(2,1)} %get-tuple-element.30), channel_id=1, source_target_pairs={{0,12},{4,8},{8,4},{12,0},{16,28},{20,24},{24,20},{28,16},{1,13},{... | collective-permute-start | bytes 393224 | tf_op jit(solution)/shard_map/ppermute | solution.py:406
  16.1 7.2 %collective-permute-start.1 = (bf16[4,128,128]{2,1,0:T(8,128)(2,1)}, bf16[4,128,128]{2,1,0:T(8,128)(2,1)}, u32[]{:S(2)}, u32[]{:S(2)}) collective-permute-start(bf16[4,128,128]{2,1,0:T(8,128)(2,1)} %get-tuple-element.30), channel_id=1, source_target_pairs={{0,8},{4,12},{8,0},{12,4},{16,24},{20,28},{24,16},{28,20},{1,9},{5... | collective-permute-start | bytes 393224 | tf_op jit(solution)/shard_map/ppermute | solution.py:406
  16.6 6.7 %collective-permute-start = (bf16[4,128,128]{2,1,0:T(8,128)(2,1)}, bf16[4,128,128]{2,1,0:T(8,128)(2,1)}, u32[]{:S(2)}, u32[]{:S(2)}) collective-permute-start(bf16[4,128,128]{2,1,0:T(8,128)(2,1)} %get-tuple-element.30), channel_id=1, source_target_pairs={{0,4},{4,0},{8,12},{12,8},{16,20},{20,16},{24,28},{28,24},{1,5},{5... | collective-permute-start | bytes 393224 | tf_op jit(solution)/shard_map/ppermute | solution.py:406
  16.7 13.0 %copy-start = (bf16[512,2048]{1,0:T(8,128)(2,1)S(1)}, bf16[512,2048]{1,0:T(8,128)(2,1)}, u32[]{:S(2)}) copy-start(bf16[512,2048]{1,0:T(8,128)(2,1)} %refs_2_.5) | copy-start | bytes 6291460
  16.7 13.0 %copy-start.1 = (bf16[1024,512]{1,0:T(8,128)(2,1)S(1)}, bf16[1024,512]{1,0:T(8,128)(2,1)}, u32[]{:S(2)}) copy-start(bf16[1024,512]{1,0:T(8,128)(2,1)} %query_ref.1) | copy-start | bytes 3145732
  22.6 0.7 %copy-start.7 = (bf16[4,128,128]{2,1,0:T(8,128)(2,1)}, bf16[4,128,128]{2,1,0:T(8,128)(2,1)S(1)}, u32[]{:S(2)}) copy-start(bf16[4,128,128]{2,1,0:T(8,128)(2,1)S(1)} %collective-permute-done.2.refs_2_) | copy-start | bytes 393220
  23.3 0.9 %copy-start.8 = (bf16[4,128,128]{2,1,0:T(8,128)(2,1)S(1)}, bf16[4,128,128]{2,1,0:T(8,128)(2,1)}, u32[]{:S(2)}) copy-start(bf16[4,128,128]{2,1,0:T(8,128)(2,1)} %copy-done.7) | copy-start | bytes 393220
  25.2 4.4 %collective-permute-start.8 = (bf16[144,2048]{1,0:T(8,128)(2,1)}, bf16[144,2048]{1,0:T(8,128)(2,1)}, u32[]{:S(2)}, u32[]{:S(2)}) collective-permute-start(bf16[144,2048]{1,0:T(8,128)(2,1)} %collective-permute-done.7.refs_3_), channel_id=1, source_target_pairs={{0,1},{1,0},{2,3},{3,2},{4,5},{5,4},{6,7},{7,6},{8,9},{9,8},{10,11... | collective-permute-start | bytes 1769480 | tf_op jit(solution)/shard_map/ppermute | solution.py:430
  29.7 2.4 %collective-permute-start.10 = (bf16[112,2048]{1,0:T(8,128)(2,1)}, bf16[112,2048]{1,0:T(8,128)(2,1)}, u32[]{:S(2)}, u32[]{:S(2)}) collective-permute-start(bf16[112,2048]{1,0:T(8,128)(2,1)} %collective-permute-done.9.refs_5_), channel_id=1, source_target_pairs={{0,1},{1,0},{2,3},{3,2},{4,5},{5,4},{6,7},{7,6},{8,9},{9,8},{10,11... | collective-permute-start | bytes 1376264 | tf_op jit(solution)/shard_map/ppermute | solution.py:430
  29.7 2.4 %copy-start.6 = (f32[2,4,128,128]{3,2,1,0:T(8,128)S(1)}, f32[2,4,128,128]{3,2,1,0:T(8,128)}, u32[]{:S(2)}) copy-start(f32[2,4,128,128]{3,2,1,0:T(8,128)} %get-tuple-element.37.refs_4_.refs_0_) | copy-start | bytes 1572868
  32.1 5.9 %copy-start.3 = (bf16[1024,512]{1,0:T(8,128)(2,1)S(1)}, bf16[1024,512]{1,0:T(8,128)(2,1)}, u32[]{:S(2)}) copy-start(bf16[1024,512]{1,0:T(8,128)(2,1)} %key_ref.7) | copy-start | bytes 3145732
  32.1 5.9 %copy-start.5 = (bf16[1024,512]{1,0:T(8,128)(2,1)S(1)}, bf16[1024,512]{1,0:T(8,128)(2,1)}, u32[]{:S(2)}) copy-start(bf16[1024,512]{1,0:T(8,128)(2,1)} %value_ref.7) | copy-start | bytes 3145732
  32.1 5.9 %copy-start.9 = (bf16[4,128,128]{2,1,0:T(8,128)(2,1)S(1)}, bf16[4,128,128]{2,1,0:T(8,128)(2,1)}, u32[]{:S(2)}) copy-start(bf16[4,128,128]{2,1,0:T(8,128)(2,1)} %copy-done.7) | copy-start | bytes 393220
  32.1 5.9 %copy-start.10 = (bf16[512,512]{1,0:T(8,128)(2,1)S(1)}, bf16[512,512]{1,0:T(8,128)(2,1)}, u32[]{:S(2)}) copy-start(bf16[512,512]{1,0:T(8,128)(2,1)} %get-tuple-element.43.refs_3_) | copy-start | bytes 1572868
  34.5 7.5 %collective-permute-start.13 = (bf16[4,128,128]{2,1,0:T(8,128)(2,1)S(1)}, bf16[4,128,128]{2,1,0:T(8,128)(2,1)S(1)}, u32[]{:S(2)}, u32[]{:S(2)}) collective-permute-start(bf16[4,128,128]{2,1,0:T(8,128)(2,1)S(1)} %get-tuple-element.42), channel_id=1, source_target_pairs={{0,12},{4,8},{8,4},{12,0},{16,28},{20,24},{24,20},{28,16},{1,13},{... | collective-permute-start | bytes 393224 | tf_op jit(solution)/shard_map/ppermute | solution.py:406
  37.3 7.2 %collective-permute-start.12 = (bf16[4,128,128]{2,1,0:T(8,128)(2,1)S(1)}, bf16[4,128,128]{2,1,0:T(8,128)(2,1)S(1)}, u32[]{:S(2)}, u32[]{:S(2)}) collective-permute-start(bf16[4,128,128]{2,1,0:T(8,128)(2,1)S(1)} %get-tuple-element.42), channel_id=1, source_target_pairs={{0,8},{4,12},{8,0},{12,4},{16,24},{20,28},{24,16},{28,20},{1,9},{5... | collective-permute-start | bytes 393224 | tf_op jit(solution)/shard_map/ppermute | solution.py:406
  37.8 6.7 %collective-permute-start.11 = (bf16[4,128,128]{2,1,0:T(8,128)(2,1)S(1)}, bf16[4,128,128]{2,1,0:T(8,128)(2,1)S(1)}, u32[]{:S(2)}, u32[]{:S(2)}) collective-permute-start(bf16[4,128,128]{2,1,0:T(8,128)(2,1)S(1)} %get-tuple-element.42), channel_id=1, source_target_pairs={{0,4},{4,0},{8,12},{12,8},{16,20},{20,16},{24,28},{28,24},{1,5},{5... | collective-permute-start | bytes 393224 | tf_op jit(solution)/shard_map/ppermute | solution.py:406
  44.6 9.0 %collective-permute-start.14 = (bf16[4,128,128]{2,1,0:T(8,128)(2,1)S(1)}, bf16[4,128,128]{2,1,0:T(8,128)(2,1)S(1)}, u32[]{:S(2)}, u32[]{:S(2)}) collective-permute-start(bf16[4,128,128]{2,1,0:T(8,128)(2,1)S(1)} %swap_state.1), channel_id=1, source_target_pairs={{0,16},{4,20},{8,24},{12,28},{16,0},{20,4},{24,8},{28,12},{1,17},{... | collective-permute-start | bytes 393224 | tf_op jit(solution)/shard_map/ppermute | solution.py:473
